TPU v7x, 128 devices: a whole 4x4x4 slice. The times are simulated.
128 devices in a mesh: rows: 16 (over y, x_hi, core), cols: 8 (over x_lo, z).
Axes of the slice: x: 4 (x_hi: 2, x_lo: 2; x = x_hi * 2 + x_lo), y: 4, z: 4, core: 2. Of those that a mesh axis runs over, the one named last changes fastest.
Arguments:
- frame: float32 [1024, 8192], P(('rows', 'cols')), may hold values from -6 to 6
- taps_row: float32 [15], replicated, may hold values from -1.5 to 1.5
- taps_col: float32 [15], replicated, may hold values from -1.5 to 1.5
- merit: bfloat16 [64, 1024, 8192], P(None, 'rows', 'cols'), may hold values from -9 to 9
- offsets: int32 [64, 2], replicated, may hold values from -8 to 8, as said below
Outputs:
- merit_next: bfloat16 [64, 1024, 8192], P(None, 'rows', 'cols')
Inputs may be any that keep to these rules, and one draw needn't show every extreme that they name: `offsets`: each component of every shift lies in -8 .. 8; some velocity has shift (-8, 8) and some other one (8, -8).
All inputs are finite; a program needn't handle non-finite values.
Results may differ from a plain program's by a relative error of at most 0.001.
Values may be sent and summed in bfloat16 or wider, within the bound.
No kernel may reach another device: no remote copies, remote signals or barrier semaphores. Data moves between devices by JAX's collectives and lax.ppermute only.
A program may use at most 192 MiB of HBM per device.

v0:
```python
import math

import jax
import jax.numpy as jnp
from jax import lax
from jax.sharding import PartitionSpec as P

VGRID = 8
MAXV = 8


forget_factor = 0.875


def with_halo(value, sides, width):
    for axis, dim in sides:
        size, length = (lax.axis_size(axis), value.shape[dim])
        up = [(i, (i + 1) % size) for i in range(size - 1)]
        down = [(j, i) for i, j in up]
        last = lax.slice_in_dim(value, length - width, length, axis=dim)
        first = lax.slice_in_dim(value, 0, width, axis=dim)
        before = lax.ppermute(last, axis, up)
        after = lax.ppermute(first, axis, down)
        value = jnp.concatenate([before, value, after], axis=dim)
    return value


def along_rows(strip, taps_row):
    half = taps_row.shape[0] // 2
    width = strip.shape[1]
    padded = jnp.pad(strip, ((0, 0), (half, half)))
    result = jnp.zeros(strip.shape, jnp.float32)
    for j in range(taps_row.shape[0]):
        result = result + taps_row[j] * padded[:, j : j + width]
    return result


def along_cols(extended, taps_col, count):
    result = jnp.zeros((count, extended.shape[1]), jnp.float32)
    for i in range(taps_col.shape[0]):
        result = result + taps_col[i] * extended[i : i + count, :]
    return result


def neighbour_max(grid, axis):
    total = grid.shape[axis]
    lower = jnp.concatenate(
        [lax.slice_in_dim(grid, 0, 1, axis=axis), lax.slice_in_dim(grid, 0, total - 1, axis=axis)],
        axis=axis,
    )
    upper = jnp.concatenate(
        [
            lax.slice_in_dim(grid, 1, total, axis=axis),
            lax.slice_in_dim(grid, total - 1, total, axis=axis),
        ],
        axis=axis,
    )
    return jnp.maximum(grid, jnp.maximum(lower, upper))


def move_planes(widened, offsets, tile_rows, tile_cols):
    block = math.gcd(tile_cols, 128)
    count = tile_cols // block
    span = block + 2 * MAXV
    windows = jnp.stack(
        [lax.slice_in_dim(widened, b * block, b * block + span, axis=2) for b in range(count)],
        axis=2,
    )
    inner = jnp.arange(span, dtype=jnp.int32)
    outer = jnp.arange(block, dtype=jnp.int32)
    col_start = MAXV - offsets[:, 1]
    select_col = (inner[None, :, None] == outer[None, None, :] + col_start[:, None, None]).astype(
        jnp.bfloat16
    )
    moved = jnp.einsum(
        "vrnk,vkc->vrnc", windows, select_col, preferred_element_type=jnp.float32
    ).astype(jnp.bfloat16)
    source = jnp.arange(tile_rows + 2 * MAXV, dtype=jnp.int32)
    target = jnp.arange(tile_rows, dtype=jnp.int32)
    row_start = MAXV - offsets[:, 0]
    select_row = (source[None, None, :] == target[None, :, None] + row_start[:, None, None]).astype(
        jnp.bfloat16
    )
    shifted = jnp.einsum("vsr,vrnc->vsnc", select_row, moved, preferred_element_type=jnp.float32)
    return shifted.reshape(widened.shape[0], tile_rows, tile_cols)


def on_device(frame, taps_row, taps_col, merit, offsets):
    half = taps_row.shape[0] // 2
    horiz = along_rows(frame, taps_row)
    extended = with_halo(horiz, ((("rows", "cols"), 0),), half)
    strip_done = along_cols(extended, taps_col, horiz.shape[0])
    filtered = lax.all_to_all(strip_done, "cols", split_axis=1, concat_axis=0, tiled=True)
    planes, tile_rows, tile_cols = merit.shape
    grid = merit.reshape(VGRID, VGRID, tile_rows, tile_cols)
    pooled = neighbour_max(neighbour_max(grid, 0), 1).reshape(planes, tile_rows, tile_cols)
    widened = with_halo(pooled, (("rows", 1), ("cols", 2)), MAXV)
    shifted = move_planes(widened, offsets, tile_rows, tile_cols)
    return (filtered[None, :, :] + forget_factor * shifted).astype(jnp.bfloat16)


def solution(mesh):
    in_specs = (P(("rows", "cols"), None), P(), P(), P(None, "rows", "cols"), P())
    out_specs = P(None, "rows", "cols")
    return jax.shard_map(
        on_device, mesh=mesh, in_specs=in_specs, out_specs=out_specs, check_vma=False
    )
```

profile of v0, /device:TPU:7, one launch (start us, length us, event | category | flops | bytes accessed | tf_op | source)
XLA Modules:
  0.0 352.5 jit_solution(13400317234933506895)
XLA Ops:
  0.0 11.1 %fusion.80 = (bf16[56,64,1024]{2,1,0:T(8,128)(2,1)}, bf16[56,64,1024]{2,1,0:T(8,128)(2,1)}) fusion(bf16[64,64,1024]{2,1,0:T(8,128)(2,1)} %param.8), kind=kLoop, calls=%fused_computation.135 | loop fusion | bytes 29360128 | tf_op jit(solution)/shard_map/slice | solution.py:48
  11.1 2.9 slice_bitcast_fusion.1
  14.0 13.8 %copy.22 = bf16[7,8,64,1024]{2,3,1,0:T(8,128)(2,1)} copy(bf16[7,8,64,1024]{3,2,1,0:T(8,128)(2,1)} %bitcast.121) | data formatting | bytes 14680064 | tf_op jit(solution)/shard_map/slice | solution.py:48
  27.8 13.7 %copy.23 = bf16[7,8,64,1024]{2,3,1,0:T(8,128)(2,1)} copy(bf16[7,8,64,1024]{3,2,1,0:T(8,128)(2,1)} %bitcast.120) | data formatting | bytes 14680064 | tf_op jit(solution)/shard_map/slice | solution.py:53
  41.5 2.0 copy.21
  43.5 1.8 copy.24
  45.3 15.6 %copy.26 = bf16[8,8,64,1024]{2,3,1,0:T(8,128)(2,1)} copy(bf16[8,8,64,1024]{3,2,1,0:T(8,128)(2,1)} %bitcast.119) | data formatting | bytes 16777216 | tf_op jit(solution)/shard_map/reshape | solution.py:95
  60.8 26.6 %fusion.76 = (bf16[8,8,64,1024]{2,3,1,0:T(8,128)(2,1)}, bf16[8,8,64,1024]{2,3,1,0:T(8,128)(2,1)}) fusion(bf16[8,8,64,1024]{2,3,1,0:T(8,128)(2,1)} %copy.26, bf16[1,8,64,1024]{2,3,1,0:T(8,128)(2,1)} %copy.24, bf16[7,8,64,1024]{2,3,1,0:T(8,128)(2,1)} %copy.23, bf16[7,8,64,1024]{2,3,1,0:T(8,128)(2,1)} %copy.22, bf16[1,8,64,1024]{2,3,1,0:T(8,128)(2,1)S(1)} %copy.21), kind=kLoop, calls=%fused_computation.131 | loop fusion | flops 16777216 | bytes 41943040 | tf_op jit(solution)/shard_map/max | solution.py:58
  87.5 23.6 %fusion.78 = (bf16[8,7,64,1024]{2,3,1,0:T(8,128)(2,1)}, bf16[8,7,64,1024]{2,3,1,0:T(8,128)(2,1)}) fusion(bf16[8,8,64,1024]{2,3,1,0:T(8,128)(2,1)} %get-tuple-element.5), kind=kLoop, calls=%fused_computation.133 | loop fusion | bytes 29360128 | tf_op jit(solution)/shard_map/slice | solution.py:53
  111.1 4.7 %fusion.79 = (bf16[8,1,64,1024]{2,3,1,0:T(8,128)(2,1)}, bf16[8,1,64,1024]{2,3,1,0:T(8,128)(2,1)}) fusion(bf16[8,8,64,1024]{2,3,1,0:T(8,128)(2,1)} %get-tuple-element.5), kind=kLoop, calls=%fused_computation.134 | loop fusion | bytes 4194304 | tf_op jit(solution)/shard_map/slice | solution.py:54
  115.8 15.6 %copy.25 = bf16[64,64,1024]{1,2,0:T(8,128)(2,1)} copy(bf16[64,64,1024]{2,1,0:T(8,128)(2,1)} %param.8) | data formatting | bytes 16777216 | tf_op args[3]
  131.3 14.3 %maximum_maximum_fusion.1 = bf16[8,8,64,1024]{2,3,1,0:T(8,128)(2,1)S(1)} fusion(bf16[8,7,64,1024]{2,3,1,0:T(8,128)(2,1)} %get-tuple-element.12, bf16[8,1,64,1024]{2,3,1,0:T(8,128)(2,1)} %get-tuple-element.14, bf16[8,1,64,1024]{2,3,1,0:T(8,128)(2,1)} %get-tuple-element.13, bf16[8,7,64,1024]{2,3,1,0:T(8,128)(2,1)} %get-tuple-element.11), kind=kLoop, calls=%fused_computation.3 | loop fusion | flops 12582912 | bytes 25165824 | tf_op jit(solution)/shard_map/max | solution.py:58
  145.7 12.6 %bitcast_maximum_fusion = bf16[64,64,1024]{1,2,0:T(8,128)(2,1)S(1)} fusion(bf16[8,8,64,1024]{2,3,1,0:T(8,128)(2,1)S(1)} %maximum_maximum_fusion.1, bf16[64,64,1024]{1,2,0:T(8,128)(2,1)} %copy.25, bf16[8,8,64,1024]{2,3,1,0:T(8,128)(2,1)} %get-tuple-element.6), kind=kLoop, calls=%fused_computation.4 | loop fusion | flops 8388608 | bytes 33554432 | tf_op jit(solution)/shard_map/max | solution.py:58
  158.3 16.1 %fusion.77 = (bf16[64,8,1024]{1,2,0:T(8,128)(2,1)}, bf16[64,8,1024]{1,2,0:T(8,128)(2,1)}) fusion(bf16[64,64,1024]{1,2,0:T(8,128)(2,1)S(1)} %bitcast_maximum_fusion), kind=kLoop, calls=%fused_computation.132 | loop fusion | bytes 4194304 | tf_op jit(solution)/shard_map/slice | solution.py:20
  174.4 0.0 copy-start.4
  174.4 11.6 %copy.27 = bf16[64,8,1024]{2,1,0:T(8,128)(2,1)S(1)} copy(bf16[64,8,1024]{1,2,0:T(8,128)(2,1)} %get-tuple-element.9) | data formatting | bytes 2097152 | tf_op jit(solution)/shard_map/slice | solution.py:20
  186.1 4.6 %collective-permute-start.2 = (bf16[64,8,1024]{2,1,0:T(8,128)(2,1)S(1)}, bf16[64,8,1024]{2,1,0:T(8,128)(2,1)S(1)}, u32[]{:S(2)}, u32[]{:S(2)}) collective-permute-start(bf16[64,8,1024]{2,1,0:T(8,128)(2,1)S(1)} %copy.27), channel_id=1, source_target_pairs={{0,8},{8,16},{16,24},{24,32},{32,40},{40,48},{48,56},{56,64},{64,7... | collective-permute-start | bytes 3145736 | tf_op jit(solution)/shard_map/ppermute | solution.py:22
  190.7 11.6 %copy.28 = bf16[64,8,1024]{2,1,0:T(8,128)(2,1)S(1)} copy(bf16[64,8,1024]{1,2,0:T(8,128)(2,1)} %get-tuple-element.10) | data formatting | bytes 2097152 | tf_op jit(solution)/shard_map/slice | solution.py:21
  202.3 1.9 collective-permute-start.3
  204.2 0.7 fusion.83
  205.0 14.4 %multiply_add_fusion = f32[8,8192]{1,0:T(8,128)S(1)} fusion(f32[8,8192]{1,0:T(8,128)} %param.5, f32[]{:T(128)} %bitcast.15, f32[]{:T(128)} %bitcast.14, f32[]{:T(128)} %bitcast.13, f32[]{:T(128)} %bitcast.12, f32[]{:T(128)} %bitcast.11, f32[]{:T(128)} %bitcast.10, f32[]{:T(128)} %bitcast.9, f32[]{:T(128)} %bitcast.8, f32[]{:T(128)} %bitcast.7, f32[]{:T(128)} %bitcast.6, ...), kind=kLoop, calls=%fused_computation.106 | loop fusion | flops 1900544 | bytes 524348 | tf_op jit(solution)/shard_map/add | solution.py:34
  219.3 0.8 fusion.81
  220.2 3.5 %collective-permute-start = (f32[7,8192]{1,0:T(8,128)}, f32[7,8192]{1,0:T(8,128)}, u32[]{:S(2)}, u32[]{:S(2)}) collective-permute-start(f32[7,8192]{1,0:T(8,128)} %get-tuple-element.19), channel_id=1, source_target_pairs={{0,1},{1,2},{2,3},{3,4},{4,5},{5,6},{6,7},{7,8},{8,9},{9,10},{10,1... | collective-permute-start | bytes 688136 | tf_op jit(solution)/shard_map/ppermute | solution.py:22
  223.7 3.8 %collective-permute-start.1 = (f32[7,8192]{1,0:T(8,128)}, f32[7,8192]{1,0:T(8,128)}, u32[]{:S(2)}, u32[]{:S(2)}) collective-permute-start(f32[7,8192]{1,0:T(8,128)} %get-tuple-element.20), channel_id=1, source_target_pairs={{1,0},{2,1},{3,2},{4,3},{5,4},{6,5},{7,6},{8,7},{9,8},{10,9},{11,1... | collective-permute-start | bytes 688136 | tf_op jit(solution)/shard_map/ppermute | solution.py:23
  227.6 0.7 iota_add_fusion
  228.3 0.7 iota_add_fusion.1
  229.0 0.7 fusion.82
  229.7 0.0 collective-permute-done.2
  229.7 9.9 %copy.29 = bf16[64,8,1024]{1,2,0:T(8,128)(2,1)} copy(bf16[64,8,1024]{2,1,0:T(8,128)(2,1)S(1)} %collective-permute-done.2) | data formatting | bytes 2097152 | tf_op jit(solution)/shard_map/ppermute | solution.py:22
  239.6 0.0 collective-permute-done.3
  239.6 11.5 %copy.30 = bf16[64,8,1024]{1,2,0:T(8,128)(2,1)} copy(bf16[64,8,1024]{2,1,0:T(8,128)(2,1)} %collective-permute-done.3) | data formatting | bytes 2097152 | tf_op jit(solution)/shard_map/ppermute | solution.py:23
  251.1 2.1 pad_maximum_fusion.8
  253.2 1.9 collective-permute-start.4
  255.1 13.5 %fusion.28 = f32[8,8192]{1,0:T(8,128)} fusion(f32[8,8192]{1,0:T(8,128)S(1)} %multiply_add_fusion, f32[7,8192]{1,0:T(8,128)} %collective-permute-done.1, f32[7,8192]{1,0:T(8,128)} %collective-permute-done, f32[]{:T(128)} %bitcast.29, f32[]{:T(128)} %bitcast.28, f32[]{:T(128)} %bitcast.27, f32[]{:T(128)} %bitcast.26, f32[]{:T(128)} %bitcast.25, f32[]{:T(128)} %bitcast.24, ...), kind=kLoop, calls=%fused_computation.67 | loop fusion | flops 2818048 | bytes 983100 | tf_op jit(solution)/shard_map/add | solution.py:41
  268.6 6.4 %all-to-all-start = ((f32[8,8,1024]{2,0,1:T(8,128)}), f32[8,8,1024]{2,0,1:T(8,128)}, u32[]{:S(2)}, u32[]{:S(2)}) async-start(f32[8,8,1024]{2,0,1:T(8,128)} %bitcast.30), calls=%async_computation | async-start | bytes 524288 | tf_op jit(solution)/shard_map/all_to_all | solution.py:93
  275.1 4.7 %collective-permute-start.5 = (bf16[64,80,8]{1,2,0:T(8,128)(2,1)S(1)}, bf16[64,80,8]{1,2,0:T(8,128)(2,1)}, u32[]{:S(2)}, u32[]{:S(2)}) collective-permute-start(bf16[64,80,8]{1,2,0:T(8,128)(2,1)S(1)} %get-tuple-element.7), channel_id=1, source_target_pairs={{1,0},{2,1},{3,2},{4,3},{5,4},{6,5},{7,6},{9,8},{10,9},{11,10},{12... | collective-permute-start | bytes 245768 | tf_op jit(solution)/shard_map/ppermute | solution.py:23
  279.8 6.0 %fusion.19 = bf16[64,80,8,144]{1,3,2,0:T(8,128)(2,1)} fusion(bf16[64,80,8]{1,2,0:T(8,128)(2,1)} %collective-permute-done.4, bf16[64,8,1024]{1,2,0:T(8,128)(2,1)} %copy.30, bf16[64,64,1024]{1,2,0:T(8,128)(2,1)} %copy-done, bf16[64,8,1024]{1,2,0:T(8,128)(2,1)} %copy.29), kind=kLoop, calls=%fused_computation.31 | loop fusion | flops 5898239 | bytes 12926976
  285.9 1.5 slice-done.6
  287.4 1.2 slice-done.7
  288.6 5.3 %fusion.17 = bf16[64,80,8,144]{1,3,2,0:T(8,128)(2,1)} fusion(bf16[64,80,8,144]{1,3,2,0:T(8,128)(2,1)} %fusion.19, bf16[64,8,1024]{1,2,0:T(8,128)(2,1)} %copy.30, bf16[64,64,1024]{1,2,0:T(8,128)(2,1)S(1)} %bitcast.116, bf16[64,8,1024]{1,2,0:T(8,128)(2,1)S(1)} %bitcast.118), kind=kLoop, calls=%fused_computation.28 | loop fusion | flops 4423680 | bytes 28573696
  293.9 5.3 %fusion.16 = bf16[64,80,8,144]{1,3,2,0:T(8,128)(2,1)} fusion(bf16[64,80,8,144]{1,3,2,0:T(8,128)(2,1)} %fusion.17, bf16[64,8,1024]{1,2,0:T(8,128)(2,1)} %copy.30, bf16[64,64,1024]{1,2,0:T(8,128)(2,1)S(1)} %bitcast.116, bf16[64,8,1024]{1,2,0:T(8,128)(2,1)S(1)} %bitcast.118), kind=kLoop, calls=%fused_computation.26 | loop fusion | flops 4423680 | bytes 28573696
  299.2 5.2 %fusion.15 = bf16[64,80,8,144]{1,3,2,0:T(8,128)(2,1)} fusion(bf16[64,80,8,144]{1,3,2,0:T(8,128)(2,1)} %fusion.16, bf16[64,8,1024]{1,2,0:T(8,128)(2,1)} %copy.30, bf16[64,64,1024]{1,2,0:T(8,128)(2,1)S(1)} %bitcast.116, bf16[64,8,1024]{1,2,0:T(8,128)(2,1)S(1)} %bitcast.118), kind=kLoop, calls=%fused_computation.24 | loop fusion | flops 4423680 | bytes 28573696
  304.4 5.2 %fusion.14 = bf16[64,80,8,144]{1,3,2,0:T(8,128)(2,1)} fusion(bf16[64,80,8,144]{1,3,2,0:T(8,128)(2,1)} %fusion.15, bf16[64,8,1024]{1,2,0:T(8,128)(2,1)} %copy.30, bf16[64,64,1024]{1,2,0:T(8,128)(2,1)S(1)} %bitcast.116, bf16[64,8,1024]{1,2,0:T(8,128)(2,1)S(1)} %bitcast.118), kind=kLoop, calls=%fused_computation.22 | loop fusion | flops 4423680 | bytes 28573696
  309.7 5.3 %fusion.13 = bf16[64,80,8,144]{1,3,2,0:T(8,128)(2,1)} fusion(bf16[64,80,8,144]{1,3,2,0:T(8,128)(2,1)} %fusion.14, bf16[64,8,1024]{1,2,0:T(8,128)(2,1)} %copy.30, bf16[64,64,1024]{1,2,0:T(8,128)(2,1)S(1)} %bitcast.116, bf16[64,8,1024]{1,2,0:T(8,128)(2,1)S(1)} %bitcast.118), kind=kLoop, calls=%fused_computation.20 | loop fusion | flops 4423680 | bytes 28573696
  315.0 5.6 %fusion.12 = bf16[64,80,8,144]{1,3,2,0:T(8,128)(2,1)} fusion(bf16[64,80,8,144]{1,3,2,0:T(8,128)(2,1)} %fusion.13, bf16[64,8,1024]{1,2,0:T(8,128)(2,1)} %copy.30, bf16[64,64,1024]{1,2,0:T(8,128)(2,1)S(1)} %bitcast.116, bf16[64,8,1024]{1,2,0:T(8,128)(2,1)S(1)} %bitcast.118), kind=kLoop, calls=%fused_computation.18 | loop fusion | flops 4423680 | bytes 28573696
  320.5 4.6 %fusion.11 = bf16[64,80,8,144]{1,3,2,0:T(8,128)(2,1)} fusion(bf16[64,80,8,144]{1,3,2,0:T(8,128)(2,1)} %fusion.12, bf16[64,80,8]{1,2,0:T(8,128)(2,1)} %collective-permute-done.5, bf16[64,8,1024]{1,2,0:T(8,128)(2,1)} %copy.30, bf16[64,64,1024]{1,2,0:T(8,128)(2,1)S(1)} %bitcast.116, bf16[64,8,1024]{1,2,0:T(8,128)(2,1)S(1)} %bitcast.118), kind=kLoop, calls=%fused_computation.14 | loop fusion | flops 5898240 | bytes 28704768 | tf_op jit(solution)/shard_map/stack | solution.py:65
  325.2 17.6 %multiply_bitcast_fusion = f32[64,8,8,8,128]{4,3,2,1,0:T(8,128)} fusion(bf16[64,80,8,144]{1,3,2,0:T(8,128)(2,1)} %fusion.11, s32[64,128]{1,0:T(8,128)S(1)} %copy-done.1, s32[64,64]{1,0:T(8,128)S(1)} %copy-done.2), kind=kOutput, calls=%fused_computation.6 | convolution fusion | flops 2191982592 | bytes 28622848 | tf_op jit(solution)/shard_map/vsr,vrnc->vsnc/dot_general | solution.py:84
  342.8 9.7 %fusion = bf16[64,64,1024]{2,1,0:T(8,128)(2,1)} fusion(f32[64,8,8,8,128]{4,3,2,1,0:T(8,128)} %multiply_bitcast_fusion, f32[64,1024]{1,0:T(8,128)} %bitcast.32), kind=kLoop, calls=%fused_computation.1 | loop fusion | flops 8388608 | bytes 25427968 | tf_op jit(solution)/shard_map/convert_element_type | solution.py:99
  (33 shorter events, 0.1 us)
Async XLA Ops:
  158.3 16.1 %copy-start = (bf16[64,64,1024]{1,2,0:T(8,128)(2,1)}, bf16[64,64,1024]{1,2,0:T(8,128)(2,1)S(1)}, u32[]{:S(2)}) copy-start(bf16[64,64,1024]{1,2,0:T(8,128)(2,1)S(1)} %bitcast_maximum_fusion) | copy-start | bytes 25165828
  174.4 29.9 %copy-start.3 = (f32[15]{0:T(128)S(1)}, f32[15]{0:T(128)}, u32[]{:S(2)}) copy-start(f32[15]{0:T(128)} %param.6) | copy-start | bytes 184
  174.4 53.2 %copy-start.5 = (s32[64,2]{0,1:T(2,128)S(1)}, s32[64,2]{0,1:T(2,128)}, u32[]{:S(2)}) copy-start(s32[64,2]{0,1:T(2,128)} %param.9) | copy-start | bytes 1540
  174.4 54.6 %copy-start.4 = (f32[15]{0:T(128)S(1)}, f32[15]{0:T(128)}, u32[]{:S(2)}) copy-start(f32[15]{0:T(128)} %param.7) | copy-start | bytes 184
  186.1 43.6 %collective-permute-start.2 = (bf16[64,8,1024]{2,1,0:T(8,128)(2,1)S(1)}, bf16[64,8,1024]{2,1,0:T(8,128)(2,1)S(1)}, u32[]{:S(2)}, u32[]{:S(2)}) collective-permute-start(bf16[64,8,1024]{2,1,0:T(8,128)(2,1)S(1)} %copy.27), channel_id=1, source_target_pairs={{0,8},{8,16},{16,24},{24,32},{32,40},{40,48},{48,56},{56,64},{64,7... | collective-permute-start | bytes 3145736 | tf_op jit(solution)/shard_map/ppermute | solution.py:22
  202.3 37.3 %collective-permute-start.3 = (bf16[64,8,1024]{2,1,0:T(8,128)(2,1)S(1)}, bf16[64,8,1024]{2,1,0:T(8,128)(2,1)}, u32[]{:S(2)}, u32[]{:S(2)}) collective-permute-start(bf16[64,8,1024]{2,1,0:T(8,128)(2,1)S(1)} %copy.28), channel_id=1, source_target_pairs={{8,0},{16,8},{24,16},{32,24},{40,32},{48,40},{56,48},{64,56},{72,6... | collective-permute-start | bytes 3145736 | tf_op jit(solution)/shard_map/ppermute | solution.py:23
  220.2 35.0 %collective-permute-start = (f32[7,8192]{1,0:T(8,128)}, f32[7,8192]{1,0:T(8,128)}, u32[]{:S(2)}, u32[]{:S(2)}) collective-permute-start(f32[7,8192]{1,0:T(8,128)} %get-tuple-element.19), channel_id=1, source_target_pairs={{0,1},{1,2},{2,3},{3,4},{4,5},{5,6},{6,7},{7,8},{8,9},{9,10},{10,1... | collective-permute-start | bytes 688136 | tf_op jit(solution)/shard_map/ppermute | solution.py:22
  223.7 31.4 %collective-permute-start.1 = (f32[7,8192]{1,0:T(8,128)}, f32[7,8192]{1,0:T(8,128)}, u32[]{:S(2)}, u32[]{:S(2)}) collective-permute-start(f32[7,8192]{1,0:T(8,128)} %get-tuple-element.20), channel_id=1, source_target_pairs={{1,0},{2,1},{3,2},{4,3},{5,4},{6,5},{7,6},{8,7},{9,8},{10,9},{11,1... | collective-permute-start | bytes 688136 | tf_op jit(solution)/shard_map/ppermute | solution.py:23
  253.2 26.6 %collective-permute-start.4 = (bf16[64,80,8]{1,2,0:T(8,128)(2,1)}, bf16[64,80,8]{1,2,0:T(8,128)(2,1)}, u32[]{:S(2)}, u32[]{:S(2)}) collective-permute-start(bf16[64,80,8]{1,2,0:T(8,128)(2,1)} %get-tuple-element.8), channel_id=1, source_target_pairs={{0,1},{1,2},{2,3},{3,4},{4,5},{5,6},{6,7},{8,9},{9,10},{10,11},{11... | collective-permute-start | bytes 245768 | tf_op jit(solution)/shard_map/ppermute | solution.py:22
  268.6 74.2 %all-to-all-start = ((f32[8,8,1024]{2,0,1:T(8,128)}), f32[8,8,1024]{2,0,1:T(8,128)}, u32[]{:S(2)}, u32[]{:S(2)}) async-start(f32[8,8,1024]{2,0,1:T(8,128)} %bitcast.30), calls=%async_computation | async-start | bytes 524288 | tf_op jit(solution)/shard_map/all_to_all | solution.py:93
  275.1 10.8 %slice-start = ((s8[16777216]{0:T(1024)(128)(4,1)}), s8[4194304]{0:T(1024)(128)(4,1)S(1)}, s32[]{:S(2)}) async-start(s8[16777216]{0:T(1024)(128)(4,1)} %bitcast.115), calls=%async_computation.1 | async-start | bytes 8388608
  275.1 10.8 %slice-start.4 = ((s8[16777216]{0:T(1024)(128)(4,1)}), s8[4194304]{0:T(1024)(128)(4,1)S(1)}, s32[]{:S(2)}) async-start(s8[16777216]{0:T(1024)(128)(4,1)} %bitcast.117), calls=%async_computation.5 | async-start | bytes 8388608
  275.1 10.8 %slice-start.1 = ((s8[16777216]{0:T(1024)(128)(4,1)}), s8[4194304]{0:T(1024)(128)(4,1)S(1)}, s32[]{:S(2)}) async-start(s8[16777216]{0:T(1024)(128)(4,1)} %bitcast.115), calls=%async_computation.2 | async-start | bytes 8388608
  275.1 10.8 %slice-start.2 = ((s8[16777216]{0:T(1024)(128)(4,1)}), s8[4194304]{0:T(1024)(128)(4,1)S(1)}, s32[]{:S(2)}) async-start(s8[16777216]{0:T(1024)(128)(4,1)} %bitcast.115), calls=%async_computation.3 | async-start | bytes 8388608
  275.1 10.8 %slice-start.3 = ((s8[16777216]{0:T(1024)(128)(4,1)}), s8[4194304]{0:T(1024)(128)(4,1)S(1)}, s32[]{:S(2)}) async-start(s8[16777216]{0:T(1024)(128)(4,1)} %bitcast.115), calls=%async_computation.4 | async-start | bytes 8388608
  275.1 10.8 %slice-start.5 = ((s8[16777216]{0:T(1024)(128)(4,1)}), s8[4194304]{0:T(1024)(128)(4,1)S(1)}, s32[]{:S(2)}) async-start(s8[16777216]{0:T(1024)(128)(4,1)} %bitcast.117), calls=%async_computation.6 | async-start | bytes 8388608
  275.1 12.3 %slice-start.6 = ((s8[16777216]{0:T(1024)(128)(4,1)}), s8[4194304]{0:T(1024)(128)(4,1)S(1)}, s32[]{:S(2)}) async-start(s8[16777216]{0:T(1024)(128)(4,1)} %bitcast.117), calls=%async_computation.7 | async-start | bytes 8388608
  275.1 13.5 %slice-start.7 = ((s8[16777216]{0:T(1024)(128)(4,1)}), s8[4194304]{0:T(1024)(128)(4,1)S(1)}, s32[]{:S(2)}) async-start(s8[16777216]{0:T(1024)(128)(4,1)} %bitcast.117), calls=%async_computation.8 | async-start | bytes 8388608
  275.1 45.4 %collective-permute-start.5 = (bf16[64,80,8]{1,2,0:T(8,128)(2,1)S(1)}, bf16[64,80,8]{1,2,0:T(8,128)(2,1)}, u32[]{:S(2)}, u32[]{:S(2)}) collective-permute-start(bf16[64,80,8]{1,2,0:T(8,128)(2,1)S(1)} %get-tuple-element.7), channel_id=1, source_target_pairs={{1,0},{2,1},{3,2},{4,3},{5,4},{6,5},{7,6},{9,8},{10,9},{11,10},{12... | collective-permute-start | bytes 245768 | tf_op jit(solution)/shard_map/ppermute | solution.py:23
  320.5 4.6 %copy-start.1 = (s32[64,128]{1,0:T(8,128)S(1)}, s32[64,128]{1,0:T(8,128)}, u32[]{:S(2)}) copy-start(s32[64,128]{1,0:T(8,128)} %iota_add_fusion) | copy-start | bytes 98308
  320.5 4.6 %copy-start.2 = (s32[64,64]{1,0:T(8,128)S(1)}, s32[64,64]{1,0:T(8,128)}, u32[]{:S(2)}) copy-start(s32[64,64]{1,0:T(8,128)} %iota_add_fusion.1) | copy-start | bytes 49156
where the time goes:
time: 358 us; the launch traced here: 353 us
  local copies, waits for them, and re-layouts  170 us (47%)
  other arithmetic  137 us (38%)
  starting transfers between devices  26.9 us (8%)
  matrix products  17.6 us (5%)
    max x3, other arithmetic, neighbour_max(): return jnp.maximum(grid, jnp.maximum(lower, upper))  53.5 us
    unnamed x9, other arithmetic  37.9 us
    slice x2, local copies, waits for them, and re-layouts, neighbour_max(): lax.slice_in_dim(grid, 1, total, axis=axis)  37.4 us
    slice x3, local copies, waits for them, and re-layouts, with_halo(): last = lax.slice_in_dim(value, length - width, length, axis=dim)  28.6 us
    slice x2, local copies, waits for them, and re-layouts, neighbour_max(): lax.slice_in_dim(grid, 0, total - 1, axis=axis)  24.9 us
    unnamed x29, local copies, waits for them, and re-layouts  18.3 us
    dot_general x1, matrix products, move_planes(): jnp.einsum('vsr,vrnc->vsnc', select_row, moved, preferred_element_type=jn...  17.6 us
    reshape x1, local copies, waits for them, and re-layouts, on_device(): grid = merit.reshape(VGRID, VGRID, tile_rows, tile_cols)  15.6 us
  transfers between devices with their start and end apart: 7, of which 0 were waited for; matrix products, arithmetic and copies ran while one was open for 36% of the time, Pallas kernels for 0%

commit v1 on v0

v1 whole, which is shorter than its diff:
```python
import functools

import jax
import jax.numpy as jnp
from jax import lax
from jax.experimental import pallas as pl
from jax.experimental.pallas import tpu as pltpu
from jax.sharding import PartitionSpec as P

VGRID = 8
MAXV = 8
VELS = VGRID * VGRID
LANES = 128
FORGET = 0.875
SEAM = 16
SOME_ROWS = 192
ALL_ROWS = VELS * MAXV
LIMIT = 56 * 2**20

f32 = jnp.float32
bf16 = jnp.bfloat16


def params(limit=LIMIT):
    return pltpu.CompilerParams(vmem_limit_bytes=limit)


def smem():
    return pl.BlockSpec(memory_space=pltpu.SMEM)


def filter_rows_kernel(taps_ref, strip_ref, out_ref, pad_ref):
    half = taps_ref.shape[0] // 2
    height, width = strip_ref.shape
    pad_ref[:, :LANES] = jnp.zeros((height, LANES), f32)
    pad_ref[:, LANES + width :] = jnp.zeros((height, LANES), f32)
    pad_ref[:, LANES : LANES + width] = strip_ref[...]
    count, _, span = out_ref.shape
    for piece in range(count):
        start = LANES + piece * span
        total = jnp.zeros((height, span), f32)
        for j in range(taps_ref.shape[0]):
            total = total + taps_ref[j] * pad_ref[:, start + j - half : start + j - half + span]
        out_ref[piece] = total


def filter_rows(strip, taps_row, pieces):
    height, width = strip.shape
    return pl.pallas_call(
        filter_rows_kernel,
        out_shape=jax.ShapeDtypeStruct((pieces, height, width // pieces), f32),
        in_specs=[smem(), pl.BlockSpec(memory_space=pltpu.VMEM)],
        out_specs=pl.BlockSpec(memory_space=pltpu.VMEM),
        scratch_shapes=[pltpu.VMEM((height, width + 2 * LANES), f32)],
        compiler_params=params(),
        name="filter_rows",
    )(taps_row, strip)


def max_of_three(values):
    total = len(values)
    pairs = [jnp.maximum(values[i], values[i + 1]) for i in range(total - 1)]
    middle = [jnp.maximum(pairs[i - 1], values[i + 1]) for i in range(1, total - 1)]
    return [pairs[0]] + middle + [pairs[-1]]


def pool_kernel(rows, offsets_ref, merit_ref, pooled_ref, right_ref, left_ref, down_ref, up_ref, bottom_ref, top_ref):
    step = pl.program_id(0)
    steps = pl.num_programs(0)
    _, height, width = merit_ref.shape
    blocks = width // LANES

    def pool_block(k, carry):
        cols = pl.ds(pl.multiple_of(k * LANES, LANES), LANES)

        def line(a):
            return max_of_three([merit_ref[a * VGRID + b, :, cols] for b in range(VGRID)])

        def emit(a, planes):
            for b in range(VGRID):
                pooled_ref[a * VGRID + b, :, cols] = planes[b]

        last, here = line(0), line(1)
        pair = [jnp.maximum(x, y) for x, y in zip(last, here)]
        emit(0, pair)
        for a in range(2, VGRID):
            after = line(a)
            emit(a - 1, [jnp.maximum(x, y) for x, y in zip(pair, after)])
            pair = [jnp.maximum(x, y) for x, y in zip(here, after)]
            here = after
        emit(VGRID - 1, pair)
        return carry

    lax.fori_loop(0, blocks, pool_block, 0)

    lane_group = lax.broadcasted_iota(jnp.int32, (height, LANES), 1) // MAXV
    share = LANES // MAXV
    for g in range(VELS // share):
        right = jnp.zeros((height, LANES), f32)
        left = jnp.zeros((height, LANES), f32)
        for w in range(share):
            v = g * share + w
            last = pooled_ref[v, :, width - LANES :].astype(f32)
            first = pooled_ref[v, :, :LANES].astype(f32)
            right = jnp.where(lane_group == w, pltpu.roll(last, (w + 1) * MAXV % LANES, 1), right)
            left = jnp.where(lane_group == w, pltpu.roll(first, w * MAXV, 1), left)
        right_ref[g] = right.astype(bf16)
        left_ref[g] = left.astype(bf16)

    @pl.when(step == 0)
    def _():
        def pack(v, at):
            for k in range(blocks):
                tile = pooled_ref[v, :, k * LANES : (k + 1) * LANES].astype(f32)
                top_ref[k, pl.ds(at + MAXV, MAXV), :] = tile[:MAXV]
            return at + jnp.maximum(-offsets_ref[v, 0], 0)

        lax.fori_loop(0, VELS, pack, 0)
        for k in range(blocks):
            up_ref[SEAM:, k * LANES : (k + 1) * LANES] = top_ref[k, MAXV : MAXV + rows, :].astype(bf16)

    @pl.when(step == steps - 1)
    def _():
        def count(v, total):
            return total + jnp.maximum(offsets_ref[v, 0], 0)

        def pack(i, at):
            v = VELS - 1 - i
            for k in range(blocks):
                tile = pooled_ref[v, :, k * LANES : (k + 1) * LANES].astype(f32)
                bottom_ref[k, pl.ds(at, MAXV), :] = tile[height - MAXV :]
            return at - jnp.maximum(offsets_ref[v, 0], 0)

        lax.fori_loop(0, VELS, pack, lax.fori_loop(0, VELS, count, 0))
        for k in range(blocks):
            down_ref[SEAM:, k * LANES : (k + 1) * LANES] = bottom_ref[k, MAXV : MAXV + rows, :].astype(bf16)


def pool(merit, offsets, rows):
    planes, height, width = merit.shape
    chunk = 16
    blocks = width // LANES
    groups = planes * MAXV // LANES
    whole = pl.BlockSpec((SEAM + rows, width), lambda i: (0, 0))
    sides = pl.BlockSpec((groups, chunk, LANES), lambda i: (0, i, 0))
    return pl.pallas_call(
        functools.partial(pool_kernel, rows),
        grid=(height // chunk,),
        out_shape=[
            jax.ShapeDtypeStruct(merit.shape, bf16),
            jax.ShapeDtypeStruct((groups, height, LANES), bf16),
            jax.ShapeDtypeStruct((groups, height, LANES), bf16),
            jax.ShapeDtypeStruct((SEAM + rows, width), bf16),
            jax.ShapeDtypeStruct((SEAM + rows, width), bf16),
        ],
        in_specs=[smem(), pl.BlockSpec((planes, chunk, width), lambda i: (0, i, 0))],
        out_specs=[pl.BlockSpec((planes, chunk, width), lambda i: (0, i, 0)), sides, sides, whole, whole],
        scratch_shapes=[pltpu.VMEM((blocks, ALL_ROWS + 2 * MAXV, LANES), f32)] * 2,
        cost_estimate=pl.CostEstimate(flops=4 * merit.size, bytes_accessed=4 * merit.size, transcendentals=0),
        compiler_params=params(),
        name="pool",
    )(offsets, merit)


def seam_kernel(tile_ref, down_in, up_in, down_ref, up_ref, buf_ref, sems):
    del down_in, up_in
    height = tile_ref.shape[0]
    for i, (edge, target) in enumerate(((tile_ref[height - MAXV :, :], down_ref), (tile_ref[:MAXV, :], up_ref))):
        lead = edge.astype(bf16).astype(f32)
        buf_ref[i] = jnp.concatenate([lead, edge - lead], axis=0).astype(bf16)
    copies = [
        pltpu.make_async_copy(buf_ref.at[i], target.at[pl.ds(0, SEAM), :], sems.at[i])
        for i, target in enumerate((down_ref, up_ref))
    ]
    for copy in copies:
        copy.start()
    for copy in copies:
        copy.wait()


def add_seam(tile, down, up):
    anywhere = pl.BlockSpec(memory_space=pl.ANY)
    return pl.pallas_call(
        seam_kernel,
        out_shape=[jax.ShapeDtypeStruct(down.shape, bf16), jax.ShapeDtypeStruct(up.shape, bf16)],
        in_specs=[pl.BlockSpec(memory_space=pltpu.VMEM), anywhere, anywhere],
        out_specs=[anywhere, anywhere],
        input_output_aliases={1: 0, 2: 1},
        scratch_shapes=[pltpu.VMEM((2, SEAM, tile.shape[1]), bf16), pltpu.SemaphoreType.DMA((2,))],
        compiler_params=params(),
        name="add_seam",
    )(tile, down, up)


def merge_kernel(
    rows, offsets_ref, taps_ref, pooled_ref, tile_ref, above_ref, below_ref, west_ref, east_ref, out_ref,
    halo_ref, side_ref, column_ref, filtered_ref, moved_ref, at_ref,
):
    step = pl.program_id(0)
    planes, height, width = pooled_ref.shape
    blocks = width // LANES
    groups = VELS * MAXV // LANES
    share = LANES // MAXV

    @pl.when(step == 0)
    def _():
        at_ref[0] = 0
        at_ref[1] = 0
        near = groups * height
        for e, ref in enumerate((above_ref, below_ref)):
            for k in range(blocks):
                halo_ref[e, k + 1, MAXV : MAXV + rows, :] = ref[SEAM:, k * LANES : (k + 1) * LANES].astype(f32)
            start = near + e * rows
            halo_ref[e, 0, MAXV : MAXV + rows, :] = west_ref[start : start + rows, :].astype(f32)
            halo_ref[e, blocks + 1, MAXV : MAXV + rows, :] = east_ref[start : start + rows, :].astype(f32)
        for e, ref in enumerate((west_ref, east_ref)):
            for g in range(groups):
                side_ref[e, g] = ref[g * height : (g + 1) * height, :].astype(f32)
        half = taps_ref.shape[0] // 2
        for k in range(blocks):
            cols = slice(k * LANES, (k + 1) * LANES)
            over = above_ref[:SEAM, cols].astype(f32)
            under = below_ref[:SEAM, cols].astype(f32)
            column_ref[k, :MAXV, :] = over[:MAXV] + over[MAXV:]
            column_ref[k, MAXV : MAXV + height, :] = tile_ref[:, cols]
            column_ref[k, MAXV + height :, :] = under[:MAXV] + under[MAXV:]
        for k in range(blocks):
            total = jnp.zeros((height, LANES), f32)
            for i in range(taps_ref.shape[0]):
                start = MAXV - half + i
                total = total + taps_ref[i] * column_ref[k, start : start + height, :]
            filtered_ref[k] = total

    moves = []
    for p in range(planes):
        v = step * planes + p
        dy = offsets_ref[v, 0]
        dx = offsets_ref[v, 1]
        turn = dx & (LANES - 1)
        west = dx >= 0
        q = jnp.where(west, 0, 1)
        moves.append((dy, turn, q))
        for k in range(blocks):
            here = pooled_ref[p, :, k * LANES : (k + 1) * LANES].astype(f32)
            moved_ref[p, k + 1, MAXV : MAXV + height, :] = pltpu.roll(here, turn, 1)
        g, w = v // share, v % share
        shift = (turn - w * MAXV - jnp.where(west, MAXV, 0) + 2 * LANES) & (LANES - 1)
        moved_ref[p, q * (blocks + 1), MAXV : MAXV + height, :] = pltpu.roll(side_ref[q, g], shift, 1)
        e = jnp.where(dy >= 0, 0, 1)
        source = jnp.where(dy >= 0, at_ref[0] + dy, at_ref[1] + MAXV)
        target = pl.multiple_of(e * (MAXV + height), MAXV)
        for k in range(blocks + 2):
            edge = halo_ref[e, k, pl.ds(source, MAXV), :]
            moved_ref[p, k, pl.ds(target, MAXV), :] = pltpu.roll(edge, turn, 1)
        at_ref[0] += jnp.maximum(dy, 0)
        at_ref[1] += jnp.maximum(-dy, 0)

    lane = lax.broadcasted_iota(jnp.int32, (height, LANES), 1)
    for p in range(planes):
        dy, turn, q = moves[p]
        window = pl.ds(MAXV - dy, height)
        for k in range(blocks):
            one = moved_ref[p, k + q, window, :]
            two = moved_ref[p, k + 1 + q, window, :]
            total = filtered_ref[k] + FORGET * jnp.where(lane < turn, one, two)
            out_ref[p, :, k * LANES : (k + 1) * LANES] = total.astype(bf16)


def merge(pooled, tile, above, below, west, east, offsets, taps_col):
    planes, height, width = pooled.shape
    rows = above.shape[0] - SEAM
    blocks = width // LANES
    groups = planes * MAXV // LANES
    slab = pl.BlockSpec((VGRID, height, width), lambda i: (i, 0, 0))

    def whole(array):
        return pl.BlockSpec(array.shape, lambda i: (0, 0))

    return pl.pallas_call(
        functools.partial(merge_kernel, rows),
        grid=(planes // VGRID,),
        out_shape=jax.ShapeDtypeStruct(pooled.shape, bf16),
        in_specs=[smem(), smem(), slab] + [whole(a) for a in (tile, above, below, west, east)],
        out_specs=slab,
        scratch_shapes=[
            pltpu.VMEM((2, blocks + 2, rows + 2 * MAXV, LANES), f32),
            pltpu.VMEM((2, groups, height, LANES), f32),
            pltpu.VMEM((blocks, height + 2 * MAXV, LANES), f32),
            pltpu.VMEM((blocks, height, LANES), f32),
            pltpu.VMEM((VGRID, blocks + 2, height + 2 * MAXV, LANES), f32),
            pltpu.SMEM((2,), jnp.int32),
        ],
        compiler_params=params(),
        name="merge",
    )(offsets, taps_col, pooled, tile, above, below, west, east)


def pass_on(value, axis):
    count = lax.axis_size(axis)
    return lax.ppermute(value, axis, [(i, i + 1) for i in range(count - 1)])


def pass_back(value, axis):
    count = lax.axis_size(axis)
    return lax.ppermute(value, axis, [(i + 1, i) for i in range(count - 1)])


def step_with(rows, frame, taps_row, taps_col, merit, offsets):
    _, height, width = merit.shape
    pieces = filter_rows(frame, taps_row, frame.shape[1] // width)
    tile = lax.all_to_all(pieces, "cols", split_axis=0, concat_axis=0, tiled=True).reshape(height, width)
    pooled, right, left, down, up = pool(merit, offsets, rows)
    down, up = add_seam(tile, down, up)
    above = pass_on(down, "rows")
    below = pass_back(up, "rows")
    last = [right.reshape(-1, LANES), above[SEAM:, width - LANES :], below[SEAM:, width - LANES :]]
    first = [left.reshape(-1, LANES), above[SEAM:, :LANES], below[SEAM:, :LANES]]
    west = pass_on(jnp.concatenate(last, axis=0), "cols")
    east = pass_back(jnp.concatenate(first, axis=0), "cols")
    return merge(pooled, tile, above, below, west, east, offsets, taps_col)


def on_device(frame, taps_row, taps_col, merit, offsets):
    shifts = offsets[:, 0]
    most = jnp.maximum(jnp.sum(jnp.maximum(shifts, 0)), jnp.sum(jnp.maximum(-shifts, 0)))
    return lax.cond(
        most <= SOME_ROWS,
        functools.partial(step_with, SOME_ROWS),
        functools.partial(step_with, ALL_ROWS),
        frame, taps_row, taps_col, merit, offsets,
    )


def solution(mesh):
    in_specs = (P(("rows", "cols"), None), P(), P(), P(None, "rows", "cols"), P())
    out_specs = P(None, "rows", "cols")
    return jax.shard_map(on_device, mesh=mesh, in_specs=in_specs, out_specs=out_specs, check_vma=False)
```

time: 358 us -> 67.8 us (0.19); the launches traced: 353 us -> 67.2 us
  local copies, waits for them, and re-layouts: 170 us -> 2.77 us
  other arithmetic: 137 us -> 1.42 us
  Pallas kernels: 0 us -> 27.7 us
  matrix products: 17.6 us -> 0 us
  waiting for transfers between devices: 0.02 us -> 13.1 us
  starting transfers between devices: 26.9 us -> 20.7 us
    slice x14 -> x2, local copies, waits for them, and re-layouts: 115 us -> 0.03 us  [the longest x1 0.01 us: step_with(): above[SEAM:, :LANES]]
    max x3 -> x0, other arithmetic: 53.5 us -> none  [neighbour_max(): return jnp.maximum(grid, jnp.maximum(lower, upper))]
    unnamed x9 -> x0, other arithmetic: 37.9 us -> none
    add x4 -> x0, other arithmetic: 29.3 us -> none  [the longest x1 14.4 us: along_rows(): result = result + taps_row[j] * padded[:, j:j + width]]
    pallas_call x0 -> x4, Pallas kernels: none -> 27.7 us  [the longest x1 12.2 us: merge(): pl.pallas_call(functools.partial(merge_kernel, rows), grid=(planes // VGR...]
    ppermute x2 -> x0, local copies, waits for them, and re-layouts: 21.4 us -> none  [the longest x1 11.5 us: with_halo(): after = lax.ppermute(first, axis, down)]
    unnamed x29 -> x0, local copies, waits for them, and re-layouts: 18.3 us -> none
    dot_general x1 -> x0, matrix products: 17.6 us -> none  [move_planes(): jnp.einsum('vsr,vrnc->vsnc', select_row, moved, preferred_element_type=jn...]
  transfers between devices with their start and end apart: 7 -> 5, of which waited for: 0 -> 4; matrix products, arithmetic and copies ran while one was open for 36% -> 2% of each run, Pallas kernels for 0% -> 16%
where the time goes in v1:
time: 67.8 us; the launch traced here: 67.2 us
  Pallas kernels  27.7 us (41%)
  starting transfers between devices  20.7 us (31%)
  waiting for transfers between devices  13.1 us (19%)
  local copies, waits for them, and re-layouts  2.77 us (4%)
  other arithmetic  1.42 us (2%)
  between operations  1.29 us (2%)
    pallas_call x1, Pallas kernels, merge(): pl.pallas_call(functools.partial(merge_kernel, rows), grid=(planes // VGR...  12.2 us
    pallas_call x1, Pallas kernels, pool(): pl.pallas_call(functools.partial(pool_kernel, rows), grid=(height // chun...  10.6 us
    ppermute x2, starting transfers between devices, pass_on(): return lax.ppermute(value, axis, [(i, i + 1) for i in range(count - 1)])  8.26 us
    ppermute x2, waiting for transfers between devices, pass_back(): return lax.ppermute(value, axis, [(i + 1, i) for i in range(count - 1)])  7.33 us
    ppermute x2, starting transfers between devices, pass_back(): return lax.ppermute(value, axis, [(i + 1, i) for i in range(count - 1)])  6.22 us
    all_to_all x1, starting transfers between devices, step_with(): lax.all_to_all(pieces, 'cols', split_axis=0, concat_axis=0, tiled=True)  6.21 us
    ppermute x2, waiting for transfers between devices, pass_on(): return lax.ppermute(value, axis, [(i, i + 1) for i in range(count - 1)])  5.78 us
    pallas_call x1, Pallas kernels, filter_rows(): pl.pallas_call(filter_rows_kernel, out_shape=jax.ShapeDtypeStruct((pieces...  3.36 us
  transfers between devices with their start and end apart: 5, of which 4 were waited for; matrix products, arithmetic and copies ran while one was open for 2% of the time, Pallas kernels for 16%

profile of v1, /device:TPU:7, one launch (start us, length us, event | category | flops | bytes accessed | tf_op | source)
XLA Modules:
  0.0 67.2 jit_solution(13893064492858358515)
XLA Ops:
  0.0 1.4 %maximum_reduce_fusion = (s32[]{:T(128)}, s32[]{:T(128)}) fusion(s32[64,2]{0,1:T(2,128)} %param.11), kind=kLoop, calls=%fused_computation.4 | loop fusion | flops 318 | bytes 264 | tf_op jit(solution)/shard_map/reduce_sum | solution.py:325
  2.7 64.5 %conditional.1 = (bf16[64,64,1024]{2,1,0:T(8,128)(2,1)}) conditional(s32[]{:T(128)} %convert_element_type.3, (s32[64,2]{0,1:T(2,128)}, bf16[64,64,1024]{2,1,0:T(8,128)(2,1)}, f32[15]{0:T(128)}, f32[8,8192]{1,0:T(8,128)}, f32[15]{0:T(128)}) %tuple.11, (s32[64,2]{0,1:T(2,128)}, bf16[64,64,1024]{2,1,0:T(8,128)(2,1)}, f32[15]{0:T(128)}, ...), branch_computations={%region_2.0_spmd, %region_3.0_spmd} | conditional | flops 18743296 | bytes 44041880 | solution.py:326
  2.7 3.4 %filter_rows.3 = f32[8,8,1024]{2,1,0:T(8,128)} custom-call(f32[15]{0:T(128)} %get-tuple-element.64.taps_ref, f32[8,8192]{1,0:T(8,128)} %get-tuple-element.66.strip_ref), custom_call_target="tpu_custom_call" | custom-call | tf_op jit(solution)/shard_map/cond/branch_1_fun/filter_rows/pallas_call | solution.py:49
  6.1 6.2 %all-to-all-start.1 = ((f32[8,8,1024]{2,1,0:T(8,128)}), f32[8,8,1024]{2,1,0:T(8,128)S(1)}, u32[]{:S(2)}, u32[]{:S(2)}) async-start(f32[8,8,1024]{2,1,0:T(8,128)} %filter_rows.3), calls=%async_computation.1 | async-start | bytes 524288 | tf_op jit(solution)/shard_map/cond/branch_1_fun/all_to_all | solution.py:311
  12.3 1.4 %copy.21.offsets_ref = s32[64,2]{1,0:T(8,128)} copy(s32[64,2]{0,1:T(2,128)} %get-tuple-element.74) | data formatting | bytes 1024 | tf_op jit(solution)/shard_map
  13.6 10.6 %pool.3 = (bf16[64,64,1024]{2,1,0:T(8,128)(2,1)}, bf16[4,64,128]{2,1,0:T(8,128)(2,1)}, bf16[4,64,128]{2,1,0:T(8,128)(2,1)}, bf16[208,1024]{1,0:T(8,128)(2,1)}, bf16[208,1024]{1,0:T(8,128)(2,1)}) custom-call(s32[64,2]{1,0:T(8,128)} %copy.21.offsets_ref, bf16[64,64,1024]{2,1,0:T(8,128)(2,1)} %get-tuple-element.62.merit_ref), custom_call_target="tpu_custom_call" | custom-call | flops 16777216 | bytes 16777216 | tf_op jit(solution)/shard_map/cond/branch_1_fun/pool/pallas_call | solution.py:146
  24.2 0.0 copy-start.13
  24.2 0.0 copy-start.11
  24.2 0.0 all-to-all-done.1
  24.2 0.0 copy-start.1
  24.2 0.7 %copy-done.1 = f32[8,8,1024]{2,1,0:T(8,128)} copy-done((f32[8,8,1024]{2,1,0:T(8,128)}, f32[8,8,1024]{2,1,0:T(8,128)S(1)}, u32[]{:S(2)}) %copy-start.1) | copy-done | bytes 262168 | tf_op jit(solution)/shard_map/cond
  24.9 0.0 copy-start.15
  24.9 1.6 %add_seam.3 = (bf16[208,1024]{1,0:T(8,128)(2,1)}, bf16[208,1024]{1,0:T(8,128)(2,1)}) custom-call(f32[64,1024]{1,0:T(8,128)} %bitcast.8, bf16[208,1024]{1,0:T(8,128)(2,1)} %get-tuple-element.46.down_in, bf16[208,1024]{1,0:T(8,128)(2,1)} %get-tuple-element.47.up_in), custom_call_target="tpu_custom_call", output_to_operand_aliasing={{0}: (1, {}), {1}: (2, {})} | custom-call | tf_op jit(solution)/shard_map/cond/branch_1_fun/add_seam/pallas_call | solution.py:183
  26.5 5.2 %collective-permute-start.4 = (bf16[208,1024]{1,0:T(8,128)(2,1)}, bf16[208,1024]{1,0:T(8,128)(2,1)S(1)}, u32[]{:S(2)}, u32[]{:S(2)}) collective-permute-start(bf16[208,1024]{1,0:T(8,128)(2,1)} %get-tuple-element.48), channel_id=1, source_target_pairs={{0,8},{8,16},{16,24},{24,32},{32,40},{40,48},{48,56},{56,64},{64,7... | collective-permute-start | bytes 1277960 | tf_op jit(solution)/shard_map/cond/branch_1_fun/ppermute | solution.py:300
  31.7 1.9 %collective-permute-start.5 = (bf16[208,1024]{1,0:T(8,128)(2,1)}, bf16[208,1024]{1,0:T(8,128)(2,1)S(1)}, u32[]{:S(2)}, u32[]{:S(2)}) collective-permute-start(bf16[208,1024]{1,0:T(8,128)(2,1)} %get-tuple-element.49), channel_id=1, source_target_pairs={{8,0},{16,8},{24,16},{32,24},{40,32},{48,40},{56,48},{64,56},{72,6... | collective-permute-start | bytes 1277960 | tf_op jit(solution)/shard_map/cond/branch_1_fun/ppermute | solution.py:305
  33.6 4.6 %collective-permute-done.4.above_ref = bf16[208,1024]{1,0:T(8,128)(2,1)S(1)} collective-permute-done((bf16[208,1024]{1,0:T(8,128)(2,1)}, bf16[208,1024]{1,0:T(8,128)(2,1)S(1)}, u32[]{:S(2)}, u32[]{:S(2)}) %collective-permute-start.4) | collective-permute-done | bytes 426016 | tf_op jit(solution)/shard_map/cond/branch_1_fun/ppermute | solution.py:300
  38.3 0.0 copy-start.4
  38.3 5.5 %collective-permute-done.5.below_ref = bf16[208,1024]{1,0:T(8,128)(2,1)S(1)} collective-permute-done((bf16[208,1024]{1,0:T(8,128)(2,1)}, bf16[208,1024]{1,0:T(8,128)(2,1)S(1)}, u32[]{:S(2)}, u32[]{:S(2)}) %collective-permute-start.5) | collective-permute-done | bytes 426016 | tf_op jit(solution)/shard_map/cond/branch_1_fun/ppermute | solution.py:305
  43.8 0.0 copy-start.5
  43.8 0.0 copy-done.13
  43.9 3.1 %collective-permute-start.6 = (bf16[640,128]{1,0:T(8,128)(2,1)S(1)}, bf16[640,128]{1,0:T(8,128)(2,1)S(1)}, u32[]{:S(2)}, u32[]{:S(2)}) collective-permute-start(bf16[640,128]{1,0:T(8,128)(2,1)S(1)} %pad_maximum_fusion.2), channel_id=1, source_target_pairs={{0,1},{1,2},{2,3},{3,4},{4,5},{5,6},{6,7},{8,9},{9,10},{10,11},{11... | collective-permute-start | bytes 491528 | tf_op jit(solution)/shard_map/cond/branch_1_fun/ppermute | solution.py:300
  47.0 0.0 copy-done.11
  47.0 4.3 %collective-permute-start.7 = (bf16[640,128]{1,0:T(8,128)(2,1)S(1)}, bf16[640,128]{1,0:T(8,128)(2,1)S(1)}, u32[]{:S(2)}, u32[]{:S(2)}) collective-permute-start(bf16[640,128]{1,0:T(8,128)(2,1)S(1)} %pad_maximum_fusion.3), channel_id=1, source_target_pairs={{1,0},{2,1},{3,2},{4,3},{5,4},{6,5},{7,6},{9,8},{10,9},{11,10},{12... | collective-permute-start | bytes 491528 | tf_op jit(solution)/shard_map/cond/branch_1_fun/ppermute | solution.py:305
  51.3 1.2 %collective-permute-done.6.west_ref = bf16[640,128]{1,0:T(8,128)(2,1)S(1)} collective-permute-done((bf16[640,128]{1,0:T(8,128)(2,1)S(1)}, bf16[640,128]{1,0:T(8,128)(2,1)S(1)}, u32[]{:S(2)}, u32[]{:S(2)}) %collective-permute-start.6) | collective-permute-done | bytes 163872 | tf_op jit(solution)/shard_map/cond/branch_1_fun/ppermute | solution.py:300
  52.5 0.0 copy-start.8
  52.5 1.8 %collective-permute-done.7.east_ref = bf16[640,128]{1,0:T(8,128)(2,1)S(1)} collective-permute-done((bf16[640,128]{1,0:T(8,128)(2,1)S(1)}, bf16[640,128]{1,0:T(8,128)(2,1)S(1)}, u32[]{:S(2)}, u32[]{:S(2)}) %collective-permute-start.7) | collective-permute-done | bytes 163872 | tf_op jit(solution)/shard_map/cond/branch_1_fun/ppermute | solution.py:305
  54.3 0.0 copy-start.9
  54.3 0.0 copy-done.4
  54.3 0.0 copy-done.5
  54.3 0.0 copy-done.8
  54.3 0.7 copy-done.9
  54.9 0.0 copy-done.15
  54.9 12.2 %merge.3 = bf16[64,64,1024]{2,1,0:T(8,128)(2,1)} custom-call(s32[64,2]{1,0:T(8,128)} %copy.21.offsets_ref, f32[15]{0:T(128)S(1)} %copy-done.15, bf16[64,64,1024]{2,1,0:T(8,128)(2,1)} %get-tuple-element.43.pooled_ref, f32[64,1024]{1,0:T(8,128)} %bitcast.9, bf16[208,1024]{1,0:T(8,128)(2,1)} %copy-done.4, bf16[208,1024]{1,0:T(8,128)(2,1)} %copy-done.5, ...), custom_call_target="tpu_custom_call" | custom-call | tf_op jit(solution)/shard_map/cond/branch_1_fun/merge/pallas_call | solution.py:279
  (4 shorter events, 0.1 us)
Async XLA Ops:
  6.1 18.2 %all-to-all-start.1 = ((f32[8,8,1024]{2,1,0:T(8,128)}), f32[8,8,1024]{2,1,0:T(8,128)S(1)}, u32[]{:S(2)}, u32[]{:S(2)}) async-start(f32[8,8,1024]{2,1,0:T(8,128)} %filter_rows.3), calls=%async_computation.1 | async-start | bytes 524288 | tf_op jit(solution)/shard_map/cond/branch_1_fun/all_to_all | solution.py:311
  24.2 19.6 %copy-start.13 = (bf16[4,64,128]{2,1,0:T(8,128)(2,1)S(1)}, bf16[4,64,128]{2,1,0:T(8,128)(2,1)}, u32[]{:S(2)}) copy-start(bf16[4,64,128]{2,1,0:T(8,128)(2,1)} %get-tuple-element.50) | copy-start | bytes 196612 | tf_op jit(solution)/shard_map/cond
  24.2 22.8 %copy-start.11 = (bf16[4,64,128]{2,1,0:T(8,128)(2,1)S(1)}, bf16[4,64,128]{2,1,0:T(8,128)(2,1)}, u32[]{:S(2)}) copy-start(bf16[4,64,128]{2,1,0:T(8,128)(2,1)} %get-tuple-element.51) | copy-start | bytes 196612 | tf_op jit(solution)/shard_map/cond
  24.2 0.7 %copy-start.1 = (f32[8,8,1024]{2,1,0:T(8,128)}, f32[8,8,1024]{2,1,0:T(8,128)S(1)}, u32[]{:S(2)}) copy-start(f32[8,8,1024]{2,1,0:T(8,128)S(1)} %all-to-all-done.1) | copy-start | bytes 786436 | tf_op jit(solution)/shard_map/cond
  24.9 30.0 %copy-start.15 = (f32[15]{0:T(128)S(1)}, f32[15]{0:T(128)}, u32[]{:S(2)}) copy-start(f32[15]{0:T(128)} %get-tuple-element.68.taps_ref) | copy-start | bytes 184 | tf_op jit(solution)/shard_map/cond
  26.5 11.7 %collective-permute-start.4 = (bf16[208,1024]{1,0:T(8,128)(2,1)}, bf16[208,1024]{1,0:T(8,128)(2,1)S(1)}, u32[]{:S(2)}, u32[]{:S(2)}) collective-permute-start(bf16[208,1024]{1,0:T(8,128)(2,1)} %get-tuple-element.48), channel_id=1, source_target_pairs={{0,8},{8,16},{16,24},{24,32},{32,40},{40,48},{48,56},{56,64},{64,7... | collective-permute-start | bytes 1277960 | tf_op jit(solution)/shard_map/cond/branch_1_fun/ppermute | solution.py:300
  31.7 12.1 %collective-permute-start.5 = (bf16[208,1024]{1,0:T(8,128)(2,1)}, bf16[208,1024]{1,0:T(8,128)(2,1)S(1)}, u32[]{:S(2)}, u32[]{:S(2)}) collective-permute-start(bf16[208,1024]{1,0:T(8,128)(2,1)} %get-tuple-element.49), channel_id=1, source_target_pairs={{8,0},{16,8},{24,16},{32,24},{40,32},{48,40},{56,48},{64,56},{72,6... | collective-permute-start | bytes 1277960 | tf_op jit(solution)/shard_map/cond/branch_1_fun/ppermute | solution.py:305
  38.3 16.0 %copy-start.4 = (bf16[208,1024]{1,0:T(8,128)(2,1)}, bf16[208,1024]{1,0:T(8,128)(2,1)S(1)}, u32[]{:S(2)}) copy-start(bf16[208,1024]{1,0:T(8,128)(2,1)S(1)} %collective-permute-done.4.above_ref) | copy-start | bytes 1277956 | tf_op jit(solution)/shard_map/cond
  43.8 10.4 %copy-start.5 = (bf16[208,1024]{1,0:T(8,128)(2,1)}, bf16[208,1024]{1,0:T(8,128)(2,1)S(1)}, u32[]{:S(2)}) copy-start(bf16[208,1024]{1,0:T(8,128)(2,1)S(1)} %collective-permute-done.5.below_ref) | copy-start | bytes 1277956 | tf_op jit(solution)/shard_map/cond
  43.9 8.6 %collective-permute-start.6 = (bf16[640,128]{1,0:T(8,128)(2,1)S(1)}, bf16[640,128]{1,0:T(8,128)(2,1)S(1)}, u32[]{:S(2)}, u32[]{:S(2)}) collective-permute-start(bf16[640,128]{1,0:T(8,128)(2,1)S(1)} %pad_maximum_fusion.2), channel_id=1, source_target_pairs={{0,1},{1,2},{2,3},{3,4},{4,5},{5,6},{6,7},{8,9},{9,10},{10,11},{11... | collective-permute-start | bytes 491528 | tf_op jit(solution)/shard_map/cond/branch_1_fun/ppermute | solution.py:300
  47.0 7.3 %collective-permute-start.7 = (bf16[640,128]{1,0:T(8,128)(2,1)S(1)}, bf16[640,128]{1,0:T(8,128)(2,1)S(1)}, u32[]{:S(2)}, u32[]{:S(2)}) collective-permute-start(bf16[640,128]{1,0:T(8,128)(2,1)S(1)} %pad_maximum_fusion.3), channel_id=1, source_target_pairs={{1,0},{2,1},{3,2},{4,3},{5,4},{6,5},{7,6},{9,8},{10,9},{11,10},{12... | collective-permute-start | bytes 491528 | tf_op jit(solution)/shard_map/cond/branch_1_fun/ppermute | solution.py:305
  52.5 1.8 %copy-start.8 = (bf16[640,128]{1,0:T(8,128)(2,1)}, bf16[640,128]{1,0:T(8,128)(2,1)S(1)}, u32[]{:S(2)}) copy-start(bf16[640,128]{1,0:T(8,128)(2,1)S(1)} %collective-permute-done.6.west_ref) | copy-start | bytes 491524 | tf_op jit(solution)/shard_map/cond
  54.3 0.7 copy-start.9

commit v2 on v0

v2 whole, which is shorter than its diff:
```python
import functools

import jax
import jax.numpy as jnp
from jax import lax
from jax.experimental import pallas as pl
from jax.experimental.pallas import tpu as pltpu
from jax.sharding import PartitionSpec as P

VGRID = 8
MAXV = 8
VELS = VGRID * VGRID
LANES = 128
FORGET = 0.875
SOME_ROWS = 192
ALL_ROWS = VELS * MAXV
SLAB = 8
CHUNK = 16
LIMIT = 58 * 2**20

f32 = jnp.float32
bf16 = jnp.bfloat16


def params(limit=LIMIT):
    return pltpu.CompilerParams(vmem_limit_bytes=limit)


def smem():
    return pl.BlockSpec(memory_space=pltpu.SMEM)


def filter_rows_kernel(taps_ref, strip_ref, after_ref, out_ref, pad_ref):
    del after_ref
    half = taps_ref.shape[0] // 2
    height, width = strip_ref.shape
    pad_ref[:, :LANES] = jnp.zeros((height, LANES), f32)
    pad_ref[:, LANES + width :] = jnp.zeros((height, LANES), f32)
    pad_ref[:, LANES : LANES + width] = strip_ref[...]
    count, _, span = out_ref.shape
    for piece in range(count):
        start = LANES + piece * span
        total = jnp.zeros((height, span), f32)
        for j in range(taps_ref.shape[0]):
            total = total + taps_ref[j] * pad_ref[:, start + j - half : start + j - half + span]
        out_ref[piece] = total


def filter_rows(strip, taps_row, pieces, after):
    height, width = strip.shape
    return pl.pallas_call(
        filter_rows_kernel,
        out_shape=jax.ShapeDtypeStruct((pieces, height, width // pieces), f32),
        in_specs=[smem(), pl.BlockSpec(memory_space=pltpu.VMEM), pl.BlockSpec(memory_space=pl.ANY)],
        out_specs=pl.BlockSpec(memory_space=pltpu.VMEM),
        scratch_shapes=[pltpu.VMEM((height, width + 2 * LANES), f32)],
        compiler_params=params(),
        name="filter_rows",
    )(taps_row, strip, after)


def max_of_three(values):
    total = len(values)
    pairs = [jnp.maximum(values[i], values[i + 1]) for i in range(total - 1)]
    middle = [jnp.maximum(pairs[i - 1], values[i + 1]) for i in range(1, total - 1)]
    return [pairs[0]] + middle + [pairs[-1]]


def pool_chunk(merit_ref, pooled_ref, rows, cols):
    def line(a):
        return max_of_three([merit_ref[a * VGRID + b, rows, cols] for b in range(VGRID)])

    def emit(a, planes):
        for b in range(VGRID):
            pooled_ref[a * VGRID + b, rows, cols] = planes[b]

    last, here = line(0), line(1)
    pair = [jnp.maximum(x, y) for x, y in zip(last, here)]
    emit(0, pair)
    for a in range(2, VGRID):
        after = line(a)
        emit(a - 1, [jnp.maximum(x, y) for x, y in zip(pair, after)])
        pair = [jnp.maximum(x, y) for x, y in zip(here, after)]
        here = after
    emit(VGRID - 1, pair)


def pack_side(pooled_ref, cols, turn, target_ref):
    height = pooled_ref.shape[1]
    lane_group = lax.broadcasted_iota(jnp.int32, (height, LANES), 1) // MAXV
    share = LANES // MAXV
    for g in range(VELS // share):
        total = jnp.zeros((height, LANES), f32)
        for w in range(share):
            edge = pooled_ref[g * share + w, :, cols].astype(f32)
            total = jnp.where(lane_group == w, pltpu.roll(edge, (w + turn) * MAXV % LANES, 1), total)
        target_ref[g] = total.astype(bf16)


def pool_as_they_come(copies, sizes, held_ref, pooled_ref, then=None):
    for copy in copies:
        copy.start()
    for copy, (height, top, width, left) in zip(copies, sizes):
        copy.wait()
        across = width // LANES

        def one(i, carry):
            rows = pl.ds(pl.multiple_of(top + i // across * CHUNK, CHUNK), CHUNK)
            cols = pl.ds(pl.multiple_of(left + i % across * LANES, LANES), LANES)
            pool_chunk(held_ref, pooled_ref, rows, cols)
            return carry

        lax.fori_loop(0, height // CHUNK * across, one, 0)
        if then is not None:
            then(top, left)


def pool_all_kernel(merit_ref, *refs):
    pooled_ref, held_ref, sems = refs[-3:]
    _, height, width = merit_ref.shape
    part = width // 2
    sizes = [(CHUNK, top, part, left) for top in range(0, height, CHUNK) for left in (0, part)]
    copies = []
    for n, (_, top, _, left) in enumerate(sizes):
        at = (slice(None), pl.ds(top, CHUNK), pl.ds(left, part))
        copies.append(pltpu.make_async_copy(merit_ref.at[at], held_ref.at[at], sems.at[n]))
    pool_as_they_come(copies, sizes, held_ref, pooled_ref)


def pool_sides_kernel(merit_ref, after_ref, right_ref, left_ref, held_ref, pooled_ref, sems):
    del after_ref
    _, height, width = merit_ref.shape
    sizes = [(height, 0, LANES, left) for left in (0, LANES)]
    copies = []
    for n, first in enumerate((0, width - LANES)):
        source = merit_ref.at[:, :, pl.ds(first, LANES)]
        copies.append(pltpu.make_async_copy(source, held_ref.at[:, :, pl.ds(n * LANES, LANES)], sems.at[n]))
    pool_as_they_come(copies, sizes, held_ref, pooled_ref)
    pack_side(pooled_ref, slice(0, LANES), 0, left_ref)
    pack_side(pooled_ref, slice(LANES, 2 * LANES), 1, right_ref)


def pool_outer_kernel(
    offsets_ref, merit_ref, near_a_ref, near_b_ref, far_a_ref, far_b_ref,
    held_ref, pooled_ref, packed_ref, stage_ref, sems, far_sems,
):
    _, height, width = merit_ref.shape
    blocks = width // LANES
    odd = lax.axis_index("rows") % 2

    def count(v, sign):
        return jnp.maximum(sign * offsets_ref[0, v], 0)

    up, down = 0, 0
    for v in range(VELS):
        up = up + count(v, 1)
        down = down + count(v, -1)

    part = width // 2
    sizes = [(CHUNK, top, part, left) for top in (0, CHUNK) for left in (0, part)]
    copies = []
    for n, (_, top, _, left) in enumerate(sizes):
        rows, cols = pl.ds(top and height - CHUNK, CHUNK), pl.ds(left, part)
        target = held_ref.at[:, pl.ds(top, CHUNK), cols]
        copies.append(pltpu.make_async_copy(merit_ref.at[:, rows, cols], target, sems.at[n]))

    def pack(top, left):
        edge = top // CHUNK
        mine = range(left // LANES, (left + part) // LANES)

        def tile(v, k):
            return pooled_ref[v, edge * CHUNK : (edge + 1) * CHUNK, k * LANES : (k + 1) * LANES].astype(f32)

        if edge == 0:
            at = 0
            for v in range(VELS):
                for k in mine:
                    packed_ref[0, k, pl.ds(at + MAXV, MAXV), :] = tile(v, k)[:MAXV]
                at = at + count(v, -1)
        else:
            at = up
            for v in range(VELS - 1, -1, -1):
                for k in mine:
                    packed_ref[1, k, pl.ds(at, MAXV), :] = tile(v, k)[CHUNK - MAXV :]
                at = at - count(v, 1)

    pool_as_they_come(copies, sizes, held_ref, pooled_ref, pack)

    for slot, ref in enumerate((near_a_ref, near_b_ref)):
        mine = odd if slot == 1 else 1 - odd
        for k in range(blocks):
            piece = packed_ref[mine, k, MAXV : MAXV + SOME_ROWS, :]
            ref[:, k * LANES : (k + 1) * LANES] = piece.astype(bf16)

    @pl.when(jnp.maximum(up, down) > SOME_ROWS)
    def _():
        for slot, ref in enumerate((far_a_ref, far_b_ref)):
            mine = odd if slot == 1 else 1 - odd
            for k in range(blocks):
                piece = packed_ref[mine, k, MAXV + SOME_ROWS : MAXV + ALL_ROWS, :]
                stage_ref[:, k * LANES : (k + 1) * LANES] = piece.astype(bf16)
            copy = pltpu.make_async_copy(stage_ref, ref, far_sems.at[slot])
            copy.start()
            copy.wait()


def pool_cost(merit):
    return pl.CostEstimate(flops=2 * merit.size, bytes_accessed=merit.size, transcendentals=0)


def pool_all(merit, after):
    anywhere = pl.BlockSpec(memory_space=pl.ANY)
    return pl.pallas_call(
        pool_all_kernel,
        out_shape=pltpu.VMEM(merit.shape, bf16),
        in_specs=[anywhere] * (1 + len(after)),
        out_specs=pl.BlockSpec(memory_space=pltpu.VMEM),
        scratch_shapes=[pltpu.VMEM(merit.shape, bf16), pltpu.SemaphoreType.DMA((2 * merit.shape[1] // CHUNK,))],
        cost_estimate=pool_cost(merit),
        compiler_params=params(48 * 2**20),
        name="pool_all",
    )(merit, *after)


def pool_sides(merit, after):
    planes, height, _ = merit.shape
    side = (planes * MAXV // LANES, height, LANES)
    anywhere = pl.BlockSpec(memory_space=pl.ANY)
    return pl.pallas_call(
        pool_sides_kernel,
        out_shape=[jax.ShapeDtypeStruct(side, bf16)] * 2,
        in_specs=[anywhere, anywhere],
        out_specs=[pl.BlockSpec(memory_space=pltpu.VMEM)] * 2,
        scratch_shapes=[pltpu.VMEM((planes, height, 2 * LANES), bf16)] * 2 + [pltpu.SemaphoreType.DMA((2,))],
        cost_estimate=pool_cost(merit),
        compiler_params=params(),
        name="pool_sides",
    )(merit, after)


def pool_outer(merit, offsets):
    planes, height, width = merit.shape
    part = (planes, 2 * CHUNK, width)
    near, far = (SOME_ROWS, width), (ALL_ROWS - SOME_ROWS, width)
    return pl.pallas_call(
        pool_outer_kernel,
        out_shape=[jax.ShapeDtypeStruct(near, bf16)] * 2 + [jax.ShapeDtypeStruct(far, bf16)] * 2,
        in_specs=[smem(), pl.BlockSpec(memory_space=pl.ANY)],
        out_specs=[pl.BlockSpec(memory_space=pltpu.VMEM)] * 2 + [pl.BlockSpec(memory_space=pl.ANY)] * 2,
        scratch_shapes=[
            pltpu.VMEM(part, bf16),
            pltpu.VMEM(part, bf16),
            pltpu.VMEM((2, width // LANES, ALL_ROWS + 2 * MAXV, LANES), f32),
            pltpu.VMEM(far, bf16),
            pltpu.SemaphoreType.DMA((4,)),
            pltpu.SemaphoreType.DMA((2,)),
        ],
        cost_estimate=pool_cost(merit),
        compiler_params=params(),
        name="pool_outer",
    )(offsets, merit)


def weighted_rows(taps_ref, column_ref, k, count):
    half = taps_ref.shape[0] // 2
    total = jnp.zeros((count, LANES), f32)
    for i in range(taps_ref.shape[0]):
        start = MAXV - half + i
        total = total + taps_ref[i] * column_ref[k, start : start + count, :]
    return total


def merge_kernel(
    offsets_ref, taps_ref, pooled_ref, tile_ref, seam_a_ref, seam_b_ref, near_a_ref, near_b_ref,
    west_ref, east_ref, far_a_ref, far_b_ref, far_west_ref, far_east_ref, out_ref,
    halo_ref, side_ref, column_ref, filtered_ref, moved_ref, at_ref, stage_ref, stage_side_ref, sem,
):
    step = pl.program_id(0)
    planes, height, width = out_ref.shape
    blocks = width // LANES
    groups = VELS * MAXV // LANES
    share = LANES // MAXV
    odd = lax.axis_index("rows") % 2
    cuts = [slice(k * LANES, (k + 1) * LANES) for k in range(blocks)]

    @pl.when(step == 0)
    def _():
        up, down = 0, 0
        for v in range(VELS):
            up = up + jnp.maximum(offsets_ref[0, v], 0)
            down = down + jnp.maximum(-offsets_ref[0, v], 0)
        at_ref[0] = 0
        at_ref[1] = 0
        near = slice(MAXV, MAXV + SOME_ROWS)
        start = groups * height
        for e, ref in enumerate((near_a_ref, near_b_ref)):
            for k in range(blocks):
                halo_ref[e, k + 1, near, :] = ref[:, cuts[k]].astype(f32)
            part = slice(start + e * SOME_ROWS, start + (e + 1) * SOME_ROWS)
            halo_ref[e, 0, near, :] = west_ref[part, :].astype(f32)
            halo_ref[e, blocks + 1, near, :] = east_ref[part, :].astype(f32)
        for e, ref in enumerate((west_ref, east_ref)):
            for g in range(groups):
                side_ref[e, g] = ref[g * height : (g + 1) * height, :].astype(f32)
        for k in range(blocks):
            a, b = seam_a_ref[:, cuts[k]], seam_b_ref[:, cuts[k]]
            column_ref[k, :MAXV, :] = jnp.where(odd == 1, a, b)
            column_ref[k, MAXV : MAXV + height, :] = tile_ref[:, cuts[k]]
            column_ref[k, MAXV + height :, :] = jnp.where(odd == 1, b, a)
        for k in range(blocks):
            filtered_ref[k] = weighted_rows(taps_ref, column_ref, k, height)

        @pl.when(jnp.maximum(up, down) > SOME_ROWS)
        def _():
            def bring(source, target):
                copy = pltpu.make_async_copy(source, target, sem)
                copy.start()
                copy.wait()

            far = slice(MAXV + SOME_ROWS, MAXV + ALL_ROWS)
            count = ALL_ROWS - SOME_ROWS
            for e, ref in enumerate((far_a_ref, far_b_ref)):
                bring(ref, stage_ref)
                for k in range(blocks):
                    halo_ref[e, k + 1, far, :] = stage_ref[:, cuts[k]].astype(f32)
            for k, ref in ((0, far_west_ref), (blocks + 1, far_east_ref)):
                bring(ref, stage_side_ref)
                for e in range(2):
                    halo_ref[e, k, far, :] = stage_side_ref[e * count : (e + 1) * count, :].astype(f32)

    def store(p, rows, turn, pieces):
        lane = lax.broadcasted_iota(jnp.int32, pieces[1].shape, 1)
        before = pieces[0]
        for k in range(1, blocks + 2):
            here = pltpu.roll(pieces[k], turn, 1) if k <= blocks else pieces[k]
            moved_ref[p, k - 1, rows, :] = jnp.where(lane < turn, before, here)
            before = here

    moves = []
    up, down = at_ref[0], at_ref[1]
    for p in range(planes):
        v = step * planes + p
        dy, dx = offsets_ref[0, v], offsets_ref[1, v]
        turn = dx & (LANES - 1)
        q = jnp.where(dx >= 0, 0, 1)
        moves.append((dy, q))
        g, w = v // share, v % share
        shift = (dx - (w + 1 - q) * MAXV) & (LANES - 1)
        beyond = pltpu.roll(side_ref[q, g], shift, 1)
        here = [pooled_ref[v, :, cut].astype(f32) for cut in cuts]
        store(p, slice(MAXV, MAXV + height), turn, [beyond] + here + [beyond])
        below = jnp.where(dy >= 0, 0, 1)
        source = pl.ds(jnp.where(dy >= 0, up + dy, down + MAXV), MAXV)
        halo = [halo_ref[below ^ (1 - odd), k, source, :] for k in range(blocks + 2)]
        halo[0] = pltpu.roll(halo[0], turn, 1)
        halo[-1] = pltpu.roll(halo[-1], turn, 1)
        store(p, pl.ds(pl.multiple_of(below * (MAXV + height), MAXV), MAXV), turn, halo)
        up = up + jnp.maximum(dy, 0)
        down = down + jnp.maximum(-dy, 0)
    at_ref[0] = up
    at_ref[1] = down

    for p in range(planes):
        dy, q = moves[p]
        for k in range(blocks):
            shifted = moved_ref[p, k + q, pl.ds(MAXV - dy, height), :]
            out_ref[p, :, cuts[k]] = (filtered_ref[k] + FORGET * shifted).astype(bf16)


def merge(pooled, tile, seams, nears, sides, fars, offsets, taps_col):
    planes, height, width = pooled.shape
    blocks = width // LANES
    groups = planes * MAXV // LANES
    vmem, anywhere = pl.BlockSpec(memory_space=pltpu.VMEM), pl.BlockSpec(memory_space=pl.ANY)
    return pl.pallas_call(
        merge_kernel,
        grid=(planes // SLAB,),
        out_shape=jax.ShapeDtypeStruct((planes, height, width), bf16),
        in_specs=[smem(), smem()] + [vmem] * 8 + [anywhere] * 4,
        out_specs=pl.BlockSpec((SLAB, height, width), lambda i: (i, 0, 0)),
        scratch_shapes=[
            pltpu.VMEM((2, blocks + 2, ALL_ROWS + 2 * MAXV, LANES), f32),
            pltpu.VMEM((2, groups, height, LANES), f32),
            pltpu.VMEM((blocks, height + 2 * MAXV, LANES), f32),
            pltpu.VMEM((blocks, height, LANES), f32),
            pltpu.VMEM((SLAB, blocks + 1, height + 2 * MAXV, LANES), f32),
            pltpu.SMEM((2,), jnp.int32),
            pltpu.VMEM(fars[0].shape, bf16),
            pltpu.VMEM(fars[2].shape, bf16),
            pltpu.SemaphoreType.DMA,
        ],
        compiler_params=params(40 * 2**20),
        name="merge",
    )(offsets, taps_col, pooled, tile, *seams, *nears, *sides, *fars)


def pass_on(value, axis):
    count = lax.axis_size(axis)
    return lax.ppermute(value, axis, [(i, i + 1) for i in range(count - 1)])


def pass_back(value, axis):
    count = lax.axis_size(axis)
    return lax.ppermute(value, axis, [(i + 1, i) for i in range(count - 1)])


def trade(value, axis, first):
    pairs = []
    for i in range(first, lax.axis_size(axis) - 1, 2):
        pairs += [(i, i + 1), (i + 1, i)]
    return lax.ppermute(value, axis, pairs)


def to_sides(right, left, a, b):
    width = a.shape[1]
    east_end, west_end = slice(width - LANES, width), slice(0, LANES)
    last = jnp.concatenate(right + [a[:, east_end], b[:, east_end]], axis=0)
    first = jnp.concatenate(left + [a[:, west_end], b[:, west_end]], axis=0)
    return pass_on(last, "cols"), pass_back(first, "cols")


def far_exchange(far_a, far_b):
    far_b = trade(far_b, "rows", 1)
    far_a = trade(far_a, "rows", 0)
    return (far_a, far_b) + to_sides([], [], far_a, far_b)


def no_exchange(far_a, far_b):
    empty = jnp.zeros((2 * far_a.shape[0], LANES), bf16)
    return far_a, far_b, empty, empty


def on_device(frame, taps_row, taps_col, merit, offsets):
    _, height, width = merit.shape
    turned = offsets.T
    near_a, near_b, far_a, far_b = pool_outer(merit, turned)
    b = trade(near_b, "rows", 1)
    a = trade(near_a, "rows", 0)
    pieces = filter_rows(frame, taps_row, frame.shape[1] // width, far_a)
    tile = lax.all_to_all(pieces, "cols", split_axis=0, concat_axis=0, tiled=True).reshape(height, width)
    shifts = offsets[:, 0]
    most = jnp.maximum(jnp.sum(jnp.maximum(shifts, 0)), jnp.sum(jnp.maximum(-shifts, 0)))
    fars = lax.cond(most > SOME_ROWS, far_exchange, no_exchange, far_a, far_b)
    right, left = pool_sides(merit, pieces)
    west, east = to_sides([right.reshape(-1, LANES)], [left.reshape(-1, LANES)], a, b)
    top, bottom = tile[:MAXV], tile[height - MAXV :]
    odd = lax.axis_index("rows") % 2 == 1
    for_b, for_a = jnp.where(odd, bottom, top), jnp.where(odd, top, bottom)
    seam_b = trade(for_b, "rows", 1)
    seam_a = trade(for_a, "rows", 0)
    pooled = pool_all(merit, (for_a, for_b, fars[2], fars[3]))
    return merge(pooled, tile, (seam_a, seam_b), (a, b), (west, east), fars, turned, taps_col)


def solution(mesh):
    in_specs = (P(("rows", "cols"), None), P(), P(), P(None, "rows", "cols"), P())
    out_specs = P(None, "rows", "cols")
    return jax.shard_map(on_device, mesh=mesh, in_specs=in_specs, out_specs=out_specs, check_vma=False)
```

time: 358 us -> 54.5 us (0.15); the launches traced: 353 us -> 54 us
  local copies, waits for them, and re-layouts: 170 us -> 2.28 us
  other arithmetic: 137 us -> 2.36 us
  Pallas kernels: 0 us -> 24.5 us
  matrix products: 17.6 us -> 0 us
    slice x14 -> x2, local copies, waits for them, and re-layouts: 115 us -> 0.03 us  [to_sides(): first = jnp.concatenate(left + [a[:, west_end], b[:, west_end]], axis=0)]
    max x3 -> x0, other arithmetic: 53.5 us -> none  [neighbour_max(): return jnp.maximum(grid, jnp.maximum(lower, upper))]
    unnamed x9 -> x0, other arithmetic: 37.9 us -> none
    add x4 -> x0, other arithmetic: 29.3 us -> none  [the longest x1 14.4 us: along_rows(): result = result + taps_row[j] * padded[:, j:j + width]]
    pallas_call x0 -> x5, Pallas kernels: none -> 24.5 us  [the longest x1 8.89 us: merge(): pl.pallas_call(merge_kernel, grid=(planes // SLAB,), out_shape=jax.ShapeD...]
    ppermute x2 -> x0, local copies, waits for them, and re-layouts: 21.4 us -> none  [the longest x1 11.5 us: with_halo(): after = lax.ppermute(first, axis, down)]
    unnamed x29 -> x8, local copies, waits for them, and re-layouts: 18.3 us -> 0.02 us
    dot_general x1 -> x0, matrix products: 17.6 us -> none  [move_planes(): jnp.einsum('vsr,vrnc->vsnc', select_row, moved, preferred_element_type=jn...]
  transfers between devices with their start and end apart: 7 -> 7, of which waited for: 0 -> 0; matrix products, arithmetic and copies ran while one was open for 36% -> 9% of each run, Pallas kernels for 0% -> 19%
where the time goes in v2:
time: 54.5 us; the launch traced here: 54 us
  Pallas kernels  24.5 us (45%)
  starting transfers between devices  23.5 us (43%)
  other arithmetic  2.36 us (4%)
  local copies, waits for them, and re-layouts  2.28 us (4%)
  between operations  1.39 us (3%)
    ppermute x4, starting transfers between devices, trade(): return lax.ppermute(value, axis, pairs)  9.91 us
    pallas_call x1, Pallas kernels, merge(): pl.pallas_call(merge_kernel, grid=(planes // SLAB,), out_shape=jax.ShapeD...  8.89 us
    all_to_all x1, starting transfers between devices, on_device(): lax.all_to_all(pieces, 'cols', split_axis=0, concat_axis=0, tiled=True)  6.21 us
    pallas_call x1, Pallas kernels, pool_outer(): pl.pallas_call(pool_outer_kernel, out_shape=[jax.ShapeDtypeStruct(near, b...  5.08 us
    ppermute x1, starting transfers between devices, pass_back(): return lax.ppermute(value, axis, [(i + 1, i) for i in range(count - 1)])  4.3 us
    pallas_call x1, Pallas kernels, pool_all(): pl.pallas_call(pool_all_kernel, out_shape=pltpu.VMEM(merit.shape, bf16),...  4.08 us
    pallas_call x1, Pallas kernels, filter_rows(): pl.pallas_call(filter_rows_kernel, out_shape=jax.ShapeDtypeStruct((pieces...  3.36 us
    ppermute x1, starting transfers between devices, pass_on(): return lax.ppermute(value, axis, [(i, i + 1) for i in range(count - 1)])  3.09 us
  transfers between devices with their start and end apart: 7, of which 0 were waited for; matrix products, arithmetic and copies ran while one was open for 9% of the time, Pallas kernels for 19%

profile of v2, /device:TPU:7, one launch (start us, length us, event | category | flops | bytes accessed | tf_op | source)
XLA Modules:
  0.0 54.0 jit_solution(6303901823186625563)
XLA Ops:
  0.0 0.0 copy-start
  0.0 5.1 %pool_outer.1 = (bf16[192,1024]{1,0:T(8,128)(2,1)}, bf16[192,1024]{1,0:T(8,128)(2,1)}, bf16[320,1024]{1,0:T(8,128)(2,1)S(1)}, bf16[320,1024]{1,0:T(8,128)(2,1)S(1)}) custom-call(s32[2,64]{1,0:T(2,128)} %bitcast.9, bf16[64,64,1024]{2,1,0:T(8,128)(2,1)} %merit_ref.5), custom_call_target="tpu_custom_call" | custom-call | flops 8388608 | bytes 4194304 | tf_op jit(solution)/shard_map/pool_outer/pallas_call | solution.py:245
  5.1 0.8 %collective-permute-start.6 = (bf16[192,1024]{1,0:T(8,128)(2,1)}, bf16[192,1024]{1,0:T(8,128)(2,1)S(1)}, u32[]{:S(2)}, u32[]{:S(2)}) collective-permute-start(bf16[192,1024]{1,0:T(8,128)(2,1)} %get-tuple-element.31), channel_id=1, source_target_pairs={{0,8},{8,0},{16,24},{24,16},{32,40},{40,32},{48,56},{56,48},{64,72... | collective-permute-start | bytes 1179656 | tf_op jit(solution)/shard_map/ppermute | solution.py:411
  5.8 3.9 %collective-permute-start.7 = (bf16[192,1024]{1,0:T(8,128)(2,1)}, bf16[192,1024]{1,0:T(8,128)(2,1)S(1)}, u32[]{:S(2)}, u32[]{:S(2)}) collective-permute-start(bf16[192,1024]{1,0:T(8,128)(2,1)} %get-tuple-element.32), channel_id=1, source_target_pairs={{8,16},{16,8},{24,32},{32,24},{40,48},{48,40},{56,64},{64,56},{72,... | collective-permute-start | bytes 1179656 | tf_op jit(solution)/shard_map/ppermute | solution.py:411
  9.8 3.4 %filter_rows.1.after_ref = f32[8,8,1024]{2,1,0:T(8,128)} custom-call(f32[15]{0:T(128)} %taps_ref.2, f32[8,8192]{1,0:T(8,128)} %strip_ref.1, bf16[320,1024]{1,0:T(8,128)(2,1)S(1)} %get-tuple-element.27.after_ref), custom_call_target="tpu_custom_call" | custom-call | tf_op jit(solution)/shard_map/filter_rows/pallas_call | solution.py:51
  13.2 6.2 %all-to-all-start = ((f32[8,8,1024]{2,1,0:T(8,128)}), f32[8,8,1024]{2,1,0:T(8,128)S(1)}, u32[]{:S(2)}, u32[]{:S(2)}) async-start(f32[8,8,1024]{2,1,0:T(8,128)} %filter_rows.1.after_ref), calls=%async_computation | async-start | bytes 524288 | tf_op jit(solution)/shard_map/all_to_all | solution.py:440
  19.4 0.0 copy-done
  19.4 0.6 %maximum_reduce_fusion = (s32[]{:T(128)}, s32[]{:T(128)}) fusion(s32[64,2]{0,1:T(2,128)S(1)} %copy-done), kind=kLoop, calls=%fused_computation.6 | loop fusion | flops 318 | bytes 264 | tf_op jit(solution)/shard_map/reduce_sum | solution.py:442
  21.2 2.2 %conditional.1 = (bf16[320,1024]{1,0:T(8,128)(2,1)}, bf16[320,1024]{1,0:T(8,128)(2,1)S(1)}, bf16[640,128]{1,0:T(8,128)(2,1)}, bf16[640,128]{1,0:T(8,128)(2,1)}) conditional(s32[]{:T(128)} %convert_element_type.3, (bf16[320,1024]{1,0:T(8,128)(2,1)S(1)}, bf16[320,1024]{1,0:T(8,128)(2,1)S(1)}) %tuple.13, (bf16[320,1024]{1,0:T(8,128)(2,1)S(1)}, ...), branch_computations={%region_2.0_spmd, %region_3.0_spmd} | conditional | flops 655360 | bytes 9175232 | solution.py:443
  21.2 0.8 %copy.6 = bf16[320,1024]{1,0:T(8,128)(2,1)} copy(bf16[320,1024]{1,0:T(8,128)(2,1)S(1)} %get-tuple-element.49) | data formatting | bytes 1310720 | tf_op jit(solution)/shard_map/cond
  22.1 0.7 %broadcast.12.clone = bf16[640,128]{1,0:T(8,128)(2,1)} broadcast(bf16[]{:T(256)} %constant.10.clone), dimensions={} | broadcast | bytes 163842 | tf_op jit(solution)/shard_map/broadcast.2
  22.8 0.7 %broadcast.12 = bf16[640,128]{1,0:T(8,128)(2,1)} broadcast(bf16[]{:T(256)} %constant.10.clone), dimensions={} | broadcast | bytes 163842 | tf_op jit(solution)/shard_map/broadcast.2
  23.4 3.1 %pool_sides.1 = (bf16[4,64,128]{2,1,0:T(8,128)(2,1)}, bf16[4,64,128]{2,1,0:T(8,128)(2,1)}) custom-call(bf16[64,64,1024]{2,1,0:T(8,128)(2,1)} %merit_ref.5, f32[8,8,1024]{2,1,0:T(8,128)} %filter_rows.1.after_ref), custom_call_target="tpu_custom_call" | custom-call | flops 8388608 | bytes 4194304 | tf_op jit(solution)/shard_map/pool_sides/pallas_call | solution.py:229
  26.5 0.0 collective-permute-done.6.near_a_ref
  26.5 0.0 collective-permute-done.7.near_b_ref
  26.6 0.9 %pad_maximum_fusion.2 = bf16[640,128]{1,0:T(8,128)(2,1)S(1)} fusion(bf16[192,128]{1,0:T(8,128)(2,1)S(1)} %get-tuple-element.46, bf16[192,128]{1,0:T(8,128)(2,1)S(1)} %get-tuple-element.44, bf16[256,128]{1,0:T(8,128)(2,1)} %bitcast.12), kind=kLoop, calls=%fused_computation.2 | loop fusion | flops 491520 | bytes 327680 | tf_op jit(solution)/shard_map/concatenate | solution.py:417
  27.4 3.1 %collective-permute-start.8 = (bf16[640,128]{1,0:T(8,128)(2,1)S(1)}, bf16[640,128]{1,0:T(8,128)(2,1)S(1)}, u32[]{:S(2)}, u32[]{:S(2)}) collective-permute-start(bf16[640,128]{1,0:T(8,128)(2,1)S(1)} %pad_maximum_fusion.2), channel_id=1, source_target_pairs={{0,1},{1,2},{2,3},{3,4},{4,5},{5,6},{6,7},{8,9},{9,10},{10,11},{11... | collective-permute-start | bytes 491528 | tf_op jit(solution)/shard_map/ppermute | solution.py:399
  30.5 0.9 %pad_maximum_fusion.3 = bf16[640,128]{1,0:T(8,128)(2,1)S(1)} fusion(bf16[192,128]{1,0:T(8,128)(2,1)S(1)} %get-tuple-element.45, bf16[192,128]{1,0:T(8,128)(2,1)S(1)} %get-tuple-element.43, bf16[256,128]{1,0:T(8,128)(2,1)} %bitcast.11), kind=kLoop, calls=%fused_computation.3 | loop fusion | flops 491520 | bytes 327680 | tf_op jit(solution)/shard_map/concatenate | solution.py:418
  31.4 4.3 %collective-permute-start.9 = (bf16[640,128]{1,0:T(8,128)(2,1)S(1)}, bf16[640,128]{1,0:T(8,128)(2,1)S(1)}, u32[]{:S(2)}, u32[]{:S(2)}) collective-permute-start(bf16[640,128]{1,0:T(8,128)(2,1)S(1)} %pad_maximum_fusion.3), channel_id=1, source_target_pairs={{1,0},{2,1},{3,2},{4,3},{5,4},{6,5},{7,6},{9,8},{10,9},{11,10},{12... | collective-permute-start | bytes 491528 | tf_op jit(solution)/shard_map/ppermute | solution.py:404
  35.7 0.0 all-to-all-done
  35.7 0.0 copy-start.2
  35.7 0.0 copy-start.3
  35.7 5.1 %collective-permute-start.5 = (f32[8,1024]{1,0:T(8,128)S(1)}, f32[8,1024]{1,0:T(8,128)S(1)}, u32[]{:S(2)}, u32[]{:S(2)}) collective-permute-start(f32[8,1024]{1,0:T(8,128)S(1)} %get-tuple-element.47.refs_1_), channel_id=1, source_target_pairs={{8,16},{16,8},{24,32},{32,24},{40,48},{48,40},{56,64},{64,56},{72,... | collective-permute-start | bytes 98312 | tf_op jit(solution)/shard_map/ppermute | solution.py:411
  40.9 0.1 collective-permute-start.4
  41.0 0.0 copy-done.2
  41.0 0.0 copy-done.3
  41.0 0.0 copy-start.1
  41.0 4.1 %pool_all.1.pooled_ref = bf16[64,64,1024]{2,1,0:T(8,128)(2,1)S(1)} custom-call(bf16[64,64,1024]{2,1,0:T(8,128)(2,1)} %merit_ref.5, f32[8,1024]{1,0:T(8,128)} %copy-done.2, f32[8,1024]{1,0:T(8,128)} %copy-done.3, bf16[640,128]{1,0:T(8,128)(2,1)} %get-tuple-element.29.refs_2_.far_west_ref, bf16[640,128]{1,0:T(8,128)(2,1)} %get-tuple-element.30.refs_3_.far_east_ref), custom_call_target="tpu_custom_call" | custom-call | flops 8388608 | bytes 4194304 | tf_op jit(solution)/shard_map/pool_all/pallas_call | solution.py:213
  45.1 0.0 collective-permute-done.5.seam_b_ref
  45.1 0.0 collective-permute-done.4.seam_a_ref
  45.1 0.0 collective-permute-done.8.west_ref
  45.1 0.0 collective-permute-done.9.east_ref
  45.1 0.0 copy-done.1
  45.1 8.9 %merge.1 = bf16[64,64,1024]{2,1,0:T(8,128)(2,1)} custom-call(s32[2,64]{1,0:T(2,128)S(1)} %bitcast.10, f32[15]{0:T(128)S(1)} %copy-done.1, bf16[64,64,1024]{2,1,0:T(8,128)(2,1)S(1)} %pool_all.1.pooled_ref, f32[64,1024]{1,0:T(8,128)S(1)} %bitcast.8, f32[8,1024]{1,0:T(8,128)S(1)} %collective-permute-done.4.seam_a_ref, ...), custom_call_target="tpu_custom_call" | custom-call | tf_op jit(solution)/shard_map/merge/pallas_call | solution.py:375
  (3 shorter events, 0.0 us)
Async XLA Ops:
  0.0 19.4 %copy-start = (s32[64,2]{0,1:T(2,128)S(1)}, s32[64,2]{0,1:T(2,128)}, u32[]{:S(2)}) copy-start(s32[64,2]{0,1:T(2,128)} %param.11) | copy-start | bytes 1540
  5.1 21.4 %collective-permute-start.6 = (bf16[192,1024]{1,0:T(8,128)(2,1)}, bf16[192,1024]{1,0:T(8,128)(2,1)S(1)}, u32[]{:S(2)}, u32[]{:S(2)}) collective-permute-start(bf16[192,1024]{1,0:T(8,128)(2,1)} %get-tuple-element.31), channel_id=1, source_target_pairs={{0,8},{8,0},{16,24},{24,16},{32,40},{40,32},{48,56},{56,48},{64,72... | collective-permute-start | bytes 1179656 | tf_op jit(solution)/shard_map/ppermute | solution.py:411
  5.8 20.7 %collective-permute-start.7 = (bf16[192,1024]{1,0:T(8,128)(2,1)}, bf16[192,1024]{1,0:T(8,128)(2,1)S(1)}, u32[]{:S(2)}, u32[]{:S(2)}) collective-permute-start(bf16[192,1024]{1,0:T(8,128)(2,1)} %get-tuple-element.32), channel_id=1, source_target_pairs={{8,16},{16,8},{24,32},{32,24},{40,48},{48,40},{56,64},{64,56},{72,... | collective-permute-start | bytes 1179656 | tf_op jit(solution)/shard_map/ppermute | solution.py:411
  13.2 22.5 %all-to-all-start = ((f32[8,8,1024]{2,1,0:T(8,128)}), f32[8,8,1024]{2,1,0:T(8,128)S(1)}, u32[]{:S(2)}, u32[]{:S(2)}) async-start(f32[8,8,1024]{2,1,0:T(8,128)} %filter_rows.1.after_ref), calls=%async_computation | async-start | bytes 524288 | tf_op jit(solution)/shard_map/all_to_all | solution.py:440
  27.4 17.7 %collective-permute-start.8 = (bf16[640,128]{1,0:T(8,128)(2,1)S(1)}, bf16[640,128]{1,0:T(8,128)(2,1)S(1)}, u32[]{:S(2)}, u32[]{:S(2)}) collective-permute-start(bf16[640,128]{1,0:T(8,128)(2,1)S(1)} %pad_maximum_fusion.2), channel_id=1, source_target_pairs={{0,1},{1,2},{2,3},{3,4},{4,5},{5,6},{6,7},{8,9},{9,10},{10,11},{11... | collective-permute-start | bytes 491528 | tf_op jit(solution)/shard_map/ppermute | solution.py:399
  31.4 13.7 %collective-permute-start.9 = (bf16[640,128]{1,0:T(8,128)(2,1)S(1)}, bf16[640,128]{1,0:T(8,128)(2,1)S(1)}, u32[]{:S(2)}, u32[]{:S(2)}) collective-permute-start(bf16[640,128]{1,0:T(8,128)(2,1)S(1)} %pad_maximum_fusion.3), channel_id=1, source_target_pairs={{1,0},{2,1},{3,2},{4,3},{5,4},{6,5},{7,6},{9,8},{10,9},{11,10},{12... | collective-permute-start | bytes 491528 | tf_op jit(solution)/shard_map/ppermute | solution.py:404
  35.7 5.3 %copy-start.2 = (f32[8,1024]{1,0:T(8,128)}, f32[8,1024]{1,0:T(8,128)S(1)}, u32[]{:S(2)}) copy-start(f32[8,1024]{1,0:T(8,128)S(1)} %get-tuple-element.48.refs_0_) | copy-start | bytes 98308
  35.7 5.3 %copy-start.3 = (f32[8,1024]{1,0:T(8,128)}, f32[8,1024]{1,0:T(8,128)S(1)}, u32[]{:S(2)}) copy-start(f32[8,1024]{1,0:T(8,128)S(1)} %get-tuple-element.47.refs_1_) | copy-start | bytes 98308
  35.7 9.3 %collective-permute-start.5 = (f32[8,1024]{1,0:T(8,128)S(1)}, f32[8,1024]{1,0:T(8,128)S(1)}, u32[]{:S(2)}, u32[]{:S(2)}) collective-permute-start(f32[8,1024]{1,0:T(8,128)S(1)} %get-tuple-element.47.refs_1_), channel_id=1, source_target_pairs={{8,16},{16,8},{24,32},{32,24},{40,48},{48,40},{56,64},{64,56},{72,... | collective-permute-start | bytes 98312 | tf_op jit(solution)/shard_map/ppermute | solution.py:411
  40.9 4.2 %collective-permute-start.4 = (f32[8,1024]{1,0:T(8,128)S(1)}, f32[8,1024]{1,0:T(8,128)S(1)}, u32[]{:S(2)}, u32[]{:S(2)}) collective-permute-start(f32[8,1024]{1,0:T(8,128)S(1)} %get-tuple-element.48.refs_0_), channel_id=1, source_target_pairs={{0,8},{8,0},{16,24},{24,16},{32,40},{40,32},{48,56},{56,48},{64,72... | collective-permute-start | bytes 98312 | tf_op jit(solution)/shard_map/ppermute | solution.py:411
  41.0 4.1 %copy-start.1 = (f32[15]{0:T(128)S(1)}, f32[15]{0:T(128)}, u32[]{:S(2)}) copy-start(f32[15]{0:T(128)} %taps_ref.3) | copy-start | bytes 184

commit v3 on v2

--- a/solution.py
+++ b/solution.py
@@ -14,7 +14,7 @@
 FORGET = 0.875
 SOME_ROWS = 192
 ALL_ROWS = VELS * MAXV
-SLAB = 8
+SLAB = 16
 CHUNK = 16
 LIMIT = 58 * 2**20
 
@@ -24,6 +24,10 @@
 
 def params(limit=LIMIT):
     return pltpu.CompilerParams(vmem_limit_bytes=limit)
+
+
+def brief():
+    return pl.CostEstimate(flops=1000, bytes_accessed=1000, transcendentals=0)
 
 
 def smem():
@@ -54,7 +58,8 @@
         in_specs=[smem(), pl.BlockSpec(memory_space=pltpu.VMEM), pl.BlockSpec(memory_space=pl.ANY)],
         out_specs=pl.BlockSpec(memory_space=pltpu.VMEM),
         scratch_shapes=[pltpu.VMEM((height, width + 2 * LANES), f32)],
-        compiler_params=params(),
+        cost_estimate=brief(),
+        compiler_params=params(16 * 2**20),
         name="filter_rows",
     )(taps_row, strip, after)
 
@@ -141,9 +146,10 @@
 
 
 def pool_outer_kernel(
-    offsets_ref, merit_ref, near_a_ref, near_b_ref, far_a_ref, far_b_ref,
+    offsets_ref, merit_ref, near_a_ref, near_b_ref, far_a_ref, far_b_ref, far_west_ref, far_east_ref, more_ref,
     held_ref, pooled_ref, packed_ref, stage_ref, sems, far_sems,
 ):
+    del far_west_ref, far_east_ref
     _, height, width = merit_ref.shape
     blocks = width // LANES
     odd = lax.axis_index("rows") % 2
@@ -192,7 +198,10 @@
             piece = packed_ref[mine, k, MAXV : MAXV + SOME_ROWS, :]
             ref[:, k * LANES : (k + 1) * LANES] = piece.astype(bf16)
 
-    @pl.when(jnp.maximum(up, down) > SOME_ROWS)
+    more = jnp.maximum(up, down) > SOME_ROWS
+    more_ref[0] = more.astype(jnp.int32)
+
+    @pl.when(more)
     def _():
         for slot, ref in enumerate((far_a_ref, far_b_ref)):
             mine = odd if slot == 1 else 1 - odd
@@ -213,7 +222,7 @@
     return pl.pallas_call(
         pool_all_kernel,
         out_shape=pltpu.VMEM(merit.shape, bf16),
-        in_specs=[anywhere] * (1 + len(after)),
+        in_specs=[anywhere] + [pl.BlockSpec(memory_space=pltpu.VMEM)] * 2 + [anywhere] * 2,
         out_specs=pl.BlockSpec(memory_space=pltpu.VMEM),
         scratch_shapes=[pltpu.VMEM(merit.shape, bf16), pltpu.SemaphoreType.DMA((2 * merit.shape[1] // CHUNK,))],
         cost_estimate=pool_cost(merit),
@@ -228,11 +237,11 @@
     anywhere = pl.BlockSpec(memory_space=pl.ANY)
     return pl.pallas_call(
         pool_sides_kernel,
-        out_shape=[jax.ShapeDtypeStruct(side, bf16)] * 2,
+        out_shape=[pltpu.VMEM(side, bf16)] * 2,
         in_specs=[anywhere, anywhere],
         out_specs=[pl.BlockSpec(memory_space=pltpu.VMEM)] * 2,
         scratch_shapes=[pltpu.VMEM((planes, height, 2 * LANES), bf16)] * 2 + [pltpu.SemaphoreType.DMA((2,))],
-        cost_estimate=pool_cost(merit),
+        cost_estimate=brief(),
         compiler_params=params(),
         name="pool_sides",
     )(merit, after)
@@ -244,9 +253,12 @@
     near, far = (SOME_ROWS, width), (ALL_ROWS - SOME_ROWS, width)
     return pl.pallas_call(
         pool_outer_kernel,
-        out_shape=[jax.ShapeDtypeStruct(near, bf16)] * 2 + [jax.ShapeDtypeStruct(far, bf16)] * 2,
+        out_shape=[jax.ShapeDtypeStruct(near, bf16)] * 2
+        + [pltpu.HBM(far, bf16)] * 2
+        + [pltpu.HBM((2 * far[0], LANES), bf16)] * 2
+        + [jax.ShapeDtypeStruct((1,), jnp.int32)],
         in_specs=[smem(), pl.BlockSpec(memory_space=pl.ANY)],
-        out_specs=[pl.BlockSpec(memory_space=pltpu.VMEM)] * 2 + [pl.BlockSpec(memory_space=pl.ANY)] * 2,
+        out_specs=[pl.BlockSpec(memory_space=pltpu.VMEM)] * 2 + [pl.BlockSpec(memory_space=pl.ANY)] * 4 + [smem()],
         scratch_shapes=[
             pltpu.VMEM(part, bf16),
             pltpu.VMEM(part, bf16),
@@ -259,6 +271,31 @@
         compiler_params=params(),
         name="pool_outer",
     )(offsets, merit)
+
+
+def join_kernel(right_ref, left_ref, a_ref, b_ref, last_ref, first_ref):
+    groups, height, _ = right_ref.shape
+    width = a_ref.shape[1]
+    for side, out, edge in ((right_ref, last_ref, width - LANES), (left_ref, first_ref, 0)):
+        for g in range(groups):
+            out[g * height : (g + 1) * height, :] = side[g]
+        for e, ref in enumerate((a_ref, b_ref)):
+            start = groups * height + e * SOME_ROWS
+            out[start : start + SOME_ROWS, :] = ref[:, edge : edge + LANES]
+
+
+def join(right, left, a, b):
+    groups, height, _ = right.shape
+    vmem = pl.BlockSpec(memory_space=pltpu.VMEM)
+    return pl.pallas_call(
+        join_kernel,
+        out_shape=[jax.ShapeDtypeStruct((groups * height + 2 * SOME_ROWS, LANES), bf16)] * 2,
+        in_specs=[vmem] * 4,
+        out_specs=[vmem] * 2,
+        cost_estimate=brief(),
+        compiler_params=params(16 * 2**20),
+        name="join",
+    )(right, left, a, b)
 
 
 def weighted_rows(taps_ref, column_ref, k, count):
@@ -411,38 +448,28 @@
     return lax.ppermute(value, axis, pairs)
 
 
-def to_sides(right, left, a, b):
-    width = a.shape[1]
-    east_end, west_end = slice(width - LANES, width), slice(0, LANES)
-    last = jnp.concatenate(right + [a[:, east_end], b[:, east_end]], axis=0)
-    first = jnp.concatenate(left + [a[:, west_end], b[:, west_end]], axis=0)
-    return pass_on(last, "cols"), pass_back(first, "cols")
-
-
-def far_exchange(far_a, far_b):
+def far_exchange(state):
+    count, far_a, far_b, _, _ = state
     far_b = trade(far_b, "rows", 1)
     far_a = trade(far_a, "rows", 0)
-    return (far_a, far_b) + to_sides([], [], far_a, far_b)
-
-
-def no_exchange(far_a, far_b):
-    empty = jnp.zeros((2 * far_a.shape[0], LANES), bf16)
-    return far_a, far_b, empty, empty
+    width = far_a.shape[1]
+    last = jnp.concatenate([far_a[:, width - LANES :], far_b[:, width - LANES :]], axis=0)
+    first = jnp.concatenate([far_a[:, :LANES], far_b[:, :LANES]], axis=0)
+    return count - 1, far_a, far_b, pass_on(last, "cols"), pass_back(first, "cols")
 
 
 def on_device(frame, taps_row, taps_col, merit, offsets):
     _, height, width = merit.shape
     turned = offsets.T
-    near_a, near_b, far_a, far_b = pool_outer(merit, turned)
+    near_a, near_b, *fars, more = pool_outer(merit, turned)
     b = trade(near_b, "rows", 1)
     a = trade(near_a, "rows", 0)
-    pieces = filter_rows(frame, taps_row, frame.shape[1] // width, far_a)
+    pieces = filter_rows(frame, taps_row, frame.shape[1] // width, a)
     tile = lax.all_to_all(pieces, "cols", split_axis=0, concat_axis=0, tiled=True).reshape(height, width)
-    shifts = offsets[:, 0]
-    most = jnp.maximum(jnp.sum(jnp.maximum(shifts, 0)), jnp.sum(jnp.maximum(-shifts, 0)))
-    fars = lax.cond(most > SOME_ROWS, far_exchange, no_exchange, far_a, far_b)
+    _, *fars = lax.while_loop(lambda state: state[0] > 0, far_exchange, (more.reshape(()), *fars))
     right, left = pool_sides(merit, pieces)
-    west, east = to_sides([right.reshape(-1, LANES)], [left.reshape(-1, LANES)], a, b)
+    last, first = join(right, left, a, b)
+    west, east = pass_on(last, "cols"), pass_back(first, "cols")
     top, bottom = tile[:MAXV], tile[height - MAXV :]
     odd = lax.axis_index("rows") % 2 == 1
     for_b, for_a = jnp.where(odd, bottom, top), jnp.where(odd, top, bottom)

time: 54.5 us -> 49.3 us (0.905)
  local copies, waits for them, and re-layouts: 2.28 us -> 0.03 us
  other arithmetic: 2.36 us -> 0.64 us
  between operations: 1.39 us -> 0.22 us
  Pallas kernels: 24.5 us -> 23.7 us
  loops' own time: 0.01 us -> 0.57 us
    concatenate x2 -> x0, other arithmetic: 1.7 us -> none  [the longest x1 0.85 us: to_sides(): last = jnp.concatenate(right + [a[:, east_end], b[:, east_end]], axis=0)]
    another operation x2 -> x0, local copies, waits for them, and re-layouts: 1.38 us -> none
    ppermute x4, starting transfers between devices: 9.91 us -> 8.87 us  [trade(): return lax.ppermute(value, axis, pairs)]
    cond x1 -> x0, local copies, waits for them, and re-layouts: 0.85 us -> none
    pallas_call x1, Pallas kernels: 4.08 us -> 4.92 us  [pool_all(): pl.pallas_call(pool_all_kernel, out_shape=pltpu.VMEM(merit.shape, bf16),...]
    ppermute x1, starting transfers between devices: 4.3 us -> 5.08 us  [pass_back(): return lax.ppermute(value, axis, [(i + 1, i) for i in range(count - 1)])]
    reduce_sum x1 -> x0, other arithmetic: 0.65 us -> none  [on_device(): jnp.sum(jnp.maximum(-shifts, 0))]
    select_n x1, other arithmetic: 0.01 us -> 0.64 us  [on_device(): for_b, for_a = (jnp.where(odd, bottom, top), jnp.where(odd, top, bottom))]
  transfers between devices with their start and end apart: 7 -> 7, of which waited for: 0 -> 0; matrix products, arithmetic and copies ran while one was open for 9% -> 1% of each run, Pallas kernels for 19% -> 21%
where the time goes in v3:
time: 49.3 us; the launch traced here: 48.7 us
  Pallas kernels  23.7 us (48%)
  starting transfers between devices  23.5 us (48%)
  other arithmetic  0.64 us (1%)
  loops' own time  0.57 us (1%)
    ppermute x4, starting transfers between devices, trade(): return lax.ppermute(value, axis, pairs)  8.87 us
    pallas_call x1, Pallas kernels, merge(): pl.pallas_call(merge_kernel, grid=(planes // SLAB,), out_shape=jax.ShapeD...  8.33 us
    all_to_all x1, starting transfers between devices, on_device(): lax.all_to_all(pieces, 'cols', split_axis=0, concat_axis=0, tiled=True)  6.21 us
    pallas_call x1, Pallas kernels, pool_outer(): pl.pallas_call(pool_outer_kernel, out_shape=[jax.ShapeDtypeStruct(near, b...  5.1 us
    ppermute x1, starting transfers between devices, pass_back(): return lax.ppermute(value, axis, [(i + 1, i) for i in range(count - 1)])  5.08 us
    pallas_call x1, Pallas kernels, pool_all(): pl.pallas_call(pool_all_kernel, out_shape=pltpu.VMEM(merit.shape, bf16),...  4.92 us
    ppermute x1, starting transfers between devices, pass_on(): return lax.ppermute(value, axis, [(i, i + 1) for i in range(count - 1)])  3.34 us
    pallas_call x1, Pallas kernels, filter_rows(): pl.pallas_call(filter_rows_kernel, out_shape=jax.ShapeDtypeStruct((pieces...  2.91 us
  transfers between devices with their start and end apart: 7, of which 0 were waited for; matrix products, arithmetic and copies ran while one was open for 1% of the time, Pallas kernels for 21%

profile of v3, /device:TPU:7, one launch (start us, length us, event | category | flops | bytes accessed | tf_op | source)
XLA Modules:
  0.0 48.7 jit_solution(11839057818617734297)
XLA Ops:
  0.0 0.0 copy-start.2
  0.0 0.0 copy-start
  0.0 5.1 %pool_outer.1 = (bf16[192,1024]{1,0:T(8,128)(2,1)}, bf16[192,1024]{1,0:T(8,128)(2,1)}, bf16[320,1024]{1,0:T(8,128)(2,1)}, bf16[320,1024]{1,0:T(8,128)(2,1)}, bf1...) custom-call(s32[2,64]{1,0:T(2,128)} %bitcast.8, bf16[64,64,1024]{2,1,0:T(8,128)(2,1)} %merit_ref.5), custom_call_target="tpu_custom_call" | custom-call | flops 8388608 | bytes 4194304 | tf_op jit(solution)/shard_map/pool_outer/pallas_call | solution.py:254
  5.1 0.8 %collective-permute-start.4 = (bf16[192,1024]{1,0:T(8,128)(2,1)}, bf16[192,1024]{1,0:T(8,128)(2,1)S(1)}, u32[]{:S(2)}, u32[]{:S(2)}) collective-permute-start(bf16[192,1024]{1,0:T(8,128)(2,1)} %get-tuple-element.44), channel_id=1, source_target_pairs={{0,8},{8,0},{16,24},{24,16},{32,40},{40,32},{48,56},{56,48},{64,72... | collective-permute-start | bytes 1179656 | tf_op jit(solution)/shard_map/ppermute | solution.py:448
  5.9 3.9 %collective-permute-start.7 = (bf16[192,1024]{1,0:T(8,128)(2,1)}, bf16[192,1024]{1,0:T(8,128)(2,1)S(1)}, u32[]{:S(2)}, u32[]{:S(2)}) collective-permute-start(bf16[192,1024]{1,0:T(8,128)(2,1)} %get-tuple-element.52), channel_id=1, source_target_pairs={{8,16},{16,8},{24,32},{32,24},{40,48},{48,40},{56,64},{64,56},{72,... | collective-permute-start | bytes 1179656 | tf_op jit(solution)/shard_map/ppermute | solution.py:448
  9.8 0.0 collective-permute-done.4.after_ref.a_ref.near_a_ref
  9.8 0.0 copy-done.2
  9.8 0.0 copy-done
  9.8 2.9 %filter_rows.1.after_ref = f32[8,8,1024]{2,1,0:T(8,128)} custom-call(f32[15]{0:T(128)S(1)} %copy-done.2, f32[8,8192]{1,0:T(8,128)S(1)} %copy-done, bf16[192,1024]{1,0:T(8,128)(2,1)S(1)} %collective-permute-done.4.after_ref.a_ref.near_a_ref), custom_call_target="tpu_custom_call" | custom-call | flops 1000 | bytes 1000 | tf_op jit(solution)/shard_map/filter_rows/pallas_call | solution.py:55
  12.8 6.2 %all-to-all-start = ((f32[8,8,1024]{2,1,0:T(8,128)}), f32[8,8,1024]{2,1,0:T(8,128)S(1)}, u32[]{:S(2)}, u32[]{:S(2)}) async-start(f32[8,8,1024]{2,1,0:T(8,128)} %filter_rows.1.after_ref), calls=%async_computation | async-start | bytes 524288 | tf_op jit(solution)/shard_map/all_to_all | solution.py:468
  19.0 2.4 %pool_sides.1 = (bf16[4,64,128]{2,1,0:T(8,128)(2,1)S(1)}, bf16[4,64,128]{2,1,0:T(8,128)(2,1)S(1)}) custom-call(bf16[64,64,1024]{2,1,0:T(8,128)(2,1)} %merit_ref.5, f32[8,8,1024]{2,1,0:T(8,128)} %filter_rows.1.after_ref), custom_call_target="tpu_custom_call" | custom-call | flops 1000 | bytes 1000 | tf_op jit(solution)/shard_map/pool_sides/pallas_call | solution.py:238
  21.4 0.0 collective-permute-done.7.b_ref.near_b_ref
  21.5 3.3 %collective-permute-start.8 = (bf16[640,128]{1,0:T(8,128)(2,1)S(1)}, bf16[640,128]{1,0:T(8,128)(2,1)S(1)}, u32[]{:S(2)}, u32[]{:S(2)}) collective-permute-start(bf16[640,128]{1,0:T(8,128)(2,1)S(1)} %get-tuple-element.55), channel_id=1, source_target_pairs={{0,1},{1,2},{2,3},{3,4},{4,5},{5,6},{6,7},{8,9},{9,10},{10,11},{11... | collective-permute-start | bytes 491528 | tf_op jit(solution)/shard_map/ppermute | solution.py:436
  24.8 5.1 %collective-permute-start.9 = (bf16[640,128]{1,0:T(8,128)(2,1)S(1)}, bf16[640,128]{1,0:T(8,128)(2,1)S(1)}, u32[]{:S(2)}, u32[]{:S(2)}) collective-permute-start(bf16[640,128]{1,0:T(8,128)(2,1)S(1)} %get-tuple-element.56), channel_id=1, source_target_pairs={{1,0},{2,1},{3,2},{4,3},{5,4},{6,5},{7,6},{9,8},{10,9},{11,10},{12... | collective-permute-start | bytes 491528 | tf_op jit(solution)/shard_map/ppermute | solution.py:441
  29.9 0.0 all-to-all-done
  29.9 0.6 %select_bitcast_fusion = (f32[8,1024]{1,0:T(8,128)}, f32[8,1024]{1,0:T(8,128)}) fusion(f32[8,8,1024]{2,1,0:T(8,128)S(1)} %all-to-all-done, pred[]{:T(512)S(6)} %eq.5), kind=kLoop, calls=%fused_computation.2 | loop fusion | flops 16384 | bytes 131073 | tf_op jit(solution)/shard_map/jit(_where)/select_n | solution.py:475
  30.6 4.1 %collective-permute-start.6 = (f32[8,1024]{1,0:T(8,128)}, f32[8,1024]{1,0:T(8,128)S(1)}, u32[]{:S(2)}, u32[]{:S(2)}) collective-permute-start(f32[8,1024]{1,0:T(8,128)} %get-tuple-element.73.refs_1_), channel_id=1, source_target_pairs={{8,16},{16,8},{24,32},{32,24},{40,48},{48,40},{56,64},{64,56},{72,... | collective-permute-start | bytes 98312 | tf_op jit(solution)/shard_map/ppermute | solution.py:448
  34.7 0.6 %while.16 = (s32[]{:T(128)}, bf16[320,1024]{1,0:T(8,128)(2,1)}, bf16[320,1024]{1,0:T(8,128)(2,1)}, bf16[640,128]{1,0:T(8,128)(2,1)}, bf16[640,128]{1,0:T(8,128)(2,1)}, /*index=5*/s32[]{:T(128)}) while((s32[]{:T(128)}, bf16[320,1024]{1,0:T(8,128)(2,1)}, bf16[320,1024]{1,0:T(8,128)(2,1)}, bf16[640,128]{1,0:T(8,128)(2,1)}, ...), condition=%wide.region_1.0_spmd, body=%wide.region_0.0_spmd.sunk | while | flops 655362 | bytes 11141377 | solution.py:469
  35.2 0.1 collective-permute-start.5
  35.3 0.0 copy-start.1
  35.3 0.0 copy-start.3
  35.4 0.0 copy-start.5
  35.4 0.0 copy-start.6
  35.4 4.9 %pool_all.1.pooled_ref = bf16[64,64,1024]{2,1,0:T(8,128)(2,1)S(1)} custom-call(bf16[64,64,1024]{2,1,0:T(8,128)(2,1)} %merit_ref.5, f32[8,1024]{1,0:T(8,128)} %get-tuple-element.74.refs_0_, f32[8,1024]{1,0:T(8,128)} %get-tuple-element.73.refs_1_, bf16[640,128]{1,0:T(8,128)(2,1)} %get-tuple-element.50.refs_2_.far_west_ref, ...), custom_call_target="tpu_custom_call" | custom-call | flops 8388608 | bytes 4194304 | tf_op jit(solution)/shard_map/pool_all/pallas_call | solution.py:222
  40.3 0.0 collective-permute-done.8.west_ref
  40.3 0.0 collective-permute-done.9.east_ref
  40.3 0.0 collective-permute-done.6.seam_b_ref
  40.3 0.0 collective-permute-done.5.seam_a_ref
  40.3 0.0 copy-done.1
  40.4 0.0 copy-done.3
  40.4 0.0 copy-done.5
  40.4 0.0 copy-done.6
  40.4 8.3 %merge.1 = bf16[64,64,1024]{2,1,0:T(8,128)(2,1)} custom-call(s32[2,64]{1,0:T(2,128)S(1)} %bitcast.9, f32[15]{0:T(128)S(1)} %copy-done.3, bf16[64,64,1024]{2,1,0:T(8,128)(2,1)S(1)} %pool_all.1.pooled_ref, f32[64,1024]{1,0:T(8,128)S(1)} %bitcast.7, f32[8,1024]{1,0:T(8,128)S(1)} %collective-permute-done.5.seam_a_ref, ...), custom_call_target="tpu_custom_call" | custom-call | tf_op jit(solution)/shard_map/merge/pallas_call | solution.py:412
  (1 shorter events, 0.0 us)
Async XLA Ops:
  0.0 9.8 %copy-start.2 = (f32[15]{0:T(128)S(1)}, f32[15]{0:T(128)}, u32[]{:S(2)}) copy-start(f32[15]{0:T(128)} %taps_ref.2) | copy-start | bytes 184
  0.0 9.8 %copy-start = (f32[8,8192]{1,0:T(8,128)S(1)}, f32[8,8192]{1,0:T(8,128)}, u32[]{:S(2)}) copy-start(f32[8,8192]{1,0:T(8,128)} %strip_ref.1) | copy-start | bytes 786436
  5.1 4.7 %collective-permute-start.4 = (bf16[192,1024]{1,0:T(8,128)(2,1)}, bf16[192,1024]{1,0:T(8,128)(2,1)S(1)}, u32[]{:S(2)}, u32[]{:S(2)}) collective-permute-start(bf16[192,1024]{1,0:T(8,128)(2,1)} %get-tuple-element.44), channel_id=1, source_target_pairs={{0,8},{8,0},{16,24},{24,16},{32,40},{40,32},{48,56},{56,48},{64,72... | collective-permute-start | bytes 1179656 | tf_op jit(solution)/shard_map/ppermute | solution.py:448
  5.9 15.5 %collective-permute-start.7 = (bf16[192,1024]{1,0:T(8,128)(2,1)}, bf16[192,1024]{1,0:T(8,128)(2,1)S(1)}, u32[]{:S(2)}, u32[]{:S(2)}) collective-permute-start(bf16[192,1024]{1,0:T(8,128)(2,1)} %get-tuple-element.52), channel_id=1, source_target_pairs={{8,16},{16,8},{24,32},{32,24},{40,48},{48,40},{56,64},{64,56},{72,... | collective-permute-start | bytes 1179656 | tf_op jit(solution)/shard_map/ppermute | solution.py:448
  12.8 17.2 %all-to-all-start = ((f32[8,8,1024]{2,1,0:T(8,128)}), f32[8,8,1024]{2,1,0:T(8,128)S(1)}, u32[]{:S(2)}, u32[]{:S(2)}) async-start(f32[8,8,1024]{2,1,0:T(8,128)} %filter_rows.1.after_ref), calls=%async_computation | async-start | bytes 524288 | tf_op jit(solution)/shard_map/all_to_all | solution.py:468
  21.5 18.8 %collective-permute-start.8 = (bf16[640,128]{1,0:T(8,128)(2,1)S(1)}, bf16[640,128]{1,0:T(8,128)(2,1)S(1)}, u32[]{:S(2)}, u32[]{:S(2)}) collective-permute-start(bf16[640,128]{1,0:T(8,128)(2,1)S(1)} %get-tuple-element.55), channel_id=1, source_target_pairs={{0,1},{1,2},{2,3},{3,4},{4,5},{5,6},{6,7},{8,9},{9,10},{10,11},{11... | collective-permute-start | bytes 491528 | tf_op jit(solution)/shard_map/ppermute | solution.py:436
  24.8 15.5 %collective-permute-start.9 = (bf16[640,128]{1,0:T(8,128)(2,1)S(1)}, bf16[640,128]{1,0:T(8,128)(2,1)S(1)}, u32[]{:S(2)}, u32[]{:S(2)}) collective-permute-start(bf16[640,128]{1,0:T(8,128)(2,1)S(1)} %get-tuple-element.56), channel_id=1, source_target_pairs={{1,0},{2,1},{3,2},{4,3},{5,4},{6,5},{7,6},{9,8},{10,9},{11,10},{12... | collective-permute-start | bytes 491528 | tf_op jit(solution)/shard_map/ppermute | solution.py:441
  30.6 9.8 %collective-permute-start.6 = (f32[8,1024]{1,0:T(8,128)}, f32[8,1024]{1,0:T(8,128)S(1)}, u32[]{:S(2)}, u32[]{:S(2)}) collective-permute-start(f32[8,1024]{1,0:T(8,128)} %get-tuple-element.73.refs_1_), channel_id=1, source_target_pairs={{8,16},{16,8},{24,32},{32,24},{40,48},{48,40},{56,64},{64,56},{72,... | collective-permute-start | bytes 98312 | tf_op jit(solution)/shard_map/ppermute | solution.py:448
  35.2 5.1 %collective-permute-start.5 = (f32[8,1024]{1,0:T(8,128)}, f32[8,1024]{1,0:T(8,128)S(1)}, u32[]{:S(2)}, u32[]{:S(2)}) collective-permute-start(f32[8,1024]{1,0:T(8,128)} %get-tuple-element.74.refs_0_), channel_id=1, source_target_pairs={{0,8},{8,0},{16,24},{24,16},{32,40},{40,32},{48,56},{56,48},{64,72... | collective-permute-start | bytes 98312 | tf_op jit(solution)/shard_map/ppermute | solution.py:448
  35.3 5.0 %copy-start.1 = (s32[64,2]{0,1:T(2,128)S(1)}, s32[64,2]{0,1:T(2,128)}, u32[]{:S(2)}) copy-start(s32[64,2]{0,1:T(2,128)} %param.11) | copy-start | bytes 1540
  35.3 5.0 %copy-start.3 = (f32[15]{0:T(128)S(1)}, f32[15]{0:T(128)}, u32[]{:S(2)}) copy-start(f32[15]{0:T(128)} %taps_ref.3) | copy-start | bytes 184
  35.4 5.0 %copy-start.5 = (bf16[640,128]{1,0:T(8,128)(2,1)S(1)}, bf16[640,128]{1,0:T(8,128)(2,1)}, u32[]{:S(2)}) copy-start(bf16[640,128]{1,0:T(8,128)(2,1)} %get-tuple-element.50.refs_2_.far_west_ref) | copy-start | bytes 491524
  35.4 5.0 %copy-start.6 = (bf16[320,1024]{1,0:T(8,128)(2,1)S(1)}, bf16[320,1024]{1,0:T(8,128)(2,1)}, u32[]{:S(2)}) copy-start(bf16[320,1024]{1,0:T(8,128)(2,1)} %get-tuple-element.58.far_b_ref) | copy-start | bytes 1966084

commit v4 on v3

--- a/solution.py
+++ b/solution.py
@@ -12,7 +12,7 @@
 VELS = VGRID * VGRID
 LANES = 128
 FORGET = 0.875
-SOME_ROWS = 192
+SOME_ROWS = 208
 ALL_ROWS = VELS * MAXV
 SLAB = 16
 CHUNK = 16
@@ -132,8 +132,8 @@
     pool_as_they_come(copies, sizes, held_ref, pooled_ref)
 
 
-def pool_sides_kernel(merit_ref, after_ref, right_ref, left_ref, held_ref, pooled_ref, sems):
-    del after_ref
+def pool_sides_kernel(merit_ref, after_ref, far_ref, right_ref, left_ref, held_ref, pooled_ref, sems):
+    del after_ref, far_ref
     _, height, width = merit_ref.shape
     sizes = [(height, 0, LANES, left) for left in (0, LANES)]
     copies = []
@@ -222,7 +222,7 @@
     return pl.pallas_call(
         pool_all_kernel,
         out_shape=pltpu.VMEM(merit.shape, bf16),
-        in_specs=[anywhere] + [pl.BlockSpec(memory_space=pltpu.VMEM)] * 2 + [anywhere] * 2,
+        in_specs=[anywhere] * (1 + len(after)),
         out_specs=pl.BlockSpec(memory_space=pltpu.VMEM),
         scratch_shapes=[pltpu.VMEM(merit.shape, bf16), pltpu.SemaphoreType.DMA((2 * merit.shape[1] // CHUNK,))],
         cost_estimate=pool_cost(merit),
@@ -231,20 +231,20 @@
     )(merit, *after)
 
 
-def pool_sides(merit, after):
+def pool_sides(merit, after, far):
     planes, height, _ = merit.shape
     side = (planes * MAXV // LANES, height, LANES)
     anywhere = pl.BlockSpec(memory_space=pl.ANY)
     return pl.pallas_call(
         pool_sides_kernel,
         out_shape=[pltpu.VMEM(side, bf16)] * 2,
-        in_specs=[anywhere, anywhere],
+        in_specs=[anywhere] * 3,
         out_specs=[pl.BlockSpec(memory_space=pltpu.VMEM)] * 2,
         scratch_shapes=[pltpu.VMEM((planes, height, 2 * LANES), bf16)] * 2 + [pltpu.SemaphoreType.DMA((2,))],
         cost_estimate=brief(),
         compiler_params=params(),
         name="pool_sides",
-    )(merit, after)
+    )(merit, after, far)
 
 
 def pool_outer(merit, offsets):
@@ -467,7 +467,7 @@
     pieces = filter_rows(frame, taps_row, frame.shape[1] // width, a)
     tile = lax.all_to_all(pieces, "cols", split_axis=0, concat_axis=0, tiled=True).reshape(height, width)
     _, *fars = lax.while_loop(lambda state: state[0] > 0, far_exchange, (more.reshape(()), *fars))
-    right, left = pool_sides(merit, pieces)
+    right, left = pool_sides(merit, pieces, fars[2])
     last, first = join(right, left, a, b)
     west, east = pass_on(last, "cols"), pass_back(first, "cols")
     top, bottom = tile[:MAXV], tile[height - MAXV :]

time: 49.3 us -> 48 us (0.974)
  other arithmetic: 0.64 us -> 0.01 us
  Pallas kernels: 23.7 us -> 23.1 us
    pallas_call x1, Pallas kernels: 4.92 us -> 4.16 us  [pool_all(): pl.pallas_call(pool_all_kernel, out_shape=pltpu.VMEM(merit.shape, bf16),...]
    select_n x1, other arithmetic: 0.64 us -> 0.01 us  [on_device(): for_b, for_a = (jnp.where(odd, bottom, top), jnp.where(odd, top, bottom))]
  transfers between devices with their start and end apart: 7 -> 7, of which waited for: 0 -> 0; matrix products, arithmetic and copies ran while one was open for 1% -> 0% of each run, Pallas kernels for 21% -> 20%
where the time goes in v4:
time: 48 us; the launch traced here: 47.5 us
  starting transfers between devices  23.5 us (49%)
  Pallas kernels  23.1 us (48%)
  loops' own time  0.55 us (1%)
    ppermute x4, starting transfers between devices, trade(): return lax.ppermute(value, axis, pairs)  8.84 us
    pallas_call x1, Pallas kernels, merge(): pl.pallas_call(merge_kernel, grid=(planes // SLAB,), out_shape=jax.ShapeD...  8.33 us
    all_to_all x1, starting transfers between devices, on_device(): lax.all_to_all(pieces, 'cols', split_axis=0, concat_axis=0, tiled=True)  6.21 us
    pallas_call x1, Pallas kernels, pool_outer(): pl.pallas_call(pool_outer_kernel, out_shape=[jax.ShapeDtypeStruct(near, b...  5.16 us
    ppermute x1, starting transfers between devices, pass_back(): return lax.ppermute(value, axis, [(i + 1, i) for i in range(count - 1)])  4.78 us
    pallas_call x1, Pallas kernels, pool_all(): pl.pallas_call(pool_all_kernel, out_shape=pltpu.VMEM(merit.shape, bf16),...  4.16 us
    ppermute x1, starting transfers between devices, pass_on(): return lax.ppermute(value, axis, [(i, i + 1) for i in range(count - 1)])  3.69 us
    pallas_call x1, Pallas kernels, filter_rows(): pl.pallas_call(filter_rows_kernel, out_shape=jax.ShapeDtypeStruct((pieces...  2.93 us
  transfers between devices with their start and end apart: 7, of which 0 were waited for; matrix products, arithmetic and copies ran while one was open for 0% of the time, Pallas kernels for 20%

profile of v4, /device:TPU:7, one launch (start us, length us, event | category | flops | bytes accessed | tf_op | source)
XLA Modules:
  0.0 47.5 jit_solution(13480252420862020045)
XLA Ops:
  0.0 0.0 copy-start.2
  0.0 0.0 copy-start
  0.0 5.2 %pool_outer.1 = (bf16[208,1024]{1,0:T(8,128)(2,1)}, bf16[208,1024]{1,0:T(8,128)(2,1)}, bf16[304,1024]{1,0:T(8,128)(2,1)}, bf16[304,1024]{1,0:T(8,128)(2,1)}, bf1...) custom-call(s32[2,64]{1,0:T(2,128)} %bitcast.8, bf16[64,64,1024]{2,1,0:T(8,128)(2,1)} %merit_ref.5), custom_call_target="tpu_custom_call" | custom-call | flops 8388608 | bytes 4194304 | tf_op jit(solution)/shard_map/pool_outer/pallas_call | solution.py:254
  5.2 0.8 %collective-permute-start.4 = (bf16[208,1024]{1,0:T(8,128)(2,1)}, bf16[208,1024]{1,0:T(8,128)(2,1)S(1)}, u32[]{:S(2)}, u32[]{:S(2)}) collective-permute-start(bf16[208,1024]{1,0:T(8,128)(2,1)} %get-tuple-element.44), channel_id=1, source_target_pairs={{0,8},{8,0},{16,24},{24,16},{32,40},{40,32},{48,56},{56,48},{64,72... | collective-permute-start | bytes 1277960 | tf_op jit(solution)/shard_map/ppermute | solution.py:448
  5.9 3.9 %collective-permute-start.7 = (bf16[208,1024]{1,0:T(8,128)(2,1)}, bf16[208,1024]{1,0:T(8,128)(2,1)S(1)}, u32[]{:S(2)}, u32[]{:S(2)}) collective-permute-start(bf16[208,1024]{1,0:T(8,128)(2,1)} %get-tuple-element.52), channel_id=1, source_target_pairs={{8,16},{16,8},{24,32},{32,24},{40,48},{48,40},{56,64},{64,56},{72,... | collective-permute-start | bytes 1277960 | tf_op jit(solution)/shard_map/ppermute | solution.py:448
  9.9 0.0 collective-permute-done.4.after_ref.a_ref.near_a_ref
  9.9 0.0 copy-done.2
  9.9 0.0 copy-done
  9.9 2.9 %filter_rows.1.after_ref = f32[8,8,1024]{2,1,0:T(8,128)} custom-call(f32[15]{0:T(128)S(1)} %copy-done.2, f32[8,8192]{1,0:T(8,128)S(1)} %copy-done, bf16[208,1024]{1,0:T(8,128)(2,1)S(1)} %collective-permute-done.4.after_ref.a_ref.near_a_ref), custom_call_target="tpu_custom_call" | custom-call | flops 1000 | bytes 1000 | tf_op jit(solution)/shard_map/filter_rows/pallas_call | solution.py:55
  12.8 6.2 %all-to-all-start = ((f32[8,8,1024]{2,1,0:T(8,128)}), f32[8,8,1024]{2,1,0:T(8,128)S(1)}, u32[]{:S(2)}, u32[]{:S(2)}) async-start(f32[8,8,1024]{2,1,0:T(8,128)} %filter_rows.1.after_ref), calls=%async_computation | async-start | bytes 524288 | tf_op jit(solution)/shard_map/all_to_all | solution.py:468
  19.1 0.6 %while.16 = (s32[]{:T(128)}, bf16[304,1024]{1,0:T(8,128)(2,1)}, bf16[304,1024]{1,0:T(8,128)(2,1)}, bf16[608,128]{1,0:T(8,128)(2,1)}, bf16[608,128]{1,0:T(8,128)(2,1)}, /*index=5*/s32[]{:T(128)}) while((s32[]{:T(128)}, bf16[304,1024]{1,0:T(8,128)(2,1)}, bf16[304,1024]{1,0:T(8,128)(2,1)}, bf16[608,128]{1,0:T(8,128)(2,1)}, ...), condition=%wide.region_1.0_spmd, body=%wide.region_0.0_spmd.sunk | while | flops 622594 | bytes 11206941 | solution.py:469
  19.6 0.0 copy-start.5
  19.6 0.0 copy-start.7
  19.6 2.5 %pool_sides.1 = (bf16[4,64,128]{2,1,0:T(8,128)(2,1)S(1)}, bf16[4,64,128]{2,1,0:T(8,128)(2,1)S(1)}) custom-call(bf16[64,64,1024]{2,1,0:T(8,128)(2,1)} %merit_ref.5, f32[8,8,1024]{2,1,0:T(8,128)} %filter_rows.1.after_ref, bf16[608,128]{1,0:T(8,128)(2,1)} %get-tuple-element.50.refs_2_.far_ref.far_west_ref), custom_call_target="tpu_custom_call" | custom-call | flops 1000 | bytes 1000 | tf_op jit(solution)/shard_map/pool_sides/pallas_call | solution.py:238
  22.1 0.0 collective-permute-done.7.b_ref.near_b_ref
  22.1 0.1 join.1
  22.2 3.7 %collective-permute-start.8 = (bf16[672,128]{1,0:T(8,128)(2,1)S(1)}, bf16[672,128]{1,0:T(8,128)(2,1)S(1)}, u32[]{:S(2)}, u32[]{:S(2)}) collective-permute-start(bf16[672,128]{1,0:T(8,128)(2,1)S(1)} %get-tuple-element.55), channel_id=1, source_target_pairs={{0,1},{1,2},{2,3},{3,4},{4,5},{5,6},{6,7},{8,9},{9,10},{10,11},{11... | collective-permute-start | bytes 516104 | tf_op jit(solution)/shard_map/ppermute | solution.py:436
  25.9 4.8 %collective-permute-start.9 = (bf16[672,128]{1,0:T(8,128)(2,1)S(1)}, bf16[672,128]{1,0:T(8,128)(2,1)S(1)}, u32[]{:S(2)}, u32[]{:S(2)}) collective-permute-start(bf16[672,128]{1,0:T(8,128)(2,1)S(1)} %get-tuple-element.56), channel_id=1, source_target_pairs={{1,0},{2,1},{3,2},{4,3},{5,4},{6,5},{7,6},{9,8},{10,9},{11,10},{12... | collective-permute-start | bytes 516104 | tf_op jit(solution)/shard_map/ppermute | solution.py:441
  30.7 0.0 all-to-all-done
  30.7 0.0 copy-start.10
  30.7 0.0 copy-start.11
  30.7 4.1 %collective-permute-start.6 = (f32[8,1024]{1,0:T(8,128)S(1)}, f32[8,1024]{1,0:T(8,128)S(1)}, u32[]{:S(2)}, u32[]{:S(2)}) collective-permute-start(f32[8,1024]{1,0:T(8,128)S(1)} %get-tuple-element.73.refs_1_), channel_id=1, source_target_pairs={{8,16},{16,8},{24,32},{32,24},{40,48},{48,40},{56,64},{64,56},{72,... | collective-permute-start | bytes 98312 | tf_op jit(solution)/shard_map/ppermute | solution.py:448
  34.8 0.1 collective-permute-start.5
  34.9 0.0 copy-done.10
  34.9 0.0 copy-done.11
  34.9 0.0 copy-done.5
  34.9 0.0 copy-done.7
  34.9 0.0 copy-start.1
  34.9 0.0 copy-start.3
  34.9 0.0 copy-start.8
  35.0 0.0 copy-start.9
  35.0 4.2 %pool_all.1.pooled_ref = bf16[64,64,1024]{2,1,0:T(8,128)(2,1)S(1)} custom-call(bf16[64,64,1024]{2,1,0:T(8,128)(2,1)} %merit_ref.5, f32[8,1024]{1,0:T(8,128)} %copy-done.10, f32[8,1024]{1,0:T(8,128)} %copy-done.11, bf16[608,128]{1,0:T(8,128)(2,1)S(1)} %copy-done.5, bf16[608,128]{1,0:T(8,128)(2,1)S(1)} %copy-done.7), custom_call_target="tpu_custom_call" | custom-call | flops 8388608 | bytes 4194304 | tf_op jit(solution)/shard_map/pool_all/pallas_call | solution.py:222
  39.1 0.0 collective-permute-done.8.west_ref
  39.1 0.0 collective-permute-done.9.east_ref
  39.2 0.0 collective-permute-done.6.seam_b_ref
  39.2 0.0 collective-permute-done.5.seam_a_ref
  39.2 0.0 copy-done.1
  39.2 0.0 copy-done.3
  39.2 0.0 copy-done.8
  39.2 0.0 copy-done.9
  39.2 8.3 %merge.1 = bf16[64,64,1024]{2,1,0:T(8,128)(2,1)} custom-call(s32[2,64]{1,0:T(2,128)S(1)} %bitcast.9, f32[15]{0:T(128)S(1)} %copy-done.3, bf16[64,64,1024]{2,1,0:T(8,128)(2,1)S(1)} %pool_all.1.pooled_ref, f32[64,1024]{1,0:T(8,128)S(1)} %bitcast.7, f32[8,1024]{1,0:T(8,128)S(1)} %collective-permute-done.5.seam_a_ref, ...), custom_call_target="tpu_custom_call" | custom-call | tf_op jit(solution)/shard_map/merge/pallas_call | solution.py:412
  (1 shorter events, 0.0 us)
Async XLA Ops:
  0.0 9.9 %copy-start.2 = (f32[15]{0:T(128)S(1)}, f32[15]{0:T(128)}, u32[]{:S(2)}) copy-start(f32[15]{0:T(128)} %taps_ref.2) | copy-start | bytes 184
  0.0 9.9 %copy-start = (f32[8,8192]{1,0:T(8,128)S(1)}, f32[8,8192]{1,0:T(8,128)}, u32[]{:S(2)}) copy-start(f32[8,8192]{1,0:T(8,128)} %strip_ref.1) | copy-start | bytes 786436
  5.2 4.7 %collective-permute-start.4 = (bf16[208,1024]{1,0:T(8,128)(2,1)}, bf16[208,1024]{1,0:T(8,128)(2,1)S(1)}, u32[]{:S(2)}, u32[]{:S(2)}) collective-permute-start(bf16[208,1024]{1,0:T(8,128)(2,1)} %get-tuple-element.44), channel_id=1, source_target_pairs={{0,8},{8,0},{16,24},{24,16},{32,40},{40,32},{48,56},{56,48},{64,72... | collective-permute-start | bytes 1277960 | tf_op jit(solution)/shard_map/ppermute | solution.py:448
  5.9 16.2 %collective-permute-start.7 = (bf16[208,1024]{1,0:T(8,128)(2,1)}, bf16[208,1024]{1,0:T(8,128)(2,1)S(1)}, u32[]{:S(2)}, u32[]{:S(2)}) collective-permute-start(bf16[208,1024]{1,0:T(8,128)(2,1)} %get-tuple-element.52), channel_id=1, source_target_pairs={{8,16},{16,8},{24,32},{32,24},{40,48},{48,40},{56,64},{64,56},{72,... | collective-permute-start | bytes 1277960 | tf_op jit(solution)/shard_map/ppermute | solution.py:448
  12.8 17.8 %all-to-all-start = ((f32[8,8,1024]{2,1,0:T(8,128)}), f32[8,8,1024]{2,1,0:T(8,128)S(1)}, u32[]{:S(2)}, u32[]{:S(2)}) async-start(f32[8,8,1024]{2,1,0:T(8,128)} %filter_rows.1.after_ref), calls=%async_computation | async-start | bytes 524288 | tf_op jit(solution)/shard_map/all_to_all | solution.py:468
  19.6 15.3 %copy-start.5 = (bf16[608,128]{1,0:T(8,128)(2,1)S(1)}, bf16[608,128]{1,0:T(8,128)(2,1)}, u32[]{:S(2)}) copy-start(bf16[608,128]{1,0:T(8,128)(2,1)} %get-tuple-element.50.refs_2_.far_ref.far_west_ref) | copy-start | bytes 466948
  19.6 15.3 %copy-start.7 = (bf16[608,128]{1,0:T(8,128)(2,1)S(1)}, bf16[608,128]{1,0:T(8,128)(2,1)}, u32[]{:S(2)}) copy-start(bf16[608,128]{1,0:T(8,128)(2,1)} %get-tuple-element.51.refs_3_.far_east_ref) | copy-start | bytes 466948
  22.2 16.9 %collective-permute-start.8 = (bf16[672,128]{1,0:T(8,128)(2,1)S(1)}, bf16[672,128]{1,0:T(8,128)(2,1)S(1)}, u32[]{:S(2)}, u32[]{:S(2)}) collective-permute-start(bf16[672,128]{1,0:T(8,128)(2,1)S(1)} %get-tuple-element.55), channel_id=1, source_target_pairs={{0,1},{1,2},{2,3},{3,4},{4,5},{5,6},{6,7},{8,9},{9,10},{10,11},{11... | collective-permute-start | bytes 516104 | tf_op jit(solution)/shard_map/ppermute | solution.py:436
  25.9 13.2 %collective-permute-start.9 = (bf16[672,128]{1,0:T(8,128)(2,1)S(1)}, bf16[672,128]{1,0:T(8,128)(2,1)S(1)}, u32[]{:S(2)}, u32[]{:S(2)}) collective-permute-start(bf16[672,128]{1,0:T(8,128)(2,1)S(1)} %get-tuple-element.56), channel_id=1, source_target_pairs={{1,0},{2,1},{3,2},{4,3},{5,4},{6,5},{7,6},{9,8},{10,9},{11,10},{12... | collective-permute-start | bytes 516104 | tf_op jit(solution)/shard_map/ppermute | solution.py:441
  30.7 4.2 %copy-start.10 = (f32[8,1024]{1,0:T(8,128)}, f32[8,1024]{1,0:T(8,128)S(1)}, u32[]{:S(2)}) copy-start(f32[8,1024]{1,0:T(8,128)S(1)} %get-tuple-element.74.refs_0_) | copy-start | bytes 98308
  30.7 4.2 %copy-start.11 = (f32[8,1024]{1,0:T(8,128)}, f32[8,1024]{1,0:T(8,128)S(1)}, u32[]{:S(2)}) copy-start(f32[8,1024]{1,0:T(8,128)S(1)} %get-tuple-element.73.refs_1_) | copy-start | bytes 98308
  30.7 8.4 %collective-permute-start.6 = (f32[8,1024]{1,0:T(8,128)S(1)}, f32[8,1024]{1,0:T(8,128)S(1)}, u32[]{:S(2)}, u32[]{:S(2)}) collective-permute-start(f32[8,1024]{1,0:T(8,128)S(1)} %get-tuple-element.73.refs_1_), channel_id=1, source_target_pairs={{8,16},{16,8},{24,32},{32,24},{40,48},{48,40},{56,64},{64,56},{72,... | collective-permute-start | bytes 98312 | tf_op jit(solution)/shard_map/ppermute | solution.py:448
  34.8 4.4 %collective-permute-start.5 = (f32[8,1024]{1,0:T(8,128)S(1)}, f32[8,1024]{1,0:T(8,128)S(1)}, u32[]{:S(2)}, u32[]{:S(2)}) collective-permute-start(f32[8,1024]{1,0:T(8,128)S(1)} %get-tuple-element.74.refs_0_), channel_id=1, source_target_pairs={{0,8},{8,0},{16,24},{24,16},{32,40},{40,32},{48,56},{56,48},{64,72... | collective-permute-start | bytes 98312 | tf_op jit(solution)/shard_map/ppermute | solution.py:448
  34.9 4.3 %copy-start.1 = (s32[64,2]{0,1:T(2,128)S(1)}, s32[64,2]{0,1:T(2,128)}, u32[]{:S(2)}) copy-start(s32[64,2]{0,1:T(2,128)} %param.11) | copy-start | bytes 1540
  34.9 4.3 %copy-start.3 = (f32[15]{0:T(128)S(1)}, f32[15]{0:T(128)}, u32[]{:S(2)}) copy-start(f32[15]{0:T(128)} %taps_ref.3) | copy-start | bytes 184
  34.9 4.2 %copy-start.8 = (bf16[304,1024]{1,0:T(8,128)(2,1)S(1)}, bf16[304,1024]{1,0:T(8,128)(2,1)}, u32[]{:S(2)}) copy-start(bf16[304,1024]{1,0:T(8,128)(2,1)} %get-tuple-element.57.far_a_ref) | copy-start | bytes 1867780
  35.0 4.2 %copy-start.9 = (bf16[304,1024]{1,0:T(8,128)(2,1)S(1)}, bf16[304,1024]{1,0:T(8,128)(2,1)}, u32[]{:S(2)}) copy-start(bf16[304,1024]{1,0:T(8,128)(2,1)} %get-tuple-element.58.far_b_ref) | copy-start | bytes 1867780

commit v5 on v4

--- a/solution.py
+++ b/solution.py
@@ -253,7 +253,7 @@
     near, far = (SOME_ROWS, width), (ALL_ROWS - SOME_ROWS, width)
     return pl.pallas_call(
         pool_outer_kernel,
-        out_shape=[jax.ShapeDtypeStruct(near, bf16)] * 2
+        out_shape=[pltpu.VMEM(near, bf16)] * 2
         + [pltpu.HBM(far, bf16)] * 2
         + [pltpu.HBM((2 * far[0], LANES), bf16)] * 2
         + [jax.ShapeDtypeStruct((1,), jnp.int32)],

time: 48 us -> 47.6 us (level)
  Pallas kernels: 23.1 us -> 22.6 us
    ppermute x1, starting transfers between devices: 3.69 us -> 3.18 us  [pass_on(): return lax.ppermute(value, axis, [(i, i + 1) for i in range(count - 1)])]
where the time goes in v5:
time: 47.6 us; the launch traced here: 47.2 us
  starting transfers between devices  23.5 us (49%)
  Pallas kernels  22.6 us (47%)
  loops' own time  0.68 us (1%)
    ppermute x4, starting transfers between devices, trade(): return lax.ppermute(value, axis, pairs)  9.16 us
    pallas_call x1, Pallas kernels, merge(): pl.pallas_call(merge_kernel, grid=(planes // SLAB,), out_shape=jax.ShapeD...  8.3 us
    all_to_all x1, starting transfers between devices, on_device(): lax.all_to_all(pieces, 'cols', split_axis=0, concat_axis=0, tiled=True)  6.21 us
    ppermute x1, starting transfers between devices, pass_back(): return lax.ppermute(value, axis, [(i + 1, i) for i in range(count - 1)])  4.97 us
    pallas_call x1, Pallas kernels, pool_outer(): pl.pallas_call(pool_outer_kernel, out_shape=[pltpu.VMEM(near, bf16)] * 2...  4.73 us
    pallas_call x1, Pallas kernels, pool_all(): pl.pallas_call(pool_all_kernel, out_shape=pltpu.VMEM(merit.shape, bf16),...  4.16 us
    ppermute x1, starting transfers between devices, pass_on(): return lax.ppermute(value, axis, [(i, i + 1) for i in range(count - 1)])  3.18 us
    pallas_call x1, Pallas kernels, filter_rows(): pl.pallas_call(filter_rows_kernel, out_shape=jax.ShapeDtypeStruct((pieces...  2.91 us
  transfers between devices with their start and end apart: 7, of which 0 were waited for; matrix products, arithmetic and copies ran while one was open for 0% of the time, Pallas kernels for 20%

profile of v5, /device:TPU:7, one launch (start us, length us, event | category | flops | bytes accessed | tf_op | source)
XLA Modules:
  0.0 47.2 jit_solution(13298820318961622665)
XLA Ops:
  0.0 0.0 copy-start.2
  0.0 0.0 copy-start
  0.0 4.7 %pool_outer.1 = (bf16[208,1024]{1,0:T(8,128)(2,1)S(1)}, bf16[208,1024]{1,0:T(8,128)(2,1)S(1)}, bf16[304,1024]{1,0:T(8,128)(2,1)}, bf16[304,1024]{1,0:T(8,128)(2,...) custom-call(s32[2,64]{1,0:T(2,128)} %bitcast.8, bf16[64,64,1024]{2,1,0:T(8,128)(2,1)} %merit_ref.5), custom_call_target="tpu_custom_call" | custom-call | flops 8388608 | bytes 4194304 | tf_op jit(solution)/shard_map/pool_outer/pallas_call | solution.py:254
  4.7 0.8 %collective-permute-start.4 = (bf16[208,1024]{1,0:T(8,128)(2,1)S(1)}, bf16[208,1024]{1,0:T(8,128)(2,1)S(1)}, u32[]{:S(2)}, u32[]{:S(2)}) collective-permute-start(bf16[208,1024]{1,0:T(8,128)(2,1)S(1)} %get-tuple-element.44), channel_id=1, source_target_pairs={{0,8},{8,0},{16,24},{24,16},{32,40},{40,32},{48,56},{56,48},{64,72... | collective-permute-start | bytes 1277960 | tf_op jit(solution)/shard_map/ppermute | solution.py:448
  5.5 3.9 %collective-permute-start.7 = (bf16[208,1024]{1,0:T(8,128)(2,1)S(1)}, bf16[208,1024]{1,0:T(8,128)(2,1)S(1)}, u32[]{:S(2)}, u32[]{:S(2)}) collective-permute-start(bf16[208,1024]{1,0:T(8,128)(2,1)S(1)} %get-tuple-element.52), channel_id=1, source_target_pairs={{8,16},{16,8},{24,32},{32,24},{40,48},{48,40},{56,64},{64,56},{72,... | collective-permute-start | bytes 1277960 | tf_op jit(solution)/shard_map/ppermute | solution.py:448
  9.5 0.0 collective-permute-done.4.after_ref.a_ref.near_a_ref
  9.5 0.0 copy-done.2
  9.5 0.0 copy-done
  9.5 2.9 %filter_rows.1.after_ref = f32[8,8,1024]{2,1,0:T(8,128)} custom-call(f32[15]{0:T(128)S(1)} %copy-done.2, f32[8,8192]{1,0:T(8,128)S(1)} %copy-done, bf16[208,1024]{1,0:T(8,128)(2,1)S(1)} %collective-permute-done.4.after_ref.a_ref.near_a_ref), custom_call_target="tpu_custom_call" | custom-call | flops 1000 | bytes 1000 | tf_op jit(solution)/shard_map/filter_rows/pallas_call | solution.py:55
  12.4 6.2 %all-to-all-start = ((f32[8,8,1024]{2,1,0:T(8,128)}), f32[8,8,1024]{2,1,0:T(8,128)S(1)}, u32[]{:S(2)}, u32[]{:S(2)}) async-start(f32[8,8,1024]{2,1,0:T(8,128)} %filter_rows.1.after_ref), calls=%async_computation | async-start | bytes 524288 | tf_op jit(solution)/shard_map/all_to_all | solution.py:468
  18.6 0.7 %while.16 = (s32[]{:T(128)}, bf16[304,1024]{1,0:T(8,128)(2,1)}, bf16[304,1024]{1,0:T(8,128)(2,1)}, bf16[608,128]{1,0:T(8,128)(2,1)}, bf16[608,128]{1,0:T(8,128)(2,1)}, /*index=5*/s32[]{:T(128)}) while((s32[]{:T(128)}, bf16[304,1024]{1,0:T(8,128)(2,1)}, bf16[304,1024]{1,0:T(8,128)(2,1)}, bf16[608,128]{1,0:T(8,128)(2,1)}, ...), condition=%wide.region_1.0_spmd, body=%wide.region_0.0_spmd.sunk | while | flops 622594 | bytes 11206941 | solution.py:469
  19.3 0.0 copy-start.5
  19.3 0.0 copy-start.7
  19.3 2.5 %pool_sides.1 = (bf16[4,64,128]{2,1,0:T(8,128)(2,1)S(1)}, bf16[4,64,128]{2,1,0:T(8,128)(2,1)S(1)}) custom-call(bf16[64,64,1024]{2,1,0:T(8,128)(2,1)} %merit_ref.5, f32[8,8,1024]{2,1,0:T(8,128)} %filter_rows.1.after_ref, bf16[608,128]{1,0:T(8,128)(2,1)} %get-tuple-element.50.refs_2_.far_ref.far_west_ref), custom_call_target="tpu_custom_call" | custom-call | flops 1000 | bytes 1000 | tf_op jit(solution)/shard_map/pool_sides/pallas_call | solution.py:238
  21.8 0.0 collective-permute-done.7.b_ref.near_b_ref
  21.8 0.1 join.1
  21.9 3.2 %collective-permute-start.8 = (bf16[672,128]{1,0:T(8,128)(2,1)S(1)}, bf16[672,128]{1,0:T(8,128)(2,1)S(1)}, u32[]{:S(2)}, u32[]{:S(2)}) collective-permute-start(bf16[672,128]{1,0:T(8,128)(2,1)S(1)} %get-tuple-element.55), channel_id=1, source_target_pairs={{0,1},{1,2},{2,3},{3,4},{4,5},{5,6},{6,7},{8,9},{9,10},{10,11},{11... | collective-permute-start | bytes 516104 | tf_op jit(solution)/shard_map/ppermute | solution.py:436
  25.1 5.0 %collective-permute-start.9 = (bf16[672,128]{1,0:T(8,128)(2,1)S(1)}, bf16[672,128]{1,0:T(8,128)(2,1)S(1)}, u32[]{:S(2)}, u32[]{:S(2)}) collective-permute-start(bf16[672,128]{1,0:T(8,128)(2,1)S(1)} %get-tuple-element.56), channel_id=1, source_target_pairs={{1,0},{2,1},{3,2},{4,3},{5,4},{6,5},{7,6},{9,8},{10,9},{11,10},{12... | collective-permute-start | bytes 516104 | tf_op jit(solution)/shard_map/ppermute | solution.py:441
  30.0 0.0 all-to-all-done
  30.1 0.0 copy-start.10
  30.1 0.0 copy-start.11
  30.1 4.4 %collective-permute-start.6 = (f32[8,1024]{1,0:T(8,128)S(1)}, f32[8,1024]{1,0:T(8,128)S(1)}, u32[]{:S(2)}, u32[]{:S(2)}) collective-permute-start(f32[8,1024]{1,0:T(8,128)S(1)} %get-tuple-element.73.refs_1_), channel_id=1, source_target_pairs={{8,16},{16,8},{24,32},{32,24},{40,48},{48,40},{56,64},{64,56},{72,... | collective-permute-start | bytes 98312 | tf_op jit(solution)/shard_map/ppermute | solution.py:448
  34.5 0.1 collective-permute-start.5
  34.6 0.0 copy-done.10
  34.6 0.0 copy-done.11
  34.6 0.0 copy-done.5
  34.6 0.0 copy-done.7
  34.6 0.0 copy-start.1
  34.6 0.0 copy-start.3
  34.6 0.0 copy-start.8
  34.6 0.0 copy-start.9
  34.7 4.2 %pool_all.1.pooled_ref = bf16[64,64,1024]{2,1,0:T(8,128)(2,1)S(1)} custom-call(bf16[64,64,1024]{2,1,0:T(8,128)(2,1)} %merit_ref.5, f32[8,1024]{1,0:T(8,128)} %copy-done.10, f32[8,1024]{1,0:T(8,128)} %copy-done.11, bf16[608,128]{1,0:T(8,128)(2,1)S(1)} %copy-done.5, bf16[608,128]{1,0:T(8,128)(2,1)S(1)} %copy-done.7), custom_call_target="tpu_custom_call" | custom-call | flops 8388608 | bytes 4194304 | tf_op jit(solution)/shard_map/pool_all/pallas_call | solution.py:222
  38.8 0.0 collective-permute-done.8.west_ref
  38.8 0.0 collective-permute-done.9.east_ref
  38.8 0.0 collective-permute-done.6.seam_b_ref
  38.9 0.0 collective-permute-done.5.seam_a_ref
  38.9 0.0 copy-done.1
  38.9 0.0 copy-done.3
  38.9 0.0 copy-done.8
  38.9 0.0 copy-done.9
  38.9 8.3 %merge.1 = bf16[64,64,1024]{2,1,0:T(8,128)(2,1)} custom-call(s32[2,64]{1,0:T(2,128)S(1)} %bitcast.9, f32[15]{0:T(128)S(1)} %copy-done.3, bf16[64,64,1024]{2,1,0:T(8,128)(2,1)S(1)} %pool_all.1.pooled_ref, f32[64,1024]{1,0:T(8,128)S(1)} %bitcast.7, f32[8,1024]{1,0:T(8,128)S(1)} %collective-permute-done.5.seam_a_ref, ...), custom_call_target="tpu_custom_call" | custom-call | tf_op jit(solution)/shard_map/merge/pallas_call | solution.py:412
  (1 shorter events, 0.0 us)
Async XLA Ops:
  0.0 9.5 %copy-start.2 = (f32[15]{0:T(128)S(1)}, f32[15]{0:T(128)}, u32[]{:S(2)}) copy-start(f32[15]{0:T(128)} %taps_ref.2) | copy-start | bytes 184
  0.0 9.5 %copy-start = (f32[8,8192]{1,0:T(8,128)S(1)}, f32[8,8192]{1,0:T(8,128)}, u32[]{:S(2)}) copy-start(f32[8,8192]{1,0:T(8,128)} %strip_ref.1) | copy-start | bytes 786436
  4.7 4.7 %collective-permute-start.4 = (bf16[208,1024]{1,0:T(8,128)(2,1)S(1)}, bf16[208,1024]{1,0:T(8,128)(2,1)S(1)}, u32[]{:S(2)}, u32[]{:S(2)}) collective-permute-start(bf16[208,1024]{1,0:T(8,128)(2,1)S(1)} %get-tuple-element.44), channel_id=1, source_target_pairs={{0,8},{8,0},{16,24},{24,16},{32,40},{40,32},{48,56},{56,48},{64,72... | collective-permute-start | bytes 1277960 | tf_op jit(solution)/shard_map/ppermute | solution.py:448
  5.5 16.3 %collective-permute-start.7 = (bf16[208,1024]{1,0:T(8,128)(2,1)S(1)}, bf16[208,1024]{1,0:T(8,128)(2,1)S(1)}, u32[]{:S(2)}, u32[]{:S(2)}) collective-permute-start(bf16[208,1024]{1,0:T(8,128)(2,1)S(1)} %get-tuple-element.52), channel_id=1, source_target_pairs={{8,16},{16,8},{24,32},{32,24},{40,48},{48,40},{56,64},{64,56},{72,... | collective-permute-start | bytes 1277960 | tf_op jit(solution)/shard_map/ppermute | solution.py:448
  12.4 17.6 %all-to-all-start = ((f32[8,8,1024]{2,1,0:T(8,128)}), f32[8,8,1024]{2,1,0:T(8,128)S(1)}, u32[]{:S(2)}, u32[]{:S(2)}) async-start(f32[8,8,1024]{2,1,0:T(8,128)} %filter_rows.1.after_ref), calls=%async_computation | async-start | bytes 524288 | tf_op jit(solution)/shard_map/all_to_all | solution.py:468
  19.3 15.3 %copy-start.5 = (bf16[608,128]{1,0:T(8,128)(2,1)S(1)}, bf16[608,128]{1,0:T(8,128)(2,1)}, u32[]{:S(2)}) copy-start(bf16[608,128]{1,0:T(8,128)(2,1)} %get-tuple-element.50.refs_2_.far_ref.far_west_ref) | copy-start | bytes 466948
  19.3 15.3 %copy-start.7 = (bf16[608,128]{1,0:T(8,128)(2,1)S(1)}, bf16[608,128]{1,0:T(8,128)(2,1)}, u32[]{:S(2)}) copy-start(bf16[608,128]{1,0:T(8,128)(2,1)} %get-tuple-element.51.refs_3_.far_east_ref) | copy-start | bytes 466948
  21.9 16.9 %collective-permute-start.8 = (bf16[672,128]{1,0:T(8,128)(2,1)S(1)}, bf16[672,128]{1,0:T(8,128)(2,1)S(1)}, u32[]{:S(2)}, u32[]{:S(2)}) collective-permute-start(bf16[672,128]{1,0:T(8,128)(2,1)S(1)} %get-tuple-element.55), channel_id=1, source_target_pairs={{0,1},{1,2},{2,3},{3,4},{4,5},{5,6},{6,7},{8,9},{9,10},{10,11},{11... | collective-permute-start | bytes 516104 | tf_op jit(solution)/shard_map/ppermute | solution.py:436
  25.1 13.8 %collective-permute-start.9 = (bf16[672,128]{1,0:T(8,128)(2,1)S(1)}, bf16[672,128]{1,0:T(8,128)(2,1)S(1)}, u32[]{:S(2)}, u32[]{:S(2)}) collective-permute-start(bf16[672,128]{1,0:T(8,128)(2,1)S(1)} %get-tuple-element.56), channel_id=1, source_target_pairs={{1,0},{2,1},{3,2},{4,3},{5,4},{6,5},{7,6},{9,8},{10,9},{11,10},{12... | collective-permute-start | bytes 516104 | tf_op jit(solution)/shard_map/ppermute | solution.py:441
  30.1 4.5 %copy-start.10 = (f32[8,1024]{1,0:T(8,128)}, f32[8,1024]{1,0:T(8,128)S(1)}, u32[]{:S(2)}) copy-start(f32[8,1024]{1,0:T(8,128)S(1)} %get-tuple-element.74.refs_0_) | copy-start | bytes 98308
  30.1 4.5 %copy-start.11 = (f32[8,1024]{1,0:T(8,128)}, f32[8,1024]{1,0:T(8,128)S(1)}, u32[]{:S(2)}) copy-start(f32[8,1024]{1,0:T(8,128)S(1)} %get-tuple-element.73.refs_1_) | copy-start | bytes 98308
  30.1 8.7 %collective-permute-start.6 = (f32[8,1024]{1,0:T(8,128)S(1)}, f32[8,1024]{1,0:T(8,128)S(1)}, u32[]{:S(2)}, u32[]{:S(2)}) collective-permute-start(f32[8,1024]{1,0:T(8,128)S(1)} %get-tuple-element.73.refs_1_), channel_id=1, source_target_pairs={{8,16},{16,8},{24,32},{32,24},{40,48},{48,40},{56,64},{64,56},{72,... | collective-permute-start | bytes 98312 | tf_op jit(solution)/shard_map/ppermute | solution.py:448
  34.5 4.4 %collective-permute-start.5 = (f32[8,1024]{1,0:T(8,128)S(1)}, f32[8,1024]{1,0:T(8,128)S(1)}, u32[]{:S(2)}, u32[]{:S(2)}) collective-permute-start(f32[8,1024]{1,0:T(8,128)S(1)} %get-tuple-element.74.refs_0_), channel_id=1, source_target_pairs={{0,8},{8,0},{16,24},{24,16},{32,40},{40,32},{48,56},{56,48},{64,72... | collective-permute-start | bytes 98312 | tf_op jit(solution)/shard_map/ppermute | solution.py:448
  34.6 4.3 %copy-start.1 = (s32[64,2]{0,1:T(2,128)S(1)}, s32[64,2]{0,1:T(2,128)}, u32[]{:S(2)}) copy-start(s32[64,2]{0,1:T(2,128)} %param.11) | copy-start | bytes 1540
  34.6 4.3 %copy-start.3 = (f32[15]{0:T(128)S(1)}, f32[15]{0:T(128)}, u32[]{:S(2)}) copy-start(f32[15]{0:T(128)} %taps_ref.3) | copy-start | bytes 184
  34.6 4.2 %copy-start.8 = (bf16[304,1024]{1,0:T(8,128)(2,1)S(1)}, bf16[304,1024]{1,0:T(8,128)(2,1)}, u32[]{:S(2)}) copy-start(bf16[304,1024]{1,0:T(8,128)(2,1)} %get-tuple-element.57.far_a_ref) | copy-start | bytes 1867780
  34.6 4.2 %copy-start.9 = (bf16[304,1024]{1,0:T(8,128)(2,1)S(1)}, bf16[304,1024]{1,0:T(8,128)(2,1)}, u32[]{:S(2)}) copy-start(bf16[304,1024]{1,0:T(8,128)(2,1)} %get-tuple-element.58.far_b_ref) | copy-start | bytes 1867780

commit v6 on v5

--- a/solution.py
+++ b/solution.py
@@ -34,7 +34,7 @@
     return pl.BlockSpec(memory_space=pltpu.SMEM)
 
 
-def filter_rows_kernel(taps_ref, strip_ref, after_ref, out_ref, pad_ref):
+def filter_rows_kernel(taps_ref, strip_ref, after_ref, out_ref, pad_ref, done_ref, sems):
     del after_ref
     half = taps_ref.shape[0] // 2
     height, width = strip_ref.shape
@@ -42,12 +42,17 @@
     pad_ref[:, LANES + width :] = jnp.zeros((height, LANES), f32)
     pad_ref[:, LANES : LANES + width] = strip_ref[...]
     count, _, span = out_ref.shape
+    copies = []
     for piece in range(count):
         start = LANES + piece * span
         total = jnp.zeros((height, span), f32)
         for j in range(taps_ref.shape[0]):
             total = total + taps_ref[j] * pad_ref[:, start + j - half : start + j - half + span]
-        out_ref[piece] = total
+        done_ref[piece] = total
+        copies.append(pltpu.make_async_copy(done_ref.at[piece], out_ref.at[piece], sems.at[piece]))
+        copies[-1].start()
+    for copy in copies:
+        copy.wait()
 
 
 def filter_rows(strip, taps_row, pieces, after):
@@ -56,8 +61,12 @@
         filter_rows_kernel,
         out_shape=jax.ShapeDtypeStruct((pieces, height, width // pieces), f32),
         in_specs=[smem(), pl.BlockSpec(memory_space=pltpu.VMEM), pl.BlockSpec(memory_space=pl.ANY)],
-        out_specs=pl.BlockSpec(memory_space=pltpu.VMEM),
-        scratch_shapes=[pltpu.VMEM((height, width + 2 * LANES), f32)],
+        out_specs=pl.BlockSpec(memory_space=pl.ANY),
+        scratch_shapes=[
+            pltpu.VMEM((height, width + 2 * LANES), f32),
+            pltpu.VMEM((pieces, height, width // pieces), f32),
+            pltpu.SemaphoreType.DMA((pieces,)),
+        ],
         cost_estimate=brief(),
         compiler_params=params(16 * 2**20),
         name="filter_rows",
@@ -467,6 +476,7 @@
     pieces = filter_rows(frame, taps_row, frame.shape[1] // width, a)
     tile = lax.all_to_all(pieces, "cols", split_axis=0, concat_axis=0, tiled=True).reshape(height, width)
     _, *fars = lax.while_loop(lambda state: state[0] > 0, far_exchange, (more.reshape(()), *fars))
+    fars = [pltpu.with_memory_space_constraint(x, pltpu.HBM) for x in fars]
     right, left = pool_sides(merit, pieces, fars[2])
     last, first = join(right, left, a, b)
     west, east = pass_on(last, "cols"), pass_back(first, "cols")

time: 47.6 us -> 47.4 us (level)
  no operation moved by 1% of the time
where the time goes in v6:
time: 47.4 us; the launch traced here: 47 us
  starting transfers between devices  23.5 us (50%)
  Pallas kernels  22.5 us (47%)
  loops' own time  0.67 us (1%)
    ppermute x4, starting transfers between devices, trade(): return lax.ppermute(value, axis, pairs)  9.1 us
    pallas_call x1, Pallas kernels, merge(): pl.pallas_call(merge_kernel, grid=(planes // SLAB,), out_shape=jax.ShapeD...  8.33 us
    all_to_all x1, starting transfers between devices, on_device(): lax.all_to_all(pieces, 'cols', split_axis=0, concat_axis=0, tiled=True)  6.22 us
    ppermute x1, starting transfers between devices, pass_back(): return lax.ppermute(value, axis, [(i + 1, i) for i in range(count - 1)])  4.98 us
    pallas_call x1, Pallas kernels, pool_outer(): pl.pallas_call(pool_outer_kernel, out_shape=[pltpu.VMEM(near, bf16)] * 2...  4.73 us
    pallas_call x1, Pallas kernels, pool_all(): pl.pallas_call(pool_all_kernel, out_shape=pltpu.VMEM(merit.shape, bf16),...  4.05 us
    ppermute x1, starting transfers between devices, pass_on(): return lax.ppermute(value, axis, [(i, i + 1) for i in range(count - 1)])  3.23 us
    pallas_call x1, Pallas kernels, filter_rows(): pl.pallas_call(filter_rows_kernel, out_shape=jax.ShapeDtypeStruct((pieces...  2.9 us
  transfers between devices with their start and end apart: 7, of which 0 were waited for; matrix products, arithmetic and copies ran while one was open for 0% of the time, Pallas kernels for 20%

profile of v6, /device:TPU:7, one launch (start us, length us, event | category | flops | bytes accessed | tf_op | source)
XLA Modules:
  0.0 47.0 jit_solution(10390955840404491954)
XLA Ops:
  0.0 0.0 copy-start.2
  0.0 0.0 copy-start
  0.0 4.7 %pool_outer.1 = (bf16[208,1024]{1,0:T(8,128)(2,1)S(1)}, bf16[208,1024]{1,0:T(8,128)(2,1)S(1)}, bf16[304,1024]{1,0:T(8,128)(2,1)}, bf16[304,1024]{1,0:T(8,128)(2,...) custom-call(s32[2,64]{1,0:T(2,128)} %bitcast.8, bf16[64,64,1024]{2,1,0:T(8,128)(2,1)} %merit_ref.5), custom_call_target="tpu_custom_call" | custom-call | flops 8388608 | bytes 4194304 | tf_op jit(solution)/shard_map/pool_outer/pallas_call | solution.py:263
  4.7 0.8 %collective-permute-start.4 = (bf16[208,1024]{1,0:T(8,128)(2,1)S(1)}, bf16[208,1024]{1,0:T(8,128)(2,1)S(1)}, u32[]{:S(2)}, u32[]{:S(2)}) collective-permute-start(bf16[208,1024]{1,0:T(8,128)(2,1)S(1)} %get-tuple-element.44), channel_id=1, source_target_pairs={{0,8},{8,0},{16,24},{24,16},{32,40},{40,32},{48,56},{56,48},{64,72... | collective-permute-start | bytes 1277960 | tf_op jit(solution)/shard_map/ppermute | solution.py:457
  5.5 3.9 %collective-permute-start.7 = (bf16[208,1024]{1,0:T(8,128)(2,1)S(1)}, bf16[208,1024]{1,0:T(8,128)(2,1)S(1)}, u32[]{:S(2)}, u32[]{:S(2)}) collective-permute-start(bf16[208,1024]{1,0:T(8,128)(2,1)S(1)} %get-tuple-element.52), channel_id=1, source_target_pairs={{8,16},{16,8},{24,32},{32,24},{40,48},{48,40},{56,64},{64,56},{72,... | collective-permute-start | bytes 1277960 | tf_op jit(solution)/shard_map/ppermute | solution.py:457
  9.5 0.0 collective-permute-done.4.after_ref.a_ref.near_a_ref
  9.5 0.0 copy-done.2
  9.5 0.0 copy-done
  9.5 2.9 %filter_rows.1.after_ref = f32[8,8,1024]{2,1,0:T(8,128)} custom-call(f32[15]{0:T(128)S(1)} %copy-done.2, f32[8,8192]{1,0:T(8,128)S(1)} %copy-done, bf16[208,1024]{1,0:T(8,128)(2,1)S(1)} %collective-permute-done.4.after_ref.a_ref.near_a_ref), custom_call_target="tpu_custom_call" | custom-call | flops 1000 | bytes 1000 | tf_op jit(solution)/shard_map/filter_rows/pallas_call | solution.py:60
  12.4 6.2 %all-to-all-start = ((f32[8,8,1024]{2,1,0:T(8,128)}), f32[8,8,1024]{2,1,0:T(8,128)S(1)}, u32[]{:S(2)}, u32[]{:S(2)}) async-start(f32[8,8,1024]{2,1,0:T(8,128)} %filter_rows.1.after_ref), calls=%async_computation | async-start | bytes 524288 | tf_op jit(solution)/shard_map/all_to_all | solution.py:477
  18.6 0.7 %while.16 = (s32[]{:T(128)}, bf16[304,1024]{1,0:T(8,128)(2,1)}, bf16[304,1024]{1,0:T(8,128)(2,1)}, bf16[608,128]{1,0:T(8,128)(2,1)}, bf16[608,128]{1,0:T(8,128)(2,1)}, /*index=5*/s32[]{:T(128)}) while((s32[]{:T(128)}, bf16[304,1024]{1,0:T(8,128)(2,1)}, bf16[304,1024]{1,0:T(8,128)(2,1)}, bf16[608,128]{1,0:T(8,128)(2,1)}, ...), condition=%wide.region_1.0_spmd, body=%wide.region_0.0_spmd.sunk | while | flops 622594 | bytes 11206941 | solution.py:478
  19.3 2.4 %pool_sides.1 = (bf16[4,64,128]{2,1,0:T(8,128)(2,1)S(1)}, bf16[4,64,128]{2,1,0:T(8,128)(2,1)S(1)}) custom-call(bf16[64,64,1024]{2,1,0:T(8,128)(2,1)} %merit_ref.5, f32[8,8,1024]{2,1,0:T(8,128)} %filter_rows.1.after_ref, bf16[608,128]{1,0:T(8,128)(2,1)} %get-tuple-element.50.refs_2_.far_ref.far_west_ref), custom_call_target="tpu_custom_call" | custom-call | flops 1000 | bytes 1000 | tf_op jit(solution)/shard_map/pool_sides/pallas_call | solution.py:247
  21.8 0.0 collective-permute-done.7.b_ref.near_b_ref
  21.8 0.1 join.1
  21.8 3.2 %collective-permute-start.8 = (bf16[672,128]{1,0:T(8,128)(2,1)S(1)}, bf16[672,128]{1,0:T(8,128)(2,1)S(1)}, u32[]{:S(2)}, u32[]{:S(2)}) collective-permute-start(bf16[672,128]{1,0:T(8,128)(2,1)S(1)} %get-tuple-element.55), channel_id=1, source_target_pairs={{0,1},{1,2},{2,3},{3,4},{4,5},{5,6},{6,7},{8,9},{9,10},{10,11},{11... | collective-permute-start | bytes 516104 | tf_op jit(solution)/shard_map/ppermute | solution.py:445
  25.1 5.0 %collective-permute-start.9 = (bf16[672,128]{1,0:T(8,128)(2,1)S(1)}, bf16[672,128]{1,0:T(8,128)(2,1)S(1)}, u32[]{:S(2)}, u32[]{:S(2)}) collective-permute-start(bf16[672,128]{1,0:T(8,128)(2,1)S(1)} %get-tuple-element.56), channel_id=1, source_target_pairs={{1,0},{2,1},{3,2},{4,3},{5,4},{6,5},{7,6},{9,8},{10,9},{11,10},{12... | collective-permute-start | bytes 516104 | tf_op jit(solution)/shard_map/ppermute | solution.py:450
  30.1 0.0 all-to-all-done
  30.1 0.0 copy-start.6
  30.1 0.0 copy-start.7
  30.1 4.3 %collective-permute-start.6 = (f32[8,1024]{1,0:T(8,128)S(1)}, f32[8,1024]{1,0:T(8,128)S(1)}, u32[]{:S(2)}, u32[]{:S(2)}) collective-permute-start(f32[8,1024]{1,0:T(8,128)S(1)} %get-tuple-element.73.refs_1_), channel_id=1, source_target_pairs={{8,16},{16,8},{24,32},{32,24},{40,48},{48,40},{56,64},{64,56},{72,... | collective-permute-start | bytes 98312 | tf_op jit(solution)/shard_map/ppermute | solution.py:457
  34.4 0.1 collective-permute-start.5
  34.5 0.0 copy-done.6
  34.5 0.0 copy-done.7
  34.5 0.0 copy-start.1
  34.5 0.0 copy-start.3
  34.6 4.1 %pool_all.1.pooled_ref = bf16[64,64,1024]{2,1,0:T(8,128)(2,1)S(1)} custom-call(bf16[64,64,1024]{2,1,0:T(8,128)(2,1)} %merit_ref.5, f32[8,1024]{1,0:T(8,128)} %copy-done.6, f32[8,1024]{1,0:T(8,128)} %copy-done.7, bf16[608,128]{1,0:T(8,128)(2,1)} %get-tuple-element.50.refs_2_.far_ref.far_west_ref, bf16[608,128]{1,0:T(8,128)(2,1)} %get-tuple-element.51.refs_3_.far_east_ref), custom_call_target="tpu_custom_call" | custom-call | flops 8388608 | bytes 4194304 | tf_op jit(solution)/shard_map/pool_all/pallas_call | solution.py:231
  38.6 0.0 collective-permute-done.8.west_ref
  38.6 0.0 collective-permute-done.9.east_ref
  38.6 0.0 collective-permute-done.6.seam_b_ref
  38.7 0.0 collective-permute-done.5.seam_a_ref
  38.7 0.0 copy-done.1
  38.7 0.0 copy-done.3
  38.7 8.3 %merge.1 = bf16[64,64,1024]{2,1,0:T(8,128)(2,1)} custom-call(s32[2,64]{1,0:T(2,128)S(1)} %bitcast.9, f32[15]{0:T(128)S(1)} %copy-done.3, bf16[64,64,1024]{2,1,0:T(8,128)(2,1)S(1)} %pool_all.1.pooled_ref, f32[64,1024]{1,0:T(8,128)S(1)} %bitcast.7, f32[8,1024]{1,0:T(8,128)S(1)} %collective-permute-done.5.seam_a_ref, ...), custom_call_target="tpu_custom_call" | custom-call | tf_op jit(solution)/shard_map/merge/pallas_call | solution.py:421
  (1 shorter events, 0.0 us)
Async XLA Ops:
  0.0 9.5 %copy-start.2 = (f32[15]{0:T(128)S(1)}, f32[15]{0:T(128)}, u32[]{:S(2)}) copy-start(f32[15]{0:T(128)} %taps_ref.2) | copy-start | bytes 184
  0.0 9.5 %copy-start = (f32[8,8192]{1,0:T(8,128)S(1)}, f32[8,8192]{1,0:T(8,128)}, u32[]{:S(2)}) copy-start(f32[8,8192]{1,0:T(8,128)} %strip_ref.1) | copy-start | bytes 786436
  4.7 4.7 %collective-permute-start.4 = (bf16[208,1024]{1,0:T(8,128)(2,1)S(1)}, bf16[208,1024]{1,0:T(8,128)(2,1)S(1)}, u32[]{:S(2)}, u32[]{:S(2)}) collective-permute-start(bf16[208,1024]{1,0:T(8,128)(2,1)S(1)} %get-tuple-element.44), channel_id=1, source_target_pairs={{0,8},{8,0},{16,24},{24,16},{32,40},{40,32},{48,56},{56,48},{64,72... | collective-permute-start | bytes 1277960 | tf_op jit(solution)/shard_map/ppermute | solution.py:457
  5.5 16.3 %collective-permute-start.7 = (bf16[208,1024]{1,0:T(8,128)(2,1)S(1)}, bf16[208,1024]{1,0:T(8,128)(2,1)S(1)}, u32[]{:S(2)}, u32[]{:S(2)}) collective-permute-start(bf16[208,1024]{1,0:T(8,128)(2,1)S(1)} %get-tuple-element.52), channel_id=1, source_target_pairs={{8,16},{16,8},{24,32},{32,24},{40,48},{48,40},{56,64},{64,56},{72,... | collective-permute-start | bytes 1277960 | tf_op jit(solution)/shard_map/ppermute | solution.py:457
  12.4 17.6 %all-to-all-start = ((f32[8,8,1024]{2,1,0:T(8,128)}), f32[8,8,1024]{2,1,0:T(8,128)S(1)}, u32[]{:S(2)}, u32[]{:S(2)}) async-start(f32[8,8,1024]{2,1,0:T(8,128)} %filter_rows.1.after_ref), calls=%async_computation | async-start | bytes 524288 | tf_op jit(solution)/shard_map/all_to_all | solution.py:477
  21.8 16.8 %collective-permute-start.8 = (bf16[672,128]{1,0:T(8,128)(2,1)S(1)}, bf16[672,128]{1,0:T(8,128)(2,1)S(1)}, u32[]{:S(2)}, u32[]{:S(2)}) collective-permute-start(bf16[672,128]{1,0:T(8,128)(2,1)S(1)} %get-tuple-element.55), channel_id=1, source_target_pairs={{0,1},{1,2},{2,3},{3,4},{4,5},{5,6},{6,7},{8,9},{9,10},{10,11},{11... | collective-permute-start | bytes 516104 | tf_op jit(solution)/shard_map/ppermute | solution.py:445
  25.1 13.6 %collective-permute-start.9 = (bf16[672,128]{1,0:T(8,128)(2,1)S(1)}, bf16[672,128]{1,0:T(8,128)(2,1)S(1)}, u32[]{:S(2)}, u32[]{:S(2)}) collective-permute-start(bf16[672,128]{1,0:T(8,128)(2,1)S(1)} %get-tuple-element.56), channel_id=1, source_target_pairs={{1,0},{2,1},{3,2},{4,3},{5,4},{6,5},{7,6},{9,8},{10,9},{11,10},{12... | collective-permute-start | bytes 516104 | tf_op jit(solution)/shard_map/ppermute | solution.py:450
  30.1 4.4 %copy-start.6 = (f32[8,1024]{1,0:T(8,128)}, f32[8,1024]{1,0:T(8,128)S(1)}, u32[]{:S(2)}) copy-start(f32[8,1024]{1,0:T(8,128)S(1)} %get-tuple-element.74.refs_0_) | copy-start | bytes 98308
  30.1 4.4 %copy-start.7 = (f32[8,1024]{1,0:T(8,128)}, f32[8,1024]{1,0:T(8,128)S(1)}, u32[]{:S(2)}) copy-start(f32[8,1024]{1,0:T(8,128)S(1)} %get-tuple-element.73.refs_1_) | copy-start | bytes 98308
  30.1 8.5 %collective-permute-start.6 = (f32[8,1024]{1,0:T(8,128)S(1)}, f32[8,1024]{1,0:T(8,128)S(1)}, u32[]{:S(2)}, u32[]{:S(2)}) collective-permute-start(f32[8,1024]{1,0:T(8,128)S(1)} %get-tuple-element.73.refs_1_), channel_id=1, source_target_pairs={{8,16},{16,8},{24,32},{32,24},{40,48},{48,40},{56,64},{64,56},{72,... | collective-permute-start | bytes 98312 | tf_op jit(solution)/shard_map/ppermute | solution.py:457
  34.4 4.2 %collective-permute-start.5 = (f32[8,1024]{1,0:T(8,128)S(1)}, f32[8,1024]{1,0:T(8,128)S(1)}, u32[]{:S(2)}, u32[]{:S(2)}) collective-permute-start(f32[8,1024]{1,0:T(8,128)S(1)} %get-tuple-element.74.refs_0_), channel_id=1, source_target_pairs={{0,8},{8,0},{16,24},{24,16},{32,40},{40,32},{48,56},{56,48},{64,72... | collective-permute-start | bytes 98312 | tf_op jit(solution)/shard_map/ppermute | solution.py:457
  34.5 4.1 %copy-start.1 = (s32[64,2]{0,1:T(2,128)S(1)}, s32[64,2]{0,1:T(2,128)}, u32[]{:S(2)}) copy-start(s32[64,2]{0,1:T(2,128)} %param.11) | copy-start | bytes 1540
  34.5 4.1 %copy-start.3 = (f32[15]{0:T(128)S(1)}, f32[15]{0:T(128)}, u32[]{:S(2)}) copy-start(f32[15]{0:T(128)} %taps_ref.3) | copy-start | bytes 184

commit v7 on v5

--- a/solution.py
+++ b/solution.py
@@ -273,7 +273,8 @@
     )(offsets, merit)
 
 
-def join_kernel(right_ref, left_ref, a_ref, b_ref, last_ref, first_ref):
+def join_kernel(right_ref, left_ref, a_ref, b_ref, after_ref, last_ref, first_ref):
+    del after_ref
     groups, height, _ = right_ref.shape
     width = a_ref.shape[1]
     for side, out, edge in ((right_ref, last_ref, width - LANES), (left_ref, first_ref, 0)):
@@ -284,18 +285,18 @@
             out[start : start + SOME_ROWS, :] = ref[:, edge : edge + LANES]
 
 
-def join(right, left, a, b):
+def join(right, left, a, b, after):
     groups, height, _ = right.shape
     vmem = pl.BlockSpec(memory_space=pltpu.VMEM)
     return pl.pallas_call(
         join_kernel,
         out_shape=[jax.ShapeDtypeStruct((groups * height + 2 * SOME_ROWS, LANES), bf16)] * 2,
-        in_specs=[vmem] * 4,
+        in_specs=[vmem] * 5,
         out_specs=[vmem] * 2,
         cost_estimate=brief(),
         compiler_params=params(16 * 2**20),
         name="join",
-    )(right, left, a, b)
+    )(right, left, a, b, after)
 
 
 def weighted_rows(taps_ref, column_ref, k, count):
@@ -468,13 +469,13 @@
     tile = lax.all_to_all(pieces, "cols", split_axis=0, concat_axis=0, tiled=True).reshape(height, width)
     _, *fars = lax.while_loop(lambda state: state[0] > 0, far_exchange, (more.reshape(()), *fars))
     right, left = pool_sides(merit, pieces, fars[2])
-    last, first = join(right, left, a, b)
-    west, east = pass_on(last, "cols"), pass_back(first, "cols")
     top, bottom = tile[:MAXV], tile[height - MAXV :]
     odd = lax.axis_index("rows") % 2 == 1
     for_b, for_a = jnp.where(odd, bottom, top), jnp.where(odd, top, bottom)
     seam_b = trade(for_b, "rows", 1)
     seam_a = trade(for_a, "rows", 0)
+    last, first = join(right, left, a, b, for_a)
+    west, east = pass_on(last, "cols"), pass_back(first, "cols")
     pooled = pool_all(merit, (for_a, for_b, fars[2], fars[3]))
     return merge(pooled, tile, (seam_a, seam_b), (a, b), (west, east), fars, turned, taps_col)
 

time: 47.6 us -> 52.1 us (1.095)
  waiting for transfers between devices: 0.02 us -> 3.26 us
  starting transfers between devices: 23.5 us -> 24.8 us
    all_to_all x1, waiting for transfers between devices: 0.01 us -> 3.25 us  [on_device(): lax.all_to_all(pieces, 'cols', split_axis=0, concat_axis=0, tiled=True)]
    ppermute x4, starting transfers between devices: 9.16 us -> 11.2 us  [trade(): return lax.ppermute(value, axis, pairs)]
    ppermute x1, starting transfers between devices: 3.18 us -> 2.49 us  [pass_on(): return lax.ppermute(value, axis, [(i, i + 1) for i in range(count - 1)])]
  transfers between devices with their start and end apart: 7 -> 7, of which waited for: 0 -> 1; matrix products, arithmetic and copies ran while one was open for 0% -> 0% of each run, Pallas kernels for 20% -> 18%
where the time goes in v7:
time: 52.1 us; the launch traced here: 51.8 us
  starting transfers between devices  24.8 us (48%)
  Pallas kernels  22.7 us (44%)
  waiting for transfers between devices  3.26 us (6%)
  loops' own time  0.68 us (1%)
    ppermute x4, starting transfers between devices, trade(): return lax.ppermute(value, axis, pairs)  11.2 us
    pallas_call x1, Pallas kernels, merge(): pl.pallas_call(merge_kernel, grid=(planes // SLAB,), out_shape=jax.ShapeD...  8.33 us
    all_to_all x1, starting transfers between devices, on_device(): lax.all_to_all(pieces, 'cols', split_axis=0, concat_axis=0, tiled=True)  6.21 us
    ppermute x1, starting transfers between devices, pass_back(): return lax.ppermute(value, axis, [(i + 1, i) for i in range(count - 1)])  4.9 us
    pallas_call x1, Pallas kernels, pool_outer(): pl.pallas_call(pool_outer_kernel, out_shape=[pltpu.VMEM(near, bf16)] * 2...  4.74 us
    pallas_call x1, Pallas kernels, pool_all(): pl.pallas_call(pool_all_kernel, out_shape=pltpu.VMEM(merit.shape, bf16),...  4.16 us
    all_to_all x1, waiting for transfers between devices, on_device(): lax.all_to_all(pieces, 'cols', split_axis=0, concat_axis=0, tiled=True)  3.25 us
    pallas_call x1, Pallas kernels, filter_rows(): pl.pallas_call(filter_rows_kernel, out_shape=jax.ShapeDtypeStruct((pieces...  2.91 us
  transfers between devices with their start and end apart: 7, of which 1 were waited for; matrix products, arithmetic and copies ran while one was open for 0% of the time, Pallas kernels for 18%

profile of v7, /device:TPU:7, one launch (start us, length us, event | category | flops | bytes accessed | tf_op | source)
XLA Modules:
  0.0 51.8 jit_solution(16117078419804399228)
XLA Ops:
  0.0 0.0 copy-start.3
  0.0 0.0 copy-start.1
  0.0 4.7 %pool_outer.1 = (bf16[208,1024]{1,0:T(8,128)(2,1)S(1)}, bf16[208,1024]{1,0:T(8,128)(2,1)S(1)}, bf16[304,1024]{1,0:T(8,128)(2,1)}, bf16[304,1024]{1,0:T(8,128)(2,...) custom-call(s32[2,64]{1,0:T(2,128)} %bitcast.8, bf16[64,64,1024]{2,1,0:T(8,128)(2,1)} %merit_ref.5), custom_call_target="tpu_custom_call" | custom-call | flops 8388608 | bytes 4194304 | tf_op jit(solution)/shard_map/pool_outer/pallas_call | solution.py:254
  4.7 0.8 %collective-permute-start.4 = (bf16[208,1024]{1,0:T(8,128)(2,1)S(1)}, bf16[208,1024]{1,0:T(8,128)(2,1)S(1)}, u32[]{:S(2)}, u32[]{:S(2)}) collective-permute-start(bf16[208,1024]{1,0:T(8,128)(2,1)S(1)} %get-tuple-element.44), channel_id=1, source_target_pairs={{0,8},{8,0},{16,24},{24,16},{32,40},{40,32},{48,56},{56,48},{64,72... | collective-permute-start | bytes 1277960 | tf_op jit(solution)/shard_map/ppermute | solution.py:449
  5.5 3.9 %collective-permute-start.7 = (bf16[208,1024]{1,0:T(8,128)(2,1)S(1)}, bf16[208,1024]{1,0:T(8,128)(2,1)S(1)}, u32[]{:S(2)}, u32[]{:S(2)}) collective-permute-start(bf16[208,1024]{1,0:T(8,128)(2,1)S(1)} %get-tuple-element.52), channel_id=1, source_target_pairs={{8,16},{16,8},{24,32},{32,24},{40,48},{48,40},{56,64},{64,56},{72,... | collective-permute-start | bytes 1277960 | tf_op jit(solution)/shard_map/ppermute | solution.py:449
  9.5 0.0 collective-permute-done.4.after_ref.a_ref.near_a_ref
  9.5 0.0 copy-done.3
  9.5 0.0 copy-done.1
  9.5 2.9 %filter_rows.1.after_ref = f32[8,8,1024]{2,1,0:T(8,128)} custom-call(f32[15]{0:T(128)S(1)} %copy-done.3, f32[8,8192]{1,0:T(8,128)S(1)} %copy-done.1, bf16[208,1024]{1,0:T(8,128)(2,1)S(1)} %collective-permute-done.4.after_ref.a_ref.near_a_ref), custom_call_target="tpu_custom_call" | custom-call | flops 1000 | bytes 1000 | tf_op jit(solution)/shard_map/filter_rows/pallas_call | solution.py:55
  12.4 6.2 %all-to-all-start = ((f32[8,8,1024]{2,1,0:T(8,128)}), f32[8,8,1024]{2,1,0:T(8,128)S(1)}, u32[]{:S(2)}, u32[]{:S(2)}) async-start(f32[8,8,1024]{2,1,0:T(8,128)} %filter_rows.1.after_ref), calls=%async_computation | async-start | bytes 524288 | tf_op jit(solution)/shard_map/all_to_all | solution.py:469
  18.6 0.7 %while.16 = (s32[]{:T(128)}, bf16[304,1024]{1,0:T(8,128)(2,1)}, bf16[304,1024]{1,0:T(8,128)(2,1)}, bf16[608,128]{1,0:T(8,128)(2,1)}, bf16[608,128]{1,0:T(8,128)(2,1)}, /*index=5*/s32[]{:T(128)}) while((s32[]{:T(128)}, bf16[304,1024]{1,0:T(8,128)(2,1)}, bf16[304,1024]{1,0:T(8,128)(2,1)}, bf16[608,128]{1,0:T(8,128)(2,1)}, ...), condition=%wide.region_1.0_spmd, body=%wide.region_0.0_spmd.sunk | while | flops 622594 | bytes 11206941 | solution.py:470
  19.3 0.0 copy-start.6
  19.3 0.0 copy-start.8
  19.3 2.5 %pool_sides.1 = (bf16[4,64,128]{2,1,0:T(8,128)(2,1)S(1)}, bf16[4,64,128]{2,1,0:T(8,128)(2,1)S(1)}) custom-call(bf16[64,64,1024]{2,1,0:T(8,128)(2,1)} %merit_ref.5, f32[8,8,1024]{2,1,0:T(8,128)} %filter_rows.1.after_ref, bf16[608,128]{1,0:T(8,128)(2,1)} %get-tuple-element.50.refs_2_.far_ref.far_west_ref), custom_call_target="tpu_custom_call" | custom-call | flops 1000 | bytes 1000 | tf_op jit(solution)/shard_map/pool_sides/pallas_call | solution.py:238
  21.8 3.2 %all-to-all-done = f32[8,8,1024]{2,1,0:T(8,128)S(1)} async-done(((f32[8,8,1024]{2,1,0:T(8,128)}), f32[8,8,1024]{2,1,0:T(8,128)S(1)}, u32[]{:S(2)}, u32[]{:S(2)}) %all-to-all-start) | async-done | bytes 262176 | tf_op jit(solution)/shard_map/all_to_all | solution.py:469
  25.1 0.0 copy-start
  25.1 0.0 copy-start.11
  25.1 0.0 collective-permute-done.7.b_ref.near_b_ref
  25.1 0.1 join.1
  25.2 2.5 %collective-permute-start.8 = (bf16[672,128]{1,0:T(8,128)(2,1)S(1)}, bf16[672,128]{1,0:T(8,128)(2,1)S(1)}, u32[]{:S(2)}, u32[]{:S(2)}) collective-permute-start(bf16[672,128]{1,0:T(8,128)(2,1)S(1)} %get-tuple-element.55), channel_id=1, source_target_pairs={{0,1},{1,2},{2,3},{3,4},{4,5},{5,6},{6,7},{8,9},{9,10},{10,11},{11... | collective-permute-start | bytes 516104 | tf_op jit(solution)/shard_map/ppermute | solution.py:437
  27.7 4.9 %collective-permute-start.9 = (bf16[672,128]{1,0:T(8,128)(2,1)S(1)}, bf16[672,128]{1,0:T(8,128)(2,1)S(1)}, u32[]{:S(2)}, u32[]{:S(2)}) collective-permute-start(bf16[672,128]{1,0:T(8,128)(2,1)S(1)} %get-tuple-element.56), channel_id=1, source_target_pairs={{1,0},{2,1},{3,2},{4,3},{5,4},{6,5},{7,6},{9,8},{10,9},{11,10},{12... | collective-permute-start | bytes 516104 | tf_op jit(solution)/shard_map/ppermute | solution.py:442
  32.6 6.4 %collective-permute-start.6 = (f32[8,1024]{1,0:T(8,128)S(1)}, f32[8,1024]{1,0:T(8,128)S(1)}, u32[]{:S(2)}, u32[]{:S(2)}) collective-permute-start(f32[8,1024]{1,0:T(8,128)S(1)} %get-tuple-element.73.refs_1_), channel_id=1, source_target_pairs={{8,16},{16,8},{24,32},{32,24},{40,48},{48,40},{56,64},{64,56},{72,... | collective-permute-start | bytes 98312 | tf_op jit(solution)/shard_map/ppermute | solution.py:449
  39.0 0.1 collective-permute-start.5
  39.1 0.0 copy-done
  39.1 0.0 copy-done.11
  39.1 0.0 copy-done.6
  39.1 0.0 copy-done.8
  39.1 0.0 copy-start.2
  39.1 0.0 copy-start.4
  39.2 0.0 copy-start.9
  39.2 0.0 copy-start.10
  39.2 4.2 %pool_all.1.pooled_ref = bf16[64,64,1024]{2,1,0:T(8,128)(2,1)S(1)} custom-call(bf16[64,64,1024]{2,1,0:T(8,128)(2,1)} %merit_ref.5, f32[8,1024]{1,0:T(8,128)} %copy-done, f32[8,1024]{1,0:T(8,128)} %copy-done.11, bf16[608,128]{1,0:T(8,128)(2,1)S(1)} %copy-done.6, bf16[608,128]{1,0:T(8,128)(2,1)S(1)} %copy-done.8), custom_call_target="tpu_custom_call" | custom-call | flops 8388608 | bytes 4194304 | tf_op jit(solution)/shard_map/pool_all/pallas_call | solution.py:222
  43.3 0.0 collective-permute-done.6.seam_b_ref
  43.4 0.0 collective-permute-done.5.seam_a_ref
  43.4 0.0 collective-permute-done.8.west_ref
  43.4 0.0 collective-permute-done.9.east_ref
  43.4 0.0 copy-done.2
  43.4 0.0 copy-done.4
  43.4 0.0 copy-done.9
  43.4 0.0 copy-done.10
  43.4 8.3 %merge.1 = bf16[64,64,1024]{2,1,0:T(8,128)(2,1)} custom-call(s32[2,64]{1,0:T(2,128)S(1)} %bitcast.9, f32[15]{0:T(128)S(1)} %copy-done.4, bf16[64,64,1024]{2,1,0:T(8,128)(2,1)S(1)} %pool_all.1.pooled_ref, f32[64,1024]{1,0:T(8,128)S(1)} %bitcast.7, f32[8,1024]{1,0:T(8,128)S(1)} %collective-permute-done.5.seam_a_ref, ...), custom_call_target="tpu_custom_call" | custom-call | tf_op jit(solution)/shard_map/merge/pallas_call | solution.py:413
  (1 shorter events, 0.0 us)
Async XLA Ops:
  0.0 9.5 %copy-start.3 = (f32[15]{0:T(128)S(1)}, f32[15]{0:T(128)}, u32[]{:S(2)}) copy-start(f32[15]{0:T(128)} %taps_ref.2) | copy-start | bytes 184
  0.0 9.5 %copy-start.1 = (f32[8,8192]{1,0:T(8,128)S(1)}, f32[8,8192]{1,0:T(8,128)}, u32[]{:S(2)}) copy-start(f32[8,8192]{1,0:T(8,128)} %strip_ref.1) | copy-start | bytes 786436
  4.7 4.7 %collective-permute-start.4 = (bf16[208,1024]{1,0:T(8,128)(2,1)S(1)}, bf16[208,1024]{1,0:T(8,128)(2,1)S(1)}, u32[]{:S(2)}, u32[]{:S(2)}) collective-permute-start(bf16[208,1024]{1,0:T(8,128)(2,1)S(1)} %get-tuple-element.44), channel_id=1, source_target_pairs={{0,8},{8,0},{16,24},{24,16},{32,40},{40,32},{48,56},{56,48},{64,72... | collective-permute-start | bytes 1277960 | tf_op jit(solution)/shard_map/ppermute | solution.py:449
  5.5 19.6 %collective-permute-start.7 = (bf16[208,1024]{1,0:T(8,128)(2,1)S(1)}, bf16[208,1024]{1,0:T(8,128)(2,1)S(1)}, u32[]{:S(2)}, u32[]{:S(2)}) collective-permute-start(bf16[208,1024]{1,0:T(8,128)(2,1)S(1)} %get-tuple-element.52), channel_id=1, source_target_pairs={{8,16},{16,8},{24,32},{32,24},{40,48},{48,40},{56,64},{64,56},{72,... | collective-permute-start | bytes 1277960 | tf_op jit(solution)/shard_map/ppermute | solution.py:449
  12.4 12.7 %all-to-all-start = ((f32[8,8,1024]{2,1,0:T(8,128)}), f32[8,8,1024]{2,1,0:T(8,128)S(1)}, u32[]{:S(2)}, u32[]{:S(2)}) async-start(f32[8,8,1024]{2,1,0:T(8,128)} %filter_rows.1.after_ref), calls=%async_computation | async-start | bytes 524288 | tf_op jit(solution)/shard_map/all_to_all | solution.py:469
  19.3 19.8 %copy-start.6 = (bf16[608,128]{1,0:T(8,128)(2,1)S(1)}, bf16[608,128]{1,0:T(8,128)(2,1)}, u32[]{:S(2)}) copy-start(bf16[608,128]{1,0:T(8,128)(2,1)} %get-tuple-element.50.refs_2_.far_ref.far_west_ref) | copy-start | bytes 466948
  19.3 19.8 %copy-start.8 = (bf16[608,128]{1,0:T(8,128)(2,1)S(1)}, bf16[608,128]{1,0:T(8,128)(2,1)}, u32[]{:S(2)}) copy-start(bf16[608,128]{1,0:T(8,128)(2,1)} %get-tuple-element.51.refs_3_.far_east_ref) | copy-start | bytes 466948
  25.1 14.0 %copy-start = (f32[8,1024]{1,0:T(8,128)}, f32[8,1024]{1,0:T(8,128)S(1)}, u32[]{:S(2)}) copy-start(f32[8,1024]{1,0:T(8,128)S(1)} %get-tuple-element.74.refs_0_.after_ref) | copy-start | bytes 98308
  25.1 14.0 %copy-start.11 = (f32[8,1024]{1,0:T(8,128)}, f32[8,1024]{1,0:T(8,128)S(1)}, u32[]{:S(2)}) copy-start(f32[8,1024]{1,0:T(8,128)S(1)} %get-tuple-element.73.refs_1_) | copy-start | bytes 98308
  25.2 18.2 %collective-permute-start.8 = (bf16[672,128]{1,0:T(8,128)(2,1)S(1)}, bf16[672,128]{1,0:T(8,128)(2,1)S(1)}, u32[]{:S(2)}, u32[]{:S(2)}) collective-permute-start(bf16[672,128]{1,0:T(8,128)(2,1)S(1)} %get-tuple-element.55), channel_id=1, source_target_pairs={{0,1},{1,2},{2,3},{3,4},{4,5},{5,6},{6,7},{8,9},{9,10},{10,11},{11... | collective-permute-start | bytes 516104 | tf_op jit(solution)/shard_map/ppermute | solution.py:437
  27.7 15.7 %collective-permute-start.9 = (bf16[672,128]{1,0:T(8,128)(2,1)S(1)}, bf16[672,128]{1,0:T(8,128)(2,1)S(1)}, u32[]{:S(2)}, u32[]{:S(2)}) collective-permute-start(bf16[672,128]{1,0:T(8,128)(2,1)S(1)} %get-tuple-element.56), channel_id=1, source_target_pairs={{1,0},{2,1},{3,2},{4,3},{5,4},{6,5},{7,6},{9,8},{10,9},{11,10},{12... | collective-permute-start | bytes 516104 | tf_op jit(solution)/shard_map/ppermute | solution.py:442
  32.6 10.8 %collective-permute-start.6 = (f32[8,1024]{1,0:T(8,128)S(1)}, f32[8,1024]{1,0:T(8,128)S(1)}, u32[]{:S(2)}, u32[]{:S(2)}) collective-permute-start(f32[8,1024]{1,0:T(8,128)S(1)} %get-tuple-element.73.refs_1_), channel_id=1, source_target_pairs={{8,16},{16,8},{24,32},{32,24},{40,48},{48,40},{56,64},{64,56},{72,... | collective-permute-start | bytes 98312 | tf_op jit(solution)/shard_map/ppermute | solution.py:449
  39.0 4.4 %collective-permute-start.5 = (f32[8,1024]{1,0:T(8,128)S(1)}, f32[8,1024]{1,0:T(8,128)S(1)}, u32[]{:S(2)}, u32[]{:S(2)}) collective-permute-start(f32[8,1024]{1,0:T(8,128)S(1)} %get-tuple-element.74.refs_0_.after_ref), channel_id=1, source_target_pairs={{0,8},{8,0},{16,24},{24,16},{32,40},{40,32},{48,56},{56,48},{64,72... | collective-permute-start | bytes 98312 | tf_op jit(solution)/shard_map/ppermute | solution.py:449
  39.1 4.3 %copy-start.2 = (s32[64,2]{0,1:T(2,128)S(1)}, s32[64,2]{0,1:T(2,128)}, u32[]{:S(2)}) copy-start(s32[64,2]{0,1:T(2,128)} %param.11) | copy-start | bytes 1540
  39.1 4.3 %copy-start.4 = (f32[15]{0:T(128)S(1)}, f32[15]{0:T(128)}, u32[]{:S(2)}) copy-start(f32[15]{0:T(128)} %taps_ref.3) | copy-start | bytes 184
  39.2 4.2 %copy-start.9 = (bf16[304,1024]{1,0:T(8,128)(2,1)S(1)}, bf16[304,1024]{1,0:T(8,128)(2,1)}, u32[]{:S(2)}) copy-start(bf16[304,1024]{1,0:T(8,128)(2,1)} %get-tuple-element.57.far_a_ref) | copy-start | bytes 1867780
  39.2 4.2 %copy-start.10 = (bf16[304,1024]{1,0:T(8,128)(2,1)S(1)}, bf16[304,1024]{1,0:T(8,128)(2,1)}, u32[]{:S(2)}) copy-start(bf16[304,1024]{1,0:T(8,128)(2,1)} %get-tuple-element.58.far_b_ref) | copy-start | bytes 1867780
